TPU v7x, 512 devices: a whole 4x4x16 slice. The times are simulated.
512 devices in a mesh: sect: 4 (over z_hi), tok: 4 (over z_lo), vocab: 32 (over y, x, core).
Axes of the slice: x: 4, y: 4, z: 16 (z_hi: 4, z_lo: 4; z = z_hi * 4 + z_lo), core: 2. Of those that a mesh axis runs over, the one named last changes fastest.
Arguments:
- hidden: bfloat16 [2048, 4096], P('sect', ('tok', 'vocab')), may hold values from -256 to 256
- head_weight: bfloat16 [4096, 65536], P('tok', 'vocab'), may hold values from -1 to 1
- teacher_logits: bfloat16 [2048, 65536], P(('sect', 'tok', 'vocab')), may hold values from -16 to 390
- pairing: int32 [4, 4], replicated, may hold values from 0 to 3, as said below
Outputs:
- grad_hidden: float32 [2048, 4096], P('sect', ('tok', 'vocab'))
- divergence: float32 [2048], P(('sect', 'tok'))
Inputs may be any that keep to these rules, and one draw needn't show every extreme that they name: `pairing`: every row is a permutation of the sections.
All inputs are finite; a program needn't handle non-finite values.
Results may differ from a plain program's by a relative error of at most 0.0027.
Values may be sent and summed in bfloat16 or wider, within the bound.
No kernel may reach another device: no remote copies, remote signals or barrier semaphores. Data moves between devices by JAX's collectives and lax.ppermute only.
A program may use at most 64 MiB of HBM per device.

v0:
```python
import jax
import jax.numpy as jnp
from jax import lax
from jax.sharding import PartitionSpec as P

loss_scale = 16.0


def teacher_order(teacher_logits, pairing, sect_count, vocab_count, shard_width):
    section = lax.axis_index("sect")
    pairs_row = lax.dynamic_slice_in_dim(pairing, section, 1, 0)[0]
    select = (pairs_row[None, :] == jnp.arange(sect_count, dtype=jnp.int32)[:, None]).astype(
        jnp.bfloat16
    )
    ordered = jnp.dot(select, teacher_logits, preferred_element_type=jnp.float32).astype(
        jnp.bfloat16
    )
    piece_rows = teacher_logits.shape[0] // sect_count
    ordered = ordered.reshape(sect_count, piece_rows, vocab_count, shard_width)
    arrived = lax.all_to_all(
        lax.all_to_all(ordered, "sect", split_axis=0, concat_axis=0, tiled=True),
        "vocab",
        split_axis=2,
        concat_axis=2,
        tiled=True,
    )
    return arrived.reshape(sect_count * piece_rows * vocab_count, shard_width)


def shards(hidden, head_weight, teacher_logits, pairing):
    sect_count = lax.axis_size("sect")
    tok_count = lax.axis_size("tok")
    vocab_count = lax.axis_size("vocab")
    shard_width = head_weight.shape[1]
    feat_cols = hidden.shape[1]
    teacher_vals = teacher_order(
        teacher_logits, pairing, sect_count, vocab_count, shard_width
    ).astype(jnp.float32)
    own_count = teacher_vals.shape[0]
    narrow = lax.all_to_all(hidden, "tok", split_axis=0, concat_axis=1, tiled=True)
    spread = lax.all_gather(narrow, "vocab", axis=1, tiled=True)
    features = spread.reshape(own_count, vocab_count, tok_count, feat_cols).transpose(0, 2, 1, 3)
    features = features.reshape(own_count, tok_count * vocab_count * feat_cols)
    column = lax.all_gather(head_weight, "tok", axis=0, tiled=True)
    logits = jnp.dot(features, column, preferred_element_type=jnp.float32)
    top_student, top_teacher = lax.pmax(
        (jnp.max(logits, axis=1), jnp.max(teacher_vals, axis=1)), "vocab"
    )
    exp_student = jnp.exp(logits - top_student[:, None])
    exp_teacher = jnp.exp(teacher_vals - top_teacher[:, None])
    total_student, total_teacher, cross = lax.psum(
        (
            jnp.sum(exp_student, axis=1),
            jnp.sum(exp_teacher, axis=1),
            jnp.sum(exp_teacher * (teacher_vals - logits), axis=1),
        ),
        "vocab",
    )
    diverge = (
        cross / total_teacher
        - top_teacher
        - jnp.log(total_teacher)
        + top_student
        + jnp.log(total_student)
    )
    grad_logits = (
        loss_scale * (exp_student / total_student[:, None] - exp_teacher / total_teacher[:, None])
    ).astype(jnp.bfloat16)
    own_grad = lax.dot_general(
        grad_logits, column, (((1,), (1,)), ((), ())), preferred_element_type=jnp.float32
    )
    regroup = (
        own_grad.reshape(own_count, tok_count, vocab_count, feat_cols)
        .transpose(0, 2, 1, 3)
        .reshape(own_count, -1)
    )
    summed = lax.psum_scatter(regroup, "vocab", scatter_dimension=1, tiled=True)
    grads = lax.all_to_all(summed, "tok", split_axis=1, concat_axis=0, tiled=True)
    return (grads, diverge)


def solution(mesh):
    placed = (
        P("sect", ("tok", "vocab")),
        P("tok", "vocab"),
        P(("sect", "tok", "vocab"), None),
        P(),
    )
    return jax.shard_map(
        shards,
        mesh=mesh,
        in_specs=placed,
        out_specs=(P("sect", ("tok", "vocab")), P(("sect", "tok"))),
        check_vma=False,
    )
```

profile of v0, /device:TPU:6, one launch (start us, length us, event | category | flops | bytes accessed | tf_op | source)
XLA Modules:
  0.0 643.1 jit_solution(5026866139109011436)
XLA Ops:
  7.2 0.0 copy-start
  7.2 0.0 all-gather.3.cloned.1.call-start
  7.2 0.8 copy_bitcast_fusion.1
  8.0 11.4 %all_to_all.48 = bf16[4,128,32]{1,2,0:T(8,128)(2,1)} all-to-all(bf16[4,128,32]{1,2,0:T(8,128)(2,1)S(1)} %copy_bitcast_fusion.1), channel_id=1, replica_groups=mesh['sect'=4,'tok'=4,'vocab'=32] {'tok'}, dimensions={0} | all-to-all | bytes 65536 | tf_op jit(solution)/shard_map/all_to_all | solution.py:40
  19.5 0.0 all-gather.3.cloned.1.call-update
  19.5 0.0 all-gather.5.cloned.1.call-start
  19.6 0.7 all-gather.5.cloned.1.call-update
  20.3 0.0 reduce-scatter.2.cloned.1.call-start
  20.3 0.7 dynamic-slice_bitcast_fusion
  21.0 0.0 copy-done
  21.0 0.4 convolution_convert_fusion
  21.4 0.3 copy.53
  21.7 38.4 %all_to_all.49 = bf16[4,1,32,2048]{3,2,1,0:T(8,128)(2,1)S(1)} all-to-all(bf16[4,1,32,2048]{3,2,1,0:T(8,128)(2,1)S(1)} %bitcast.56), channel_id=1, replica_groups=mesh['sect'=4,'tok'=4,'vocab'=32] {'sect'}, dimensions={0} | all-to-all | bytes 1048576 | tf_op jit(solution)/shard_map/all_to_all | solution.py:21
  60.1 0.4 copy.37
  60.5 17.7 %all_to_all.50 = bf16[4,1,32,2048]{3,0,1,2:T(4,128)(2,1)S(1)} all-to-all(bf16[4,1,32,2048]{3,0,1,2:T(4,128)(2,1)S(1)} %copy.37), channel_id=1, replica_groups=mesh['sect'=4,'tok'=4,'vocab'=32] {'vocab'}, dimensions={2} | all-to-all | bytes 1048576 | tf_op jit(solution)/shard_map/all_to_all | solution.py:20
  78.2 0.3 reduce_max.26
  78.5 0.1 copy.49
  78.6 0.1 reshape.52
  78.7 0.3 copy.38
  79.0 1.7 all-gather.3.cloned.1.call-done
  80.7 2.4 copy.35
  83.0 296.7 %all-gather.5.cloned.1.call-done = bf16[4096,2048]{1,0:T(8,128)(2,1)} async-done(((bf16[1024,2048]{1,0:T(8,128)(2,1)}), bf16[4096,2048]{1,0:T(8,128)(2,1)}) %all-gather.5.cloned.1.call-update) | async-done | bytes 16777232 | tf_op jit(solution)/shard_map/all_gather | solution.py:44
  379.8 8.5 %fusion.5 = (f32[128]{0:T(128)S(1)}, f32[128,2048]{1,0:T(8,128)S(1)}) fusion(bf16[128,4096]{0,1:T(8,128)(2,1)} %bitcast.54, bf16[4096,2048]{1,0:T(8,128)(2,1)} %all-gather.5.cloned.1.call-done), kind=kOutput, calls=%fused_computation.17 | convolution fusion | flops 2147745792 | bytes 18874880 | tf_op jit(solution)/shard_map/dot_general | solution.py:45
  388.3 52.4 %all-reduce.1 = (f32[128]{0:T(128)S(1)}, f32[128]{0:T(128)S(1)}) all-reduce(f32[128]{0:T(128)S(1)} %reshape.52, f32[128]{0:T(128)S(1)} %get-tuple-element.9), channel_id=1, replica_groups=mesh['sect'=4,'tok'=4,'vocab'=32] {'vocab'}, use_global_device_ids=true, to_apply=%region_5.0 | all-reduce | flops 256 | bytes 2048 | tf_op jit(solution)/shard_map/pmax | solution.py:46
  440.7 0.1 sub.39
  440.8 0.1 copy.40
  440.9 0.6 exponential_reduce_fusion
  441.4 0.1 copy.41
  441.5 0.1 reduce_sum.31
  441.6 0.5 fusion.2
  442.1 62.7 %all-reduce = (f32[128]{0:T(128)S(1)}, f32[128]{0:T(128)S(1)}, f32[128]{0:T(128)S(1)}) all-reduce(f32[128]{0:T(128)S(1)} %reduce_sum.31, f32[128]{0:T(128)S(1)} %get-tuple-element.3, f32[128]{0:T(128)S(1)} %get-tuple-element.2), channel_id=1, replica_groups=mesh['sect'=4,'tok'=4,'vocab'=32] {'vocab'}, use_global_device_ids=true, to_apply=%region_7.0 | all-reduce | flops 384 | bytes 3072 | tf_op jit(solution)/shard_map/psum | solution.py:51
  504.8 0.5 multiply_convert_fusion
  505.3 8.2 %fusion.6 = f32[128,4096]{0,1:T(8,128)S(1)} fusion(bf16[128,2048]{1,0:T(8,128)(2,1)S(1)} %multiply_convert_fusion, bf16[4096,2048]{1,0:T(8,128)(2,1)} %all-gather.5.cloned.1.call-done), kind=kOutput, calls=%fused_computation.18 | convolution fusion | flops 2147483648 | bytes 19398656 | tf_op jit(solution)/shard_map/dot_general | solution.py:69
  513.5 1.6 copy.43
  515.0 0.0 reduce-scatter.2.cloned.1.call-update
  515.0 110.4 %reduce-scatter.2.cloned.1.call-done = f32[128,128]{0,1:T(8,128)} async-done(((f32[128,4096]{0,1:T(8,128)}), f32[128,128]{0,1:T(8,128)}) %reduce-scatter.2.cloned.1.call-update) | async-done | bytes 65552 | tf_op jit(solution)/shard_map/reduce_scatter | solution.py:77
  625.4 4.8 all-to-all-start.3
  630.2 0.5 log_add_fusion
  630.7 5.2 all-to-all-done.3
  635.9 0.6 copy_bitcast_fusion
Async XLA Ops:
  7.2 13.8 %copy-start = (bf16[4,65536]{1,0:T(4,128)(2,1)S(1)}, bf16[4,65536]{1,0:T(4,128)(2,1)}, u32[]{:S(2)}) copy-start(bf16[4,65536]{1,0:T(4,128)(2,1)} %param.6) | copy-start | bytes 1572868
  7.2 73.5 %all-gather.3.cloned.1.call-start = ((), (), s32[]{:S(2)}) async-start(), calls=%async_computation.5 | async-start | bytes 1081344 | tf_op jit(solution)/shard_map/all_gather | solution.py:41
  19.5 360.3 %all-gather.5.cloned.1.call-start = ((), (), s32[]{:S(2)}) async-start(), calls=%async_computation.6 | async-start | bytes 20971520 | tf_op jit(solution)/shard_map/all_gather | solution.py:44
  20.3 605.1 %reduce-scatter.2.cloned.1.call-start = ((), (), s32[]{:S(2)}) async-start(), calls=%async_computation.7 | async-start | bytes 2162688 | tf_op jit(solution)/shard_map/reduce_scatter | solution.py:77
  625.4 10.5 %all-to-all-start.3 = ((f32[128,4,32]{0,2,1:T(8,128)}), f32[128,4,32]{0,2,1:T(8,128)S(1)}, u32[]{:S(2)}, u32[]{:S(2)}) async-start(f32[128,4,32]{0,2,1:T(8,128)} %bitcast.59), calls=%async_computation.4 | async-start | bytes 131072 | tf_op jit(solution)/shard_map/all_to_all | solution.py:78
Sparse Core Ops, SparseCore 0:
  19.6 60.9 all-gather.2
  82.8 296.9 all-gather.4
  515.2 110.1 reduce-scatter.1
where the time goes:
time: 644 us; the launch traced here: 643 us
  waiting for transfers between devices  415 us (64%)
  blocking collectives  183 us (28%)
  matrix products  17.1 us (3%)
  between operations  13.8 us (2%)
  local copies, waits for them, and re-layouts  7.59 us (1%)
    all_gather x1, waiting for transfers between devices, shards(): column = lax.all_gather(head_weight, 'tok', axis=0, tiled=True)  297 us
    reduce_scatter x1, waiting for transfers between devices, shards(): summed = lax.psum_scatter(regroup, 'vocab', scatter_dimension=1, tiled=True)  110 us
    psum x1, blocking collectives, shards(): lax.psum((jnp.sum(exp_student, axis=1), jnp.sum(exp_teacher, axis=1), jnp...  62.7 us
    pmax x1, blocking collectives, shards(): lax.pmax((jnp.max(logits, axis=1), jnp.max(teacher_vals, axis=1)), 'vocab')  52.4 us
    all_to_all x1, blocking collectives, teacher_order(): lax.all_to_all(ordered, 'sect', split_axis=0, concat_axis=0, tiled=True)  38.4 us
    all_to_all x1, blocking collectives, teacher_order(): lax.all_to_all(lax.all_to_all(ordered, 'sect', split_axis=0, concat_axis=...  17.7 us
  transfers between devices with their start and end apart: 4, of which 4 were waited for; matrix products, arithmetic and copies ran while one was open for 1% of the time, Pallas kernels for 0%

commit v1 on v0

v1 whole, which is shorter than its diff:
```python
import jax
import jax.numpy as jnp
from jax import lax
from jax.sharding import PartitionSpec as P

loss_scale = 16.0


def along_z(value, steps, planes):
    return lax.ppermute(
        value, ("sect", "tok"), [(i, (i + steps) % planes) for i in range(planes)]
    )


def along_sect(value, steps, sections):
    return lax.ppermute(value, "sect", [(i, (i + steps) % sections) for i in range(sections)])


def edge_offset(token_section, sections):
    return jnp.where(token_section < sections // 2, -2, 2)


def window_offsets(token_section, sections):
    return [edge_offset(token_section, sections), -1, 0, 1]


def row_block(plane, sections, toks):
    plane = (plane + sections * toks) % (sections * toks)
    return (plane % toks) * sections + plane // toks


def shards(hidden, head_weight, teacher_logits, pairing):
    sections = lax.axis_size("sect")
    toks = lax.axis_size("tok")
    vocabs = lax.axis_size("vocab")
    planes = sections * toks
    width = head_weight.shape[1]
    feats = hidden.shape[1]
    rows = hidden.shape[0]
    unit = rows // planes
    own = sections * unit
    half = own // 2
    section = lax.axis_index("sect")
    tok = lax.axis_index("tok")

    blocks = []
    for k in range(sections):
        plane = ((section + k) % sections) * toks + tok
        blocks += [row_block(plane + off, sections, toks) for off in window_offsets(section, sections)]
    source = jnp.repeat(jnp.stack(blocks), unit) * unit + jnp.tile(
        jnp.arange(unit, dtype=jnp.int32), sections * 4
    )
    pick = (jnp.arange(rows, dtype=jnp.int32)[:, None] == source[None, :]).astype(jnp.bfloat16)
    picked = lax.dot_general(
        hidden, pick, (((0,), (0,)), ((), ())), preferred_element_type=jnp.float32
    ).astype(jnp.bfloat16)
    parts = picked.reshape(feats, sections, own)
    arrived = [parts[:, 0]] + [along_sect(parts[:, k], k, sections) for k in range(1, sections)]
    by_section = jnp.zeros((sections, feats, 4, unit), jnp.bfloat16)
    for k in range(sections):
        by_section = lax.dynamic_update_slice(
            by_section,
            arrived[k].reshape(1, feats, 4, unit),
            ((section - k + sections) % sections, 0, 0, 0),
        )
    by_section = by_section.transpose(1, 2, 0, 3)
    edges = by_section[:, 0].reshape(feats, own)
    window = jnp.concatenate(
        [edges[:, :half], by_section[:, 1:].reshape(feats, 3 * own), edges[:, half:]], axis=1
    )
    spread = lax.all_to_all(
        jnp.broadcast_to(window[None], (vocabs, feats, rows)),
        "vocab",
        split_axis=0,
        concat_axis=0,
        tiled=True,
    ).reshape(vocabs * feats, rows)

    partial = lax.dot_general(
        spread, head_weight, (((0,), (0,)), ((), ())), preferred_element_type=jnp.float32
    )
    below = half
    mine = below + own
    above = mine + own
    last = above + own
    far_down = along_z(partial[:below], -1, planes)
    far_up = along_z(partial[last:], 1, planes)
    down_b = along_z(partial[below + half : mine], -1, planes)
    up_a = along_z(partial[above : above + half], 1, planes)
    down_a = along_z(partial[below : below + half] + far_down, -1, planes)
    up_b = along_z(partial[above + half : last] + far_up, 1, planes)
    logits = (
        partial[mine:above]
        + jnp.concatenate([down_a, down_b], axis=0)
        + jnp.concatenate([up_a, up_b], axis=0)
    )

    pairs_row = lax.dynamic_slice_in_dim(pairing, section, 1, 0)[0]
    select = (pairs_row[None, :] == jnp.arange(sections, dtype=jnp.int32)[:, None]).astype(
        jnp.bfloat16
    )
    ordered = jnp.dot(select, teacher_logits, preferred_element_type=jnp.float32).astype(
        jnp.bfloat16
    )
    teacher = lax.all_to_all(
        ordered.reshape(sections, vocabs, width).transpose(1, 0, 2),
        "vocab",
        split_axis=0,
        concat_axis=0,
        tiled=True,
    )
    teacher = teacher.transpose(1, 0, 2).reshape(own, width).astype(jnp.float32)

    top_s = jnp.max(logits, axis=1)
    top_t = jnp.max(teacher, axis=1)
    exp_t = jnp.exp(teacher - top_t[:, None])
    sum_s = jnp.sum(jnp.exp(logits - top_s[:, None]), axis=1)
    sum_t = jnp.sum(exp_t, axis=1)
    cross = jnp.sum(exp_t * (teacher - logits), axis=1)
    zero = jnp.zeros_like(cross)
    stats = jnp.stack([top_s, top_t, sum_s, sum_t, cross, zero, zero, zero])
    stats = lax.all_to_all(
        jnp.broadcast_to(stats[None], (vocabs,) + stats.shape),
        "vocab",
        split_axis=0,
        concat_axis=0,
        tiled=True,
    )
    top_student = jnp.max(stats[:, 0], axis=0)
    top_teacher = jnp.max(stats[:, 1], axis=0)
    scale_s = jnp.exp(stats[:, 0] - top_student[None])
    scale_t = jnp.exp(stats[:, 1] - top_teacher[None])
    total_student = jnp.sum(stats[:, 2] * scale_s, axis=0)
    total_teacher = jnp.sum(stats[:, 3] * scale_t, axis=0)
    cross = jnp.sum(stats[:, 4] * scale_t, axis=0)
    diverge = (
        cross / total_teacher
        - top_teacher
        - jnp.log(total_teacher)
        + top_student
        + jnp.log(total_student)
    )
    grad_logits = (
        loss_scale
        * (
            jnp.exp(logits - top_student[:, None]) / total_student[:, None]
            - jnp.exp(teacher - top_teacher[:, None]) / total_teacher[:, None]
        )
    ).astype(jnp.bfloat16)

    near_below = along_z(grad_logits, 1, planes)
    near_above = along_z(grad_logits, -1, planes)
    far_below = along_z(grad_logits[:half], 2, planes)
    far_above = along_z(grad_logits[half:], -2, planes)
    window_grad = jnp.concatenate(
        [far_below, near_below, grad_logits, near_above, far_above], axis=0
    )
    own_grad = lax.dot_general(
        head_weight, window_grad, (((1,), (1,)), ((), ())), preferred_element_type=jnp.float32
    )
    summed = jnp.sum(
        lax.all_to_all(
            own_grad.reshape(vocabs, feats, rows),
            "vocab",
            split_axis=0,
            concat_axis=0,
            tiled=True,
        ),
        axis=0,
    )

    edges = jnp.concatenate([summed[:, :below], summed[:, last:]], axis=1)
    returned = jnp.concatenate([edges, summed[:, below:last]], axis=1)
    returned = returned.reshape(feats, 4, sections, unit).transpose(2, 0, 1, 3)
    returned = returned.reshape(sections, feats, own)
    extra = jnp.pad(diverge.reshape(sections, 1, unit), ((0, 0), (0, 7), (0, own - unit)))
    returned = jnp.concatenate([returned, extra], axis=1)
    got = []
    for k in range(sections):
        piece = lax.dynamic_index_in_dim(returned, (section + k) % sections, 0, keepdims=False)
        got.append(piece if k == 0 else along_sect(piece, k, sections))
    grads = jnp.zeros((planes, unit, feats), jnp.float32)
    div = jnp.zeros((sections, unit), jnp.float32)
    for k in range(sections):
        sender = (section - k + sections) % sections
        piece = got[k][:feats].reshape(feats, 4, unit).transpose(1, 2, 0)
        for place, off in enumerate(window_offsets(section, sections)):
            grads = lax.dynamic_update_slice(
                grads,
                piece[place : place + 1],
                (row_block(sender * toks + tok + off, sections, toks), 0, 0),
            )
        div = lax.dynamic_update_slice(div, got[k][feats : feats + 1, :unit], (sender, 0))
    return grads.reshape(rows, feats), div.reshape(own)


def solution(mesh):
    placed = (
        P("sect", ("tok", "vocab")),
        P("tok", "vocab"),
        P(("sect", "tok", "vocab"), None),
        P(),
    )
    return jax.shard_map(
        shards,
        mesh=mesh,
        in_specs=placed,
        out_specs=(P("sect", ("tok", "vocab")), P(("sect", "tok"))),
        check_vma=False,
    )
```

time: 644 us -> 236 us (0.37)
  waiting for transfers between devices: 415 us -> 74.4 us
  blocking collectives: 183 us -> 33.5 us
  starting transfers between devices: 4.91 us -> 87.2 us
  between operations: 13.8 us -> 2.83 us
  local copies, waits for them, and re-layouts: 7.59 us -> 16.7 us
  matrix products: 17.1 us -> 9.28 us
  other arithmetic: 2.34 us -> 8.92 us
    all_gather x2 -> x0, waiting for transfers between devices: 298 us -> none  [the longest x1 297 us: shards(): column = lax.all_gather(head_weight, 'tok', axis=0, tiled=True)]
    reduce_scatter x1 -> x0, waiting for transfers between devices: 110 us -> none  [shards(): summed = lax.psum_scatter(regroup, 'vocab', scatter_dimension=1, tiled=True)]
    ppermute x0 -> x16, starting transfers between devices: none -> 75.1 us  [the longest x6 42.6 us: along_sect(): lax.ppermute(value, 'sect', [(i, (i + steps) % sections) for i in range(s...]
    psum x1 -> x0, blocking collectives: 62.7 us -> none  [shards(): lax.psum((jnp.sum(exp_student, axis=1), jnp.sum(exp_teacher, axis=1), jnp...]
    pmax x1 -> x0, blocking collectives: 52.4 us -> none  [shards(): lax.pmax((jnp.max(logits, axis=1), jnp.max(teacher_vals, axis=1)), 'vocab')]
    ppermute x0 -> x16, waiting for transfers between devices: none -> 49.1 us  [the longest x10 45.1 us: along_z(): lax.ppermute(value, ('sect', 'tok'), [(i, (i + steps) % planes) for i in...]
    all_to_all x3 -> x2, blocking collectives: 67.5 us -> 33.5 us  [the longest x1 22 us: shards(): lax.all_to_all(jnp.broadcast_to(window[None], (vocabs, feats, rows)), 'vo...]
    all_to_all x1 -> x2, waiting for transfers between devices: 5.22 us -> 25.2 us  [the longest x1 25.2 us: shards(): lax.all_to_all(own_grad.reshape(vocabs, feats, rows), 'vocab', split_axis...]
  transfers between devices with their start and end apart: 4 -> 18, of which waited for: 4 -> 9; matrix products, arithmetic and copies ran while one was open for 1% -> 6% of each run, Pallas kernels for 0% -> 0%
where the time goes in v1:
time: 236 us; the launch traced here: 233 us
  starting transfers between devices  87.2 us (37%)
  waiting for transfers between devices  74.4 us (32%)
  blocking collectives  33.5 us (14%)
  local copies, waits for them, and re-layouts  16.7 us (7%)
  matrix products  9.28 us (4%)
  other arithmetic  8.92 us (4%)
  between operations  2.83 us (1%)
    ppermute x10, waiting for transfers between devices, along_z(): lax.ppermute(value, ('sect', 'tok'), [(i, (i + steps) % planes) for i in...  45.1 us
    ppermute x6, starting transfers between devices, along_sect(): lax.ppermute(value, 'sect', [(i, (i + steps) % sections) for i in range(s...  42.6 us
    ppermute x10, starting transfers between devices, along_z(): lax.ppermute(value, ('sect', 'tok'), [(i, (i + steps) % planes) for i in...  32.5 us
    all_to_all x1, waiting for transfers between devices, shards(): lax.all_to_all(own_grad.reshape(vocabs, feats, rows), 'vocab', split_axis...  25.2 us
    all_to_all x1, blocking collectives, shards(): lax.all_to_all(jnp.broadcast_to(window[None], (vocabs, feats, rows)), 'vo...  22 us
    all_to_all x1, blocking collectives, shards(): lax.all_to_all(jnp.broadcast_to(stats[None], (vocabs,) + stats.shape), 'v...  11.5 us
    all_to_all x1, starting transfers between devices, shards(): lax.all_to_all(ordered.reshape(sections, vocabs, width).transpose(1, 0, 2...  6.51 us
    all_to_all x1, starting transfers between devices, shards(): lax.all_to_all(own_grad.reshape(vocabs, feats, rows), 'vocab', split_axis...  5.64 us
  transfers between devices with their start and end apart: 18, of which 9 were waited for; matrix products, arithmetic and copies ran while one was open for 6% of the time, Pallas kernels for 0%

profile of v1, /device:TPU:6, one launch (start us, length us, event | category | flops | bytes accessed | tf_op | source)
XLA Modules:
  0.0 232.7 jit_solution(10503055627501331089)
XLA Ops:
  1.7 0.1 stack.86
  2.0 1.0 fusion
  3.1 9.1 %collective-permute-start = (bf16[32,128]{1,0:T(8,128)(2,1)S(1)}, bf16[32,128]{1,0:T(8,128)(2,1)S(1)}, u32[]{:S(2)}, u32[]{:S(2)}) collective-permute-start(bf16[32,128]{1,0:T(8,128)(2,1)S(1)} %bitcast.121), channel_id=1, source_target_pairs={{0,128},{128,256},{256,384},{384,0},{1,129},{129,257},{257,385},{3... | collective-permute-start | bytes 24584 | tf_op jit(solution)/shard_map/ppermute | solution.py:16
  12.2 10.9 %collective-permute-start.1 = (bf16[32,128]{1,0:T(8,128)(2,1)S(1)}, bf16[32,128]{1,0:T(8,128)(2,1)S(1)}, u32[]{:S(2)}, u32[]{:S(2)}) collective-permute-start(bf16[32,128]{1,0:T(8,128)(2,1)S(1)} %bitcast.120), channel_id=1, source_target_pairs={{0,256},{128,384},{256,0},{384,128},{1,257},{129,385},{257,1},{385... | collective-permute-start | bytes 24584 | tf_op jit(solution)/shard_map/ppermute | solution.py:16
  23.2 5.5 %collective-permute-start.2 = (bf16[32,128]{1,0:T(8,128)(2,1)S(1)}, bf16[32,128]{1,0:T(8,128)(2,1)S(1)}, u32[]{:S(2)}, u32[]{:S(2)}) collective-permute-start(bf16[32,128]{1,0:T(8,128)(2,1)S(1)} %bitcast.119), channel_id=1, source_target_pairs={{0,384},{128,0},{256,128},{384,256},{1,385},{129,1},{257,129},{385... | collective-permute-start | bytes 24584 | tf_op jit(solution)/shard_map/ppermute | solution.py:16
  28.7 0.1 reshape_squeeze.8
  28.8 1.4 dynamic_update_slice.72
  30.3 1.4 dynamic_update_slice.73
  31.8 1.4 dynamic_update_slice.74
  33.2 0.1 reshape.200
  33.3 1.4 dynamic_update_slice.75
  34.8 0.1 reshape.182
  34.9 0.1 reshape_squeeze.7
  35.2 0.1 broadcast_in_dim.15
  35.3 22.0 %all_to_all.20 = bf16[32,32,512]{2,1,0:T(8,128)(2,1)S(1)} all-to-all(bf16[32,32,512]{2,1,0:T(8,128)(2,1)S(1)} %broadcast_in_dim.15), channel_id=1, replica_groups=mesh['sect'=4,'tok'=4,'vocab'=32] {'vocab'}, dimensions={0} | all-to-all | bytes 2097152 | tf_op jit(solution)/shard_map/all_to_all | solution.py:71
  57.3 4.6 %fusion.24 = f32[512,2048]{1,0:T(8,128)S(1)} fusion(bf16[1024,512]{1,0:T(8,128)(2,1)S(1)} %bitcast.103, bf16[1024,2048]{1,0:T(8,128)(2,1)} %param.5), kind=kOutput, calls=%fused_computation.63 | convolution fusion | flops 2147483648 | bytes 9437184 | tf_op jit(solution)/shard_map/dot_general | solution.py:79
  61.9 1.9 copy-done.1
  63.9 3.5 %collective-permute-start.3 = (f32[64,2048]{1,0:T(8,128)S(1)}, f32[64,2048]{1,0:T(8,128)S(1)}, u32[]{:S(2)}, u32[]{:S(2)}) collective-permute-start(f32[64,2048]{1,0:T(8,128)S(1)} %slice.209), channel_id=1, source_target_pairs={{0,480},{32,0},{64,32},{96,64},{128,96},{160,128},{192,160},{224,1... | collective-permute-start | bytes 1572872 | tf_op jit(solution)/shard_map/ppermute | solution.py:10
  67.4 0.7 fusion.12
  68.1 1.2 convolution_convert_fusion
  69.3 6.5 %all-to-all-start.1 = ((bf16[32,4,2048]{2,1,0:T(4,128)(2,1)}), bf16[32,4,2048]{2,1,0:T(4,128)(2,1)S(1)}, u32[]{:S(2)}, u32[]{:S(2)}) async-start(bf16[32,4,2048]{2,1,0:T(4,128)(2,1)} %bitcast.25), calls=%async_computation.1 | async-start | bytes 1048576 | tf_op jit(solution)/shard_map/all_to_all | solution.py:105
  75.9 4.4 %collective-permute-done.3 = f32[64,2048]{1,0:T(8,128)S(1)} collective-permute-done((f32[64,2048]{1,0:T(8,128)S(1)}, f32[64,2048]{1,0:T(8,128)S(1)}, u32[]{:S(2)}, u32[]{:S(2)}) %collective-permute-start.3) | collective-permute-done | bytes 524320 | tf_op jit(solution)/shard_map/ppermute | solution.py:10
  80.3 2.5 %slice_add_fusion.2 = (f32[64,2048]{1,0:T(8,128)}, f32[64,2048]{1,0:T(8,128)S(1)}, f32[64,2048]{1,0:T(8,128)S(1)}, f32[64,2048]{1,0:T(8,128)S(1)}) fusion(f32[64,2048]{1,0:T(8,128)S(1)} %collective-permute-done.3, f32[512,2048]{1,0:T(8,128)} %copy-done.1), kind=kLoop, calls=%fused_computation.21 | loop fusion | flops 131072 | bytes 4718592 | tf_op jit(solution)/shard_map/add | solution.py:90
  82.8 2.9 %collective-permute-start.7 = (f32[64,2048]{1,0:T(8,128)S(1)}, f32[64,2048]{1,0:T(8,128)S(1)}, u32[]{:S(2)}, u32[]{:S(2)}) collective-permute-start(f32[64,2048]{1,0:T(8,128)S(1)} %get-tuple-element.9), channel_id=1, source_target_pairs={{0,32},{32,64},{64,96},{96,128},{128,160},{160,192},{192,224},{224... | collective-permute-start | bytes 1572872 | tf_op jit(solution)/shard_map/ppermute | solution.py:10
  85.7 0.3 bitcast_reduce_fusion
  86.3 4.1 %collective-permute-start.4 = (f32[64,2048]{1,0:T(8,128)}, f32[64,2048]{1,0:T(8,128)}, u32[]{:S(2)}, u32[]{:S(2)}) collective-permute-start(f32[64,2048]{1,0:T(8,128)} %get-tuple-element.8), channel_id=1, source_target_pairs={{0,480},{32,0},{64,32},{96,64},{128,96},{160,128},{192,160},{224,1... | collective-permute-start | bytes 1572872 | tf_op jit(solution)/shard_map/ppermute | solution.py:10
  90.4 3.5 %collective-permute-start.5 = (f32[64,2048]{1,0:T(8,128)S(1)}, f32[64,2048]{1,0:T(8,128)}, u32[]{:S(2)}, u32[]{:S(2)}) collective-permute-start(f32[64,2048]{1,0:T(8,128)S(1)} %get-tuple-element.11), channel_id=1, source_target_pairs={{0,480},{32,0},{64,32},{96,64},{128,96},{160,128},{192,160},{224,1... | collective-permute-start | bytes 1572872 | tf_op jit(solution)/shard_map/ppermute | solution.py:10
  93.9 2.3 %collective-permute-start.6 = (f32[64,2048]{1,0:T(8,128)S(1)}, f32[64,2048]{1,0:T(8,128)}, u32[]{:S(2)}, u32[]{:S(2)}) collective-permute-start(f32[64,2048]{1,0:T(8,128)S(1)} %get-tuple-element.10), channel_id=1, source_target_pairs={{0,32},{32,64},{64,96},{96,128},{128,160},{160,192},{192,224},{224... | collective-permute-start | bytes 1572872 | tf_op jit(solution)/shard_map/ppermute | solution.py:10
  96.2 4.3 %collective-permute-done.7 = f32[64,2048]{1,0:T(8,128)S(1)} collective-permute-done((f32[64,2048]{1,0:T(8,128)S(1)}, f32[64,2048]{1,0:T(8,128)S(1)}, u32[]{:S(2)}, u32[]{:S(2)}) %collective-permute-start.7) | collective-permute-done | bytes 524320 | tf_op jit(solution)/shard_map/ppermute | solution.py:10
  100.6 1.9 slice_add_fusion.1
  102.5 1.9 collective-permute-start.8
  104.4 0.1 bitcast_convert_fusion
  104.5 0.6 copy.120
  105.1 0.6 exponential_reduce_fusion
  105.9 8.3 %collective-permute-done.5 = f32[64,2048]{1,0:T(8,128)} collective-permute-done((f32[64,2048]{1,0:T(8,128)S(1)}, f32[64,2048]{1,0:T(8,128)}, u32[]{:S(2)}, u32[]{:S(2)}) %collective-permute-start.5) | collective-permute-done | bytes 524320 | tf_op jit(solution)/shard_map/ppermute | solution.py:10
  114.2 8.6 %collective-permute-done.8 = f32[64,2048]{1,0:T(8,128)} collective-permute-done((f32[64,2048]{1,0:T(8,128)}, f32[64,2048]{1,0:T(8,128)}, u32[]{:S(2)}, u32[]{:S(2)}) %collective-permute-start.8) | collective-permute-done | bytes 524320 | tf_op jit(solution)/shard_map/ppermute | solution.py:10
  122.7 2.1 fusion.13
  124.8 0.5 fusion.4
  125.4 11.5 %all_to_all.21 = f32[32,8,128]{2,1,0:T(8,128)S(1)} all-to-all(f32[32,8,128]{2,1,0:T(8,128)S(1)} %broadcast_in_dim.16), channel_id=1, replica_groups=mesh['sect'=4,'tok'=4,'vocab'=32] {'vocab'}, dimensions={0} | all-to-all | bytes 262144 | tf_op jit(solution)/shard_map/all_to_all | solution.py:122
  137.0 0.5 fusion.9
  137.5 1.9 collective-permute-start.10
  139.4 4.4 %collective-permute-start.9 = (bf16[64,2048]{1,0:T(8,128)(2,1)S(1)}, bf16[64,2048]{1,0:T(8,128)(2,1)S(1)}, u32[]{:S(2)}, u32[]{:S(2)}) collective-permute-start(bf16[64,2048]{1,0:T(8,128)(2,1)S(1)} %get-tuple-element.13), channel_id=1, source_target_pairs={{0,64},{32,96},{64,128},{96,160},{128,192},{160,224},{192,256},{22... | collective-permute-start | bytes 786440 | tf_op jit(solution)/shard_map/ppermute | solution.py:10
  143.8 3.1 %collective-permute-start.11 = (bf16[128,2048]{1,0:T(8,128)(2,1)S(1)}, bf16[128,2048]{1,0:T(8,128)(2,1)S(1)}, u32[]{:S(2)}, u32[]{:S(2)}) collective-permute-start(bf16[128,2048]{1,0:T(8,128)(2,1)S(1)} %fusion.9), channel_id=1, source_target_pairs={{0,480},{32,0},{64,32},{96,64},{128,96},{160,128},{192,160},{224,1... | collective-permute-start | bytes 1572872 | tf_op jit(solution)/shard_map/ppermute | solution.py:10
  147.0 4.8 %collective-permute-start.12 = (bf16[64,2048]{1,0:T(8,128)(2,1)S(1)}, bf16[64,2048]{1,0:T(8,128)(2,1)S(1)}, u32[]{:S(2)}, u32[]{:S(2)}) collective-permute-start(bf16[64,2048]{1,0:T(8,128)(2,1)S(1)} %get-tuple-element.12), channel_id=1, source_target_pairs={{0,448},{32,480},{64,0},{96,32},{128,64},{160,96},{192,128},{224,1... | collective-permute-start | bytes 786440 | tf_op jit(solution)/shard_map/ppermute | solution.py:10
  151.8 13.9 %collective-permute-done.9 = bf16[64,2048]{1,0:T(8,128)(2,1)S(1)} collective-permute-done((bf16[64,2048]{1,0:T(8,128)(2,1)S(1)}, bf16[64,2048]{1,0:T(8,128)(2,1)S(1)}, u32[]{:S(2)}, u32[]{:S(2)}) %collective-permute-start.9) | collective-permute-done | bytes 262176 | tf_op jit(solution)/shard_map/ppermute | solution.py:10
  165.8 5.6 %collective-permute-done.12 = bf16[64,2048]{1,0:T(8,128)(2,1)S(1)} collective-permute-done((bf16[64,2048]{1,0:T(8,128)(2,1)S(1)}, bf16[64,2048]{1,0:T(8,128)(2,1)S(1)}, u32[]{:S(2)}, u32[]{:S(2)}) %collective-permute-start.12) | collective-permute-done | bytes 262176 | tf_op jit(solution)/shard_map/ppermute | solution.py:10
  171.5 2.4 %convolution_bitcast_fusion = f32[1024,512]{0,1:T(8,128)S(1)} fusion(bf16[512,2048]{1,0:T(8,128)(2,1)S(1)} %constant_dynamic-update-slice_fusion, bf16[1024,2048]{1,0:T(8,128)(2,1)S(1)} %copy-done.2), kind=kOutput, calls=%fused_computation.1 | convolution fusion | flops 2147483648 | bytes 8388608 | tf_op jit(solution)/shard_map/dot_general | solution.py:158
  173.9 1.9 copy.124
  175.7 5.6 %all-to-all-start.3 = ((f32[32,32,512]{2,1,0:T(8,128)}), f32[32,32,512]{2,1,0:T(8,128)S(1)}, u32[]{:S(2)}, u32[]{:S(2)}) async-start(f32[32,32,512]{2,1,0:T(8,128)} %bitcast.102), calls=%async_computation.3 | async-start | bytes 4194304 | tf_op jit(solution)/shard_map/all_to_all | solution.py:162
  181.8 25.2 %all-to-all-done.3 = f32[32,32,512]{2,1,0:T(8,128)S(1)} async-done(((f32[32,32,512]{2,1,0:T(8,128)}), f32[32,32,512]{2,1,0:T(8,128)S(1)}, u32[]{:S(2)}, u32[]{:S(2)}) %all-to-all-start.3) | async-done | bytes 2097184 | tf_op jit(solution)/shard_map/all_to_all | solution.py:162
  207.0 0.1 reduce_sum.68
  207.4 0.2 reshape.186
  207.6 0.2 reshape.187
  207.9 4.3 %collective-permute-start.13 = (f32[40,128]{1,0:T(8,128)S(1)}, f32[40,128]{1,0:T(8,128)S(1)}, u32[]{:S(2)}, u32[]{:S(2)}) collective-permute-start(f32[40,128]{1,0:T(8,128)S(1)} %get-tuple-element.22), channel_id=1, source_target_pairs={{0,128},{128,256},{256,384},{384,0},{1,129},{129,257},{257,385},{3... | collective-permute-start | bytes 61448 | tf_op jit(solution)/shard_map/ppermute | solution.py:16
  212.2 8.0 %collective-permute-start.14 = (f32[40,128]{1,0:T(8,128)S(1)}, f32[40,128]{1,0:T(8,128)S(1)}, u32[]{:S(2)}, u32[]{:S(2)}) collective-permute-start(f32[40,128]{1,0:T(8,128)S(1)} %get-tuple-element.21), channel_id=1, source_target_pairs={{0,256},{128,384},{256,0},{384,128},{1,257},{129,385},{257,1},{385... | collective-permute-start | bytes 61448 | tf_op jit(solution)/shard_map/ppermute | solution.py:16
  220.1 4.8 %collective-permute-start.15 = (f32[40,128]{1,0:T(8,128)S(1)}, f32[40,128]{1,0:T(8,128)S(1)}, u32[]{:S(2)}, u32[]{:S(2)}) collective-permute-start(f32[40,128]{1,0:T(8,128)S(1)} %get-tuple-element.20), channel_id=1, source_target_pairs={{0,384},{128,0},{256,128},{384,256},{1,385},{129,1},{257,129},{385... | collective-permute-start | bytes 61448 | tf_op jit(solution)/shard_map/ppermute | solution.py:16
  225.0 0.1 reshape.188
  225.7 1.0 collective-permute-done.14
  226.7 3.0 %collective-permute-done.15 = f32[40,128]{1,0:T(8,128)S(1)} collective-permute-done((f32[40,128]{1,0:T(8,128)S(1)}, f32[40,128]{1,0:T(8,128)S(1)}, u32[]{:S(2)}, u32[]{:S(2)}) %collective-permute-start.15) | collective-permute-done | bytes 20512 | tf_op jit(solution)/shard_map/ppermute | solution.py:16
  229.8 0.6 reshape.193
  230.4 0.1 reshape.189
  230.5 0.1 reshape.190
  230.7 0.1 reshape.191
  232.0 0.8 reshape.192
  (93 shorter events, 3.7 us)
Async XLA Ops:
  0.6 67.5 %copy-start = (bf16[4,65536]{1,0:T(4,128)(2,1)S(1)}, bf16[4,65536]{1,0:T(4,128)(2,1)}, u32[]{:S(2)}) copy-start(bf16[4,65536]{1,0:T(4,128)(2,1)} %param.6) | copy-start | bytes 1572868
  3.1 27.1 %collective-permute-start = (bf16[32,128]{1,0:T(8,128)(2,1)S(1)}, bf16[32,128]{1,0:T(8,128)(2,1)S(1)}, u32[]{:S(2)}, u32[]{:S(2)}) collective-permute-start(bf16[32,128]{1,0:T(8,128)(2,1)S(1)} %bitcast.121), channel_id=1, source_target_pairs={{0,128},{128,256},{256,384},{384,0},{1,129},{129,257},{257,385},{3... | collective-permute-start | bytes 24584 | tf_op jit(solution)/shard_map/ppermute | solution.py:16
  12.2 19.5 %collective-permute-start.1 = (bf16[32,128]{1,0:T(8,128)(2,1)S(1)}, bf16[32,128]{1,0:T(8,128)(2,1)S(1)}, u32[]{:S(2)}, u32[]{:S(2)}) collective-permute-start(bf16[32,128]{1,0:T(8,128)(2,1)S(1)} %bitcast.120), channel_id=1, source_target_pairs={{0,256},{128,384},{256,0},{384,128},{1,257},{129,385},{257,1},{385... | collective-permute-start | bytes 24584 | tf_op jit(solution)/shard_map/ppermute | solution.py:16
  23.2 10.1 %collective-permute-start.2 = (bf16[32,128]{1,0:T(8,128)(2,1)S(1)}, bf16[32,128]{1,0:T(8,128)(2,1)S(1)}, u32[]{:S(2)}, u32[]{:S(2)}) collective-permute-start(bf16[32,128]{1,0:T(8,128)(2,1)S(1)} %bitcast.119), channel_id=1, source_target_pairs={{0,384},{128,0},{256,128},{384,256},{1,385},{129,1},{257,129},{385... | collective-permute-start | bytes 24584 | tf_op jit(solution)/shard_map/ppermute | solution.py:16
  61.9 1.9 copy-start.1
  63.9 16.3 %collective-permute-start.3 = (f32[64,2048]{1,0:T(8,128)S(1)}, f32[64,2048]{1,0:T(8,128)S(1)}, u32[]{:S(2)}, u32[]{:S(2)}) collective-permute-start(f32[64,2048]{1,0:T(8,128)S(1)} %slice.209), channel_id=1, source_target_pairs={{0,480},{32,0},{64,32},{96,64},{128,96},{160,128},{192,160},{224,1... | collective-permute-start | bytes 1572872 | tf_op jit(solution)/shard_map/ppermute | solution.py:10
  69.3 16.4 %all-to-all-start.1 = ((bf16[32,4,2048]{2,1,0:T(4,128)(2,1)}), bf16[32,4,2048]{2,1,0:T(4,128)(2,1)S(1)}, u32[]{:S(2)}, u32[]{:S(2)}) async-start(bf16[32,4,2048]{2,1,0:T(4,128)(2,1)} %bitcast.25), calls=%async_computation.1 | async-start | bytes 1048576 | tf_op jit(solution)/shard_map/all_to_all | solution.py:105
  82.8 17.8 %collective-permute-start.7 = (f32[64,2048]{1,0:T(8,128)S(1)}, f32[64,2048]{1,0:T(8,128)S(1)}, u32[]{:S(2)}, u32[]{:S(2)}) collective-permute-start(f32[64,2048]{1,0:T(8,128)S(1)} %get-tuple-element.9), channel_id=1, source_target_pairs={{0,32},{32,64},{64,96},{96,128},{128,160},{160,192},{192,224},{224... | collective-permute-start | bytes 1572872 | tf_op jit(solution)/shard_map/ppermute | solution.py:10
  86.3 19.6 %collective-permute-start.4 = (f32[64,2048]{1,0:T(8,128)}, f32[64,2048]{1,0:T(8,128)}, u32[]{:S(2)}, u32[]{:S(2)}) collective-permute-start(f32[64,2048]{1,0:T(8,128)} %get-tuple-element.8), channel_id=1, source_target_pairs={{0,480},{32,0},{64,32},{96,64},{128,96},{160,128},{192,160},{224,1... | collective-permute-start | bytes 1572872 | tf_op jit(solution)/shard_map/ppermute | solution.py:10
  90.4 23.8 %collective-permute-start.5 = (f32[64,2048]{1,0:T(8,128)S(1)}, f32[64,2048]{1,0:T(8,128)}, u32[]{:S(2)}, u32[]{:S(2)}) collective-permute-start(f32[64,2048]{1,0:T(8,128)S(1)} %get-tuple-element.11), channel_id=1, source_target_pairs={{0,480},{32,0},{64,32},{96,64},{128,96},{160,128},{192,160},{224,1... | collective-permute-start | bytes 1572872 | tf_op jit(solution)/shard_map/ppermute | solution.py:10
  93.9 20.3 %collective-permute-start.6 = (f32[64,2048]{1,0:T(8,128)S(1)}, f32[64,2048]{1,0:T(8,128)}, u32[]{:S(2)}, u32[]{:S(2)}) collective-permute-start(f32[64,2048]{1,0:T(8,128)S(1)} %get-tuple-element.10), channel_id=1, source_target_pairs={{0,32},{32,64},{64,96},{96,128},{128,160},{160,192},{192,224},{224... | collective-permute-start | bytes 1572872 | tf_op jit(solution)/shard_map/ppermute | solution.py:10
  102.5 20.2 %collective-permute-start.8 = (f32[64,2048]{1,0:T(8,128)}, f32[64,2048]{1,0:T(8,128)}, u32[]{:S(2)}, u32[]{:S(2)}) collective-permute-start(f32[64,2048]{1,0:T(8,128)} %slice_add_fusion.1), channel_id=1, source_target_pairs={{0,32},{32,64},{64,96},{96,128},{128,160},{160,192},{192,224},{224... | collective-permute-start | bytes 1572872 | tf_op jit(solution)/shard_map/ppermute | solution.py:10
  137.5 28.2 %collective-permute-start.10 = (bf16[128,2048]{1,0:T(8,128)(2,1)S(1)}, bf16[128,2048]{1,0:T(8,128)(2,1)S(1)}, u32[]{:S(2)}, u32[]{:S(2)}) collective-permute-start(bf16[128,2048]{1,0:T(8,128)(2,1)S(1)} %fusion.9), channel_id=1, source_target_pairs={{0,32},{32,64},{64,96},{96,128},{128,160},{160,192},{192,224},{224... | collective-permute-start | bytes 1572872 | tf_op jit(solution)/shard_map/ppermute | solution.py:10
  139.4 26.2 %collective-permute-start.9 = (bf16[64,2048]{1,0:T(8,128)(2,1)S(1)}, bf16[64,2048]{1,0:T(8,128)(2,1)S(1)}, u32[]{:S(2)}, u32[]{:S(2)}) collective-permute-start(bf16[64,2048]{1,0:T(8,128)(2,1)S(1)} %get-tuple-element.13), channel_id=1, source_target_pairs={{0,64},{32,96},{64,128},{96,160},{128,192},{160,224},{192,256},{22... | collective-permute-start | bytes 786440 | tf_op jit(solution)/shard_map/ppermute | solution.py:10
  143.8 21.9 %collective-permute-start.11 = (bf16[128,2048]{1,0:T(8,128)(2,1)S(1)}, bf16[128,2048]{1,0:T(8,128)(2,1)S(1)}, u32[]{:S(2)}, u32[]{:S(2)}) collective-permute-start(bf16[128,2048]{1,0:T(8,128)(2,1)S(1)} %fusion.9), channel_id=1, source_target_pairs={{0,480},{32,0},{64,32},{96,64},{128,96},{160,128},{192,160},{224,1... | collective-permute-start | bytes 1572872 | tf_op jit(solution)/shard_map/ppermute | solution.py:10
  146.9 24.5 %copy-start.2 = (bf16[1024,2048]{1,0:T(8,128)(2,1)S(1)}, bf16[1024,2048]{1,0:T(8,128)(2,1)}, u32[]{:S(2)}) copy-start(bf16[1024,2048]{1,0:T(8,128)(2,1)} %param.5) | copy-start | bytes 12582916
  147.0 24.5 %collective-permute-start.12 = (bf16[64,2048]{1,0:T(8,128)(2,1)S(1)}, bf16[64,2048]{1,0:T(8,128)(2,1)S(1)}, u32[]{:S(2)}, u32[]{:S(2)}) collective-permute-start(bf16[64,2048]{1,0:T(8,128)(2,1)S(1)} %get-tuple-element.12), channel_id=1, source_target_pairs={{0,448},{32,480},{64,0},{96,32},{128,64},{160,96},{192,128},{224,1... | collective-permute-start | bytes 786440 | tf_op jit(solution)/shard_map/ppermute | solution.py:10
  175.7 31.3 %all-to-all-start.3 = ((f32[32,32,512]{2,1,0:T(8,128)}), f32[32,32,512]{2,1,0:T(8,128)S(1)}, u32[]{:S(2)}, u32[]{:S(2)}) async-start(f32[32,32,512]{2,1,0:T(8,128)} %bitcast.102), calls=%async_computation.3 | async-start | bytes 4194304 | tf_op jit(solution)/shard_map/all_to_all | solution.py:162
  207.9 17.7 %collective-permute-start.13 = (f32[40,128]{1,0:T(8,128)S(1)}, f32[40,128]{1,0:T(8,128)S(1)}, u32[]{:S(2)}, u32[]{:S(2)}) collective-permute-start(f32[40,128]{1,0:T(8,128)S(1)} %get-tuple-element.22), channel_id=1, source_target_pairs={{0,128},{128,256},{256,384},{384,0},{1,129},{129,257},{257,385},{3... | collective-permute-start | bytes 61448 | tf_op jit(solution)/shard_map/ppermute | solution.py:16
  212.2 14.5 %collective-permute-start.14 = (f32[40,128]{1,0:T(8,128)S(1)}, f32[40,128]{1,0:T(8,128)S(1)}, u32[]{:S(2)}, u32[]{:S(2)}) collective-permute-start(f32[40,128]{1,0:T(8,128)S(1)} %get-tuple-element.21), channel_id=1, source_target_pairs={{0,256},{128,384},{256,0},{384,128},{1,257},{129,385},{257,1},{385... | collective-permute-start | bytes 61448 | tf_op jit(solution)/shard_map/ppermute | solution.py:16
  220.1 9.6 %collective-permute-start.15 = (f32[40,128]{1,0:T(8,128)S(1)}, f32[40,128]{1,0:T(8,128)S(1)}, u32[]{:S(2)}, u32[]{:S(2)}) collective-permute-start(f32[40,128]{1,0:T(8,128)S(1)} %get-tuple-element.20), channel_id=1, source_target_pairs={{0,384},{128,0},{256,128},{384,256},{1,385},{129,1},{257,129},{385... | collective-permute-start | bytes 61448 | tf_op jit(solution)/shard_map/ppermute | solution.py:16

commit v2 on v0

v2 whole, which is shorter than its diff:
```python
import functools

import jax
import jax.numpy as jnp
from jax import lax
from jax.experimental import pallas as pl
from jax.experimental.pallas import tpu as pltpu
from jax.sharding import PartitionSpec as P

loss_scale = 16.0
VMEM_BYTES = 40 * 1024 * 1024


def along_z(value, steps, planes):
    return lax.ppermute(
        value, ("sect", "tok"), [(i, (i + steps) % planes) for i in range(planes)]
    )


def across_vocab(value):
    return lax.all_to_all(value, "vocab", split_axis=0, concat_axis=0, tiled=True)


def window_offsets(token_section, sections):
    return [jnp.where(token_section < sections // 2, -2, 2), -1, 0, 1]


def row_block(plane, sections, toks):
    plane = lax.rem(plane + sections * toks, sections * toks)
    return lax.rem(plane, toks) * sections + lax.div(plane, toks)


def params(**more):
    return pltpu.CompilerParams(vmem_limit_bytes=VMEM_BYTES, **more)


def logits_kernel(first, x_ref, w_ref, *refs):
    *outs, flipped = refs

    @pl.when(pl.program_id(0) == 0)
    def _():
        flipped[...] = x_ref[:, first:].T

    result = jnp.dot(flipped[...], w_ref[...], preferred_element_type=jnp.float32)
    start = 0
    for out in outs:
        out[...] = result[start : start + out.shape[0]]
        start += out.shape[0]


def partial_logits(spread, head_weight, first, last, sizes):
    feats, width = head_weight.shape
    tile = 512
    count = last - first
    return pl.pallas_call(
        functools.partial(logits_kernel, first),
        grid=(width // tile,),
        in_specs=[
            pl.BlockSpec((feats, last), lambda i: (0, 0)),
            pl.BlockSpec((feats, tile), lambda i: (0, i)),
        ],
        out_specs=[pl.BlockSpec((size, tile), lambda i: (0, i)) for size in sizes],
        out_shape=[jax.ShapeDtypeStruct((size, width), jnp.float32) for size in sizes],
        scratch_shapes=[pltpu.VMEM((count, feats), jnp.bfloat16)],
        compiler_params=params(),
        cost_estimate=pl.CostEstimate(
            flops=2 * count * feats * width,
            bytes_accessed=feats * width * 2 + count * width * 4,
            transcendentals=0,
        ),
    )(spread, head_weight)


def stats_kernel(own_ref, lo_a, lo_b, hi_a, hi_b, teacher_ref, logits_ref, stats_ref):
    half = lo_a.shape[0]
    logits_ref[:half] = own_ref[:half] + lo_a[...] + lo_b[...]
    logits_ref[half:] = own_ref[half:] + hi_a[...] + hi_b[...]
    logits = logits_ref[...]
    teacher = teacher_ref[...].astype(jnp.float32)
    top_s = jnp.max(logits, axis=1, keepdims=True)
    top_t = jnp.max(teacher, axis=1, keepdims=True)
    sum_s = jnp.sum(jnp.exp(logits - top_s), axis=1, keepdims=True)
    exp_t = jnp.exp(teacher - top_t)
    sum_t = jnp.sum(exp_t, axis=1, keepdims=True)
    cross = jnp.sum(exp_t * (teacher - logits), axis=1, keepdims=True)
    own = logits.shape[0]
    lane = lax.broadcasted_iota(jnp.int32, (own, 128), 1)
    packed = jnp.zeros((own, 128), jnp.float32)
    for place, column in enumerate((top_s, top_t, sum_s, sum_t, cross)):
        packed = jnp.where(lane == place, column, packed)
    rows = packed.T[:8]
    for k in range(stats_ref.shape[0]):
        stats_ref[k] = rows


def grads_kernel(logits_ref, teacher_ref, stats_ref, grad_ref, low_ref, high_ref, div_ref):
    stats = stats_ref[...]
    top = jnp.max(stats, axis=0)
    scale = jnp.exp(stats[:, :2] - top[None, :2])
    top_s, top_t = top[0:1], top[1:2]
    total_s = jnp.sum(stats[:, 2] * scale[:, 0], axis=0, keepdims=True)
    total_t = jnp.sum(stats[:, 3] * scale[:, 1], axis=0, keepdims=True)
    cross = jnp.sum(stats[:, 4] * scale[:, 1], axis=0, keepdims=True)
    div_ref[...] = cross / total_t - top_t - jnp.log(total_t) + top_s + jnp.log(total_s)
    own = logits_ref.shape[0]
    row = lax.broadcasted_iota(jnp.int32, (128, own), 0)
    packed = jnp.zeros((128, own), jnp.float32)
    for place, values in enumerate((top_s, top_t, loss_scale / total_s, loss_scale / total_t)):
        packed = jnp.where(row == place, values, packed)
    columns = packed.T
    grad = (
        jnp.exp(logits_ref[...] - columns[:, 0:1]) * columns[:, 2:3]
        - jnp.exp(teacher_ref[...].astype(jnp.float32) - columns[:, 1:2]) * columns[:, 3:4]
    ).astype(jnp.bfloat16)
    grad_ref[...] = grad
    low_ref[...] = grad[: own // 2]
    high_ref[...] = grad[own // 2 :]


def hidden_kernel(w_ref, near_below, near_above, far_below, far_above, own_ref, out_ref, window):
    half = far_below.shape[0]

    @pl.when(pl.program_id(0) == 0)
    def _():
        window[:half] = far_below[...]
        window[half : 2 * half] = far_above[...]
        window[2 * half : 3 * half] = near_below[half:]
        window[3 * half : 4 * half] = near_above[:half]
        window[4 * half : 5 * half] = near_below[:half]
        window[5 * half : 6 * half] = near_above[half:]
        window[6 * half :] = own_ref[...]

    out_ref[...] = lax.dot_general(
        w_ref[...], window[...], (((1,), (1,)), ((), ())), preferred_element_type=jnp.float32
    )


def hidden_grads(head_weight, pieces):
    feats, width = head_weight.shape
    rows = sum(piece.shape[0] for piece in pieces)
    tile = 256
    return pl.pallas_call(
        hidden_kernel,
        grid=(feats // tile,),
        in_specs=[pl.BlockSpec((tile, width), lambda i: (i, 0))]
        + [pl.BlockSpec(piece.shape, lambda i: (0, 0)) for piece in pieces],
        out_specs=pl.BlockSpec((tile, rows), lambda i: (i, 0)),
        out_shape=jax.ShapeDtypeStruct((feats, rows), jnp.float32),
        scratch_shapes=[pltpu.VMEM((rows, width), jnp.bfloat16)],
        compiler_params=params(),
        cost_estimate=pl.CostEstimate(
            flops=2 * rows * feats * width,
            bytes_accessed=feats * width * 2 + rows * width * 2 + rows * feats * 4,
            transcendentals=0,
        ),
    )(head_weight, *pieces)


def shards(hidden, head_weight, teacher_logits, pairing):
    sections = lax.axis_size("sect")
    toks = lax.axis_size("tok")
    vocabs = lax.axis_size("vocab")
    planes = sections * toks
    width = head_weight.shape[1]
    feats = hidden.shape[1]
    rows = hidden.shape[0]
    unit = rows // planes
    own = sections * unit
    half = own // 2
    section = lax.axis_index("sect")
    tok = lax.axis_index("tok")

    blocks = []
    for k in range(sections):
        plane = k * toks + tok
        blocks += [row_block(plane + off, sections, toks) for off in window_offsets(section, sections)]
    source = jnp.repeat(jnp.stack(blocks), unit) * unit + jnp.tile(
        jnp.arange(unit, dtype=jnp.int32), sections * 4
    )
    pick = (jnp.arange(rows, dtype=jnp.int32)[:, None] == source[None, :]).astype(jnp.bfloat16)
    picked = lax.dot_general(
        hidden, pick, (((0,), (0,)), ((), ())), preferred_element_type=jnp.float32
    ).astype(jnp.bfloat16)
    by_section = lax.all_to_all(
        picked.reshape(feats, sections, own).transpose(1, 0, 2),
        "sect",
        split_axis=0,
        concat_axis=0,
        tiled=True,
    ).reshape(sections, feats, 4, unit)
    by_section = by_section.transpose(1, 2, 0, 3).reshape(feats, 4, own)
    edges, below, mine, above = (by_section[:, place] for place in range(4))
    window = jnp.concatenate(
        [edges, below[:, half:], above[:, :half], below[:, :half], above[:, half:], mine], axis=1
    )
    spread = across_vocab(jnp.broadcast_to(window[None], (vocabs, feats, rows)))
    spread = spread.reshape(vocabs * feats, rows)

    edge_down, edge_up = partial_logits(spread, head_weight, 0, own, [half, half])
    far_down = along_z(edge_down, -1, planes)
    far_up = along_z(edge_up, 1, planes)
    near_down, near_up, next_down, next_up, kept = partial_logits(
        spread, head_weight, own, rows, [half, half, half, half, own]
    )
    down_b = along_z(near_down, -1, planes)
    up_a = along_z(near_up, 1, planes)
    next_down, next_up = lax.optimization_barrier((next_down + far_down, next_up + far_up))
    down_a = along_z(next_down, -1, planes)
    up_b = along_z(next_up, 1, planes)

    pairs_row = lax.dynamic_slice_in_dim(pairing, section, 1, 0)[0]
    select = (pairs_row[None, :] == jnp.arange(sections, dtype=jnp.int32)[:, None]).astype(
        jnp.bfloat16
    )
    ordered = jnp.dot(select, teacher_logits, preferred_element_type=jnp.float32).astype(
        jnp.bfloat16
    )
    ordered = ordered.reshape(sections, vocabs, width).transpose(1, 0, 2)
    ordered, kept = lax.optimization_barrier((ordered, kept))
    teacher = across_vocab(ordered).transpose(1, 0, 2).reshape(own, width)

    logits, stats = pl.pallas_call(
        stats_kernel,
        out_shape=[
            jax.ShapeDtypeStruct((own, width), jnp.float32),
            jax.ShapeDtypeStruct((vocabs, 8, own), jnp.float32),
        ],
        compiler_params=params(),
    )(kept, down_a, up_a, down_b, up_b, teacher)
    stats = across_vocab(stats)
    grad_logits, low, high, diverge = pl.pallas_call(
        grads_kernel,
        out_shape=[
            jax.ShapeDtypeStruct((own, width), jnp.bfloat16),
            jax.ShapeDtypeStruct((half, width), jnp.bfloat16),
            jax.ShapeDtypeStruct((half, width), jnp.bfloat16),
            jax.ShapeDtypeStruct((1, own), jnp.float32),
        ],
        compiler_params=params(),
    )(logits, teacher, stats)

    near_below = along_z(grad_logits, 1, planes)
    near_above = along_z(grad_logits, -1, planes)
    far_below = along_z(low, 2, planes)
    far_above = along_z(high, -2, planes)
    own_grad = hidden_grads(
        head_weight, [near_below, near_above, far_below, far_above, grad_logits]
    )
    summed = jnp.sum(across_vocab(own_grad.reshape(vocabs, feats, rows)), axis=0)

    pieces = [summed[:, place * half : (place + 1) * half] for place in range(8)]
    returned = jnp.concatenate(
        pieces[:2] + [pieces[4], pieces[2], pieces[6], pieces[7], pieces[3], pieces[5]], axis=1
    )
    returned = returned.reshape(feats, 4, sections, unit).transpose(2, 0, 1, 3)
    returned = returned.reshape(sections, feats, own)
    extra = jnp.pad(diverge.reshape(sections, 1, unit), ((0, 0), (0, 7), (0, own - unit)))
    got = lax.all_to_all(
        jnp.concatenate([returned, extra], axis=1), "sect", split_axis=0, concat_axis=0, tiled=True
    )
    places = got[:, :feats].reshape(sections, feats, 4, unit).transpose(0, 2, 3, 1)
    grads = jnp.zeros((planes, unit, feats), jnp.float32)
    for sender in range(sections):
        for place, off in enumerate(window_offsets(section, sections)):
            grads = lax.dynamic_update_slice(
                grads,
                places[sender, place][None],
                (row_block(sender * toks + tok + off, sections, toks), 0, 0),
            )
    return grads.reshape(rows, feats), got[:, feats, :unit].reshape(own)


def solution(mesh):
    placed = (
        P("sect", ("tok", "vocab")),
        P("tok", "vocab"),
        P(("sect", "tok", "vocab"), None),
        P(),
    )
    return jax.shard_map(
        shards,
        mesh=mesh,
        in_specs=placed,
        out_specs=(P("sect", ("tok", "vocab")), P(("sect", "tok"))),
        check_vma=False,
    )
```

time: 644 us -> 206 us (0.32)
  the two profiles are of different devices: /device:TPU:6 before, /device:TPU:64 now
where the time goes in v2:
time: 206 us; the launch traced here: 205 us
  blocking collectives  76.9 us (37%)
  waiting for transfers between devices  61.1 us (30%)
  starting transfers between devices  41 us (20%)
  local copies, waits for them, and re-layouts  10.6 us (5%)
  Pallas kernels  10.4 us (5%)
  other arithmetic  2.68 us (1%)
    all_to_all x3, blocking collectives, across_vocab(): lax.all_to_all(value, 'vocab', split_axis=0, concat_axis=0, tiled=True)  51.1 us
    ppermute x10, starting transfers between devices, along_z(): lax.ppermute(value, ('sect', 'tok'), [(i, (i + steps) % planes) for i in...  31.5 us
    all_to_all x1, waiting for transfers between devices, across_vocab(): lax.all_to_all(value, 'vocab', split_axis=0, concat_axis=0, tiled=True)  28.7 us
    all_to_all x1, blocking collectives, shards(): lax.all_to_all(picked.reshape(feats, sections, own).transpose(1, 0, 2), '...  25.8 us
    ppermute x10, waiting for transfers between devices, along_z(): lax.ppermute(value, ('sect', 'tok'), [(i, (i + steps) % planes) for i in...  18.9 us
    all_to_all x1, waiting for transfers between devices, shards(): lax.all_to_all(jnp.concatenate([returned, extra], axis=1), 'sect', split_...  13.6 us
    all_to_all x1, starting transfers between devices, shards(): lax.all_to_all(jnp.concatenate([returned, extra], axis=1), 'sect', split_...  5.55 us
    pallas_call x2, Pallas kernels, partial_logits(): pl.pallas_call(functools.partial(logits_kernel, first), grid=(width // ti...  5.03 us
  transfers between devices with their start and end apart: 12, of which 5 were waited for; matrix products, arithmetic and copies ran while one was open for 2% of the time, Pallas kernels for 2%

profile of v2, /device:TPU:64, one launch (start us, length us, event | category | flops | bytes accessed | tf_op | source)
XLA Modules:
  0.0 205.5 jit_solution(5636433297531686583)
XLA Ops:
  0.9 0.1 stack.67
  1.2 1.0 fusion
  2.3 25.8 %all_to_all.30 = bf16[4,32,128]{2,1,0:T(8,128)(2,1)S(1)} all-to-all(bf16[4,32,128]{2,1,0:T(8,128)(2,1)S(1)} %bitcast.127), channel_id=1, replica_groups=mesh['sect'=4,'tok'=4,'vocab'=32] {'sect'}, dimensions={0} | all-to-all | bytes 65536 | tf_op jit(solution)/shard_map/all_to_all | solution.py:184
  28.1 0.1 reshape.57
  28.2 0.1 copy.105
  28.3 0.1 reshape.58
  28.5 0.1 concatenate.10
  28.6 0.1 broadcast_in_dim.8
  28.7 24.5 %all_to_all.31 = bf16[32,32,512]{2,1,0:T(8,128)(2,1)S(1)} all-to-all(bf16[32,32,512]{2,1,0:T(8,128)(2,1)S(1)} %broadcast_in_dim.8), channel_id=1, replica_groups=mesh['sect'=4,'tok'=4,'vocab'=32] {'vocab'}, dimensions={0} | all-to-all | bytes 2097152 | tf_op jit(solution)/shard_map/all_to_all | solution.py:21
  53.2 2.2 %copy-done.1 = bf16[1024,2048]{1,0:T(8,128)(2,1)S(1)} copy-done((bf16[1024,2048]{1,0:T(8,128)(2,1)S(1)}, bf16[1024,2048]{1,0:T(8,128)(2,1)}, u32[]{:S(2)}) %copy-start.1) | copy-done | bytes 4194328
  55.4 1.9 shard_map.60
  57.3 2.9 %collective-permute-start.1 = (f32[64,2048]{1,0:T(8,128)S(1)}, f32[64,2048]{1,0:T(8,128)}, u32[]{:S(2)}, u32[]{:S(2)}) collective-permute-start(f32[64,2048]{1,0:T(8,128)S(1)} %get-tuple-element.24), channel_id=1, source_target_pairs={{0,32},{32,64},{64,96},{96,128},{128,160},{160,192},{192,224},{224... | collective-permute-start | bytes 1572872 | tf_op jit(solution)/shard_map/ppermute | solution.py:15
  60.2 2.9 %collective-permute-start = (f32[64,2048]{1,0:T(8,128)S(1)}, f32[64,2048]{1,0:T(8,128)S(1)}, u32[]{:S(2)}, u32[]{:S(2)}) collective-permute-start(f32[64,2048]{1,0:T(8,128)S(1)} %get-tuple-element.22), channel_id=1, source_target_pairs={{0,480},{32,0},{64,32},{96,64},{128,96},{160,128},{192,160},{224,1... | collective-permute-start | bytes 1572872 | tf_op jit(solution)/shard_map/ppermute | solution.py:15
  63.2 0.7 dynamic-slice_bitcast_fusion
  63.9 2.2 %copy-done.2 = bf16[1024,2048]{1,0:T(8,128)(2,1)S(1)} copy-done((bf16[1024,2048]{1,0:T(8,128)(2,1)S(1)}, bf16[1024,2048]{1,0:T(8,128)(2,1)}, u32[]{:S(2)}) %copy-start.2) | copy-done | bytes 4194328
  66.0 3.1 %shard_map.59 = (f32[64,2048]{1,0:T(8,128)S(1)}, f32[64,2048]{1,0:T(8,128)S(1)}, f32[64,2048]{1,0:T(8,128)S(1)}, f32[64,2048]{1,0:T(8,128)S(1)}, f32[128,2048]{1,0:T(8,128)S(1)}) custom-call(bf16[1024,512]{1,0:T(8,128)(2,1)S(1)} %bitcast.121, bf16[1024,2048]{1,0:T(8,128)(2,1)S(1)} %copy-done.2), custom_call_target="tpu_custom_call" | custom-call | flops 1610612736 | bytes 7340032 | tf_op jit(solution)/shard_map/pallas_call | solution.py:55
  69.2 2.9 %collective-permute-start.3 = (f32[64,2048]{1,0:T(8,128)S(1)}, f32[64,2048]{1,0:T(8,128)S(1)}, u32[]{:S(2)}, u32[]{:S(2)}) collective-permute-start(f32[64,2048]{1,0:T(8,128)S(1)} %get-tuple-element.26), channel_id=1, source_target_pairs={{0,32},{32,64},{64,96},{96,128},{128,160},{160,192},{192,224},{224... | collective-permute-start | bytes 1572872 | tf_op jit(solution)/shard_map/ppermute | solution.py:15
  72.1 2.9 %collective-permute-start.4 = (f32[64,2048]{1,0:T(8,128)S(1)}, f32[64,2048]{1,0:T(8,128)S(1)}, u32[]{:S(2)}, u32[]{:S(2)}) collective-permute-start(f32[64,2048]{1,0:T(8,128)S(1)} %get-tuple-element.27), channel_id=1, source_target_pairs={{0,480},{32,0},{64,32},{96,64},{128,96},{160,128},{192,160},{224,1... | collective-permute-start | bytes 1572872 | tf_op jit(solution)/shard_map/ppermute | solution.py:15
  75.0 1.1 add.327
  76.2 3.1 %collective-permute-start.2 = (f32[64,2048]{1,0:T(8,128)S(1)}, f32[64,2048]{1,0:T(8,128)S(1)}, u32[]{:S(2)}, u32[]{:S(2)}) collective-permute-start(f32[64,2048]{1,0:T(8,128)S(1)} %add.326), channel_id=1, source_target_pairs={{0,480},{32,0},{64,32},{96,64},{128,96},{160,128},{192,160},{224,1... | collective-permute-start | bytes 1572872 | tf_op jit(solution)/shard_map/ppermute | solution.py:15
  79.4 2.7 %collective-permute-start.5 = (f32[64,2048]{1,0:T(8,128)S(1)}, f32[64,2048]{1,0:T(8,128)S(1)}, u32[]{:S(2)}, u32[]{:S(2)}) collective-permute-start(f32[64,2048]{1,0:T(8,128)S(1)} %add.327), channel_id=1, source_target_pairs={{0,32},{32,64},{64,96},{96,128},{128,160},{160,192},{192,224},{224... | collective-permute-start | bytes 1572872 | tf_op jit(solution)/shard_map/ppermute | solution.py:15
  82.1 0.4 convolution_convert_fusion
  82.5 15.0 %all_to_all.32 = bf16[32,4,2048]{2,1,0:T(4,128)(2,1)S(1)} all-to-all(bf16[32,4,2048]{2,1,0:T(4,128)(2,1)S(1)} %bitcast.122), channel_id=1, replica_groups=mesh['sect'=4,'tok'=4,'vocab'=32] {'vocab'}, dimensions={0} | all-to-all | bytes 1048576 | tf_op jit(solution)/shard_map/all_to_all | solution.py:21
  97.5 0.3 copy.83
  97.9 0.5 collective-permute-done.2.lo_a
  98.4 0.7 shard_map.61
  99.1 11.6 %all_to_all.33.stats_ref = f32[32,8,128]{2,1,0:T(8,128)S(1)} all-to-all(f32[32,8,128]{2,1,0:T(8,128)S(1)} %get-tuple-element.31), channel_id=1, replica_groups=mesh['sect'=4,'tok'=4,'vocab'=32] {'vocab'}, dimensions={0} | all-to-all | bytes 262144 | tf_op jit(solution)/shard_map/all_to_all | solution.py:21
  110.6 0.6 shard_map.62
  111.2 4.6 %collective-permute-start.6 = (bf16[128,2048]{1,0:T(8,128)(2,1)S(1)}, bf16[128,2048]{1,0:T(8,128)(2,1)S(1)}, u32[]{:S(2)}, u32[]{:S(2)}) collective-permute-start(bf16[128,2048]{1,0:T(8,128)(2,1)S(1)} %get-tuple-element.32.own_ref), channel_id=1, source_target_pairs={{0,32},{32,64},{64,96},{96,128},{128,160},{160,192},{192,224},{224... | collective-permute-start | bytes 1572872 | tf_op jit(solution)/shard_map/ppermute | solution.py:15
  115.9 1.9 collective-permute-start.7
  117.8 4.6 %collective-permute-start.8 = (bf16[64,2048]{1,0:T(8,128)(2,1)S(1)}, bf16[64,2048]{1,0:T(8,128)(2,1)S(1)}, u32[]{:S(2)}, u32[]{:S(2)}) collective-permute-start(bf16[64,2048]{1,0:T(8,128)(2,1)S(1)} %get-tuple-element.33), channel_id=1, source_target_pairs={{0,64},{32,96},{64,128},{96,160},{128,192},{160,224},{192,256},{22... | collective-permute-start | bytes 786440 | tf_op jit(solution)/shard_map/ppermute | solution.py:15
  122.4 2.8 %collective-permute-start.9 = (bf16[64,2048]{1,0:T(8,128)(2,1)S(1)}, bf16[64,2048]{1,0:T(8,128)(2,1)S(1)}, u32[]{:S(2)}, u32[]{:S(2)}) collective-permute-start(bf16[64,2048]{1,0:T(8,128)(2,1)S(1)} %get-tuple-element.34), channel_id=1, source_target_pairs={{0,448},{32,480},{64,0},{96,32},{128,64},{160,96},{192,128},{224,1... | collective-permute-start | bytes 786440 | tf_op jit(solution)/shard_map/ppermute | solution.py:15
  125.2 13.3 %collective-permute-done.8.far_below = bf16[64,2048]{1,0:T(8,128)(2,1)S(1)} collective-permute-done((bf16[64,2048]{1,0:T(8,128)(2,1)S(1)}, bf16[64,2048]{1,0:T(8,128)(2,1)S(1)}, u32[]{:S(2)}, u32[]{:S(2)}) %collective-permute-start.8) | collective-permute-done | bytes 262176 | tf_op jit(solution)/shard_map/ppermute | solution.py:15
  138.5 5.1 %collective-permute-done.9.far_above = bf16[64,2048]{1,0:T(8,128)(2,1)S(1)} collective-permute-done((bf16[64,2048]{1,0:T(8,128)(2,1)S(1)}, bf16[64,2048]{1,0:T(8,128)(2,1)S(1)}, u32[]{:S(2)}, u32[]{:S(2)}) %collective-permute-start.9) | collective-permute-done | bytes 262176 | tf_op jit(solution)/shard_map/ppermute | solution.py:15
  143.6 4.0 %shard_map.63 = f32[1024,512]{1,0:T(8,128)} custom-call(bf16[1024,2048]{1,0:T(8,128)(2,1)S(1)} %copy-done.3, bf16[128,2048]{1,0:T(8,128)(2,1)S(1)} %collective-permute-done.6.near_below, bf16[128,2048]{1,0:T(8,128)(2,1)S(1)} %collective-permute-done.7.near_above, bf16[64,2048]{1,0:T(8,128)(2,1)S(1)} %collective-permute-done.8.far_below, ...), custom_call_target="tpu_custom_call" | custom-call | flops 2147483648 | bytes 8388608 | tf_op jit(solution)/shard_map/pallas_call | solution.py:142
  147.6 4.0 %all-to-all-start.4 = ((f32[32,32,512]{2,1,0:T(8,128)}), f32[32,32,512]{2,1,0:T(8,128)S(1)}, u32[]{:S(2)}, u32[]{:S(2)}) async-start(f32[32,32,512]{2,1,0:T(8,128)} %bitcast.29), calls=%async_computation.4 | async-start | bytes 4194304 | tf_op jit(solution)/shard_map/all_to_all | solution.py:21
  151.6 0.6 broadcast.53
  152.2 0.7 reduce.7
  153.0 28.7 %all-to-all-done.4 = f32[32,32,512]{2,1,0:T(8,128)S(1)} async-done(((f32[32,32,512]{2,1,0:T(8,128)}), f32[32,32,512]{2,1,0:T(8,128)S(1)}, u32[]{:S(2)}, u32[]{:S(2)}) %all-to-all-start.4) | async-done | bytes 2097184 | tf_op jit(solution)/shard_map/all_to_all | solution.py:21
  181.6 0.1 reduce_sum.9
  181.9 0.2 reshape.62
  182.2 0.2 reshape.63
  182.4 0.7 select_maximum_fusion
  183.0 5.5 %all-to-all-start.5 = ((f32[4,40,128]{2,1,0:T(8,128)}), f32[4,40,128]{2,1,0:T(8,128)S(1)}, u32[]{:S(2)}, u32[]{:S(2)}) async-start(f32[4,40,128]{2,1,0:T(8,128)} %select_maximum_fusion), calls=%async_computation.5 | async-start | bytes 163840 | tf_op jit(solution)/shard_map/all_to_all | solution.py:258
  188.6 13.6 %all-to-all-done.5 = f32[4,40,128]{2,1,0:T(8,128)S(1)} async-done(((f32[4,40,128]{2,1,0:T(8,128)}), f32[4,40,128]{2,1,0:T(8,128)S(1)}, u32[]{:S(2)}, u32[]{:S(2)}) %all-to-all-start.5) | async-done | bytes 81952 | tf_op jit(solution)/shard_map/all_to_all | solution.py:258
  202.2 0.2 reshape.65
  202.3 0.2 slice_bitcast_fusion
  202.6 0.1 dynamic_update_slice.48
  202.7 0.1 dynamic_update_slice.49
  202.8 0.1 dynamic_update_slice.50
  202.9 0.1 dynamic_update_slice.51
  203.0 0.1 dynamic_update_slice.52
  203.1 0.1 dynamic_update_slice.53
  203.2 0.1 dynamic_update_slice.54
  203.3 0.1 dynamic_update_slice.55
  203.3 0.1 dynamic_update_slice.56
  203.4 0.1 dynamic_update_slice.57
  203.5 0.1 dynamic_update_slice.58
  203.6 0.1 dynamic_update_slice.59
  203.7 0.1 dynamic_update_slice.60
  203.9 0.1 dynamic_update_slice.62
  204.0 0.1 dynamic_update_slice.63
  204.1 0.8 reshape.66
  204.9 0.6 reshape_squeeze.3
  (29 shorter events, 0.8 us)
Async XLA Ops:
  0.6 81.5 %copy-start = (bf16[4,65536]{1,0:T(4,128)(2,1)S(1)}, bf16[4,65536]{1,0:T(4,128)(2,1)}, u32[]{:S(2)}) copy-start(bf16[4,65536]{1,0:T(4,128)(2,1)} %param.6) | copy-start | bytes 1572868
  53.2 2.2 %copy-start.1 = (bf16[1024,2048]{1,0:T(8,128)(2,1)S(1)}, bf16[1024,2048]{1,0:T(8,128)(2,1)}, u32[]{:S(2)}) copy-start(bf16[1024,2048]{1,0:T(8,128)(2,1)} %w_ref.5) | copy-start | bytes 12582916
  57.3 17.7 %collective-permute-start.1 = (f32[64,2048]{1,0:T(8,128)S(1)}, f32[64,2048]{1,0:T(8,128)}, u32[]{:S(2)}, u32[]{:S(2)}) collective-permute-start(f32[64,2048]{1,0:T(8,128)S(1)} %get-tuple-element.24), channel_id=1, source_target_pairs={{0,32},{32,64},{64,96},{96,128},{128,160},{160,192},{192,224},{224... | collective-permute-start | bytes 1572872 | tf_op jit(solution)/shard_map/ppermute | solution.py:15
  60.2 15.9 %collective-permute-start = (f32[64,2048]{1,0:T(8,128)S(1)}, f32[64,2048]{1,0:T(8,128)S(1)}, u32[]{:S(2)}, u32[]{:S(2)}) collective-permute-start(f32[64,2048]{1,0:T(8,128)S(1)} %get-tuple-element.22), channel_id=1, source_target_pairs={{0,480},{32,0},{64,32},{96,64},{128,96},{160,128},{192,160},{224,1... | collective-permute-start | bytes 1572872 | tf_op jit(solution)/shard_map/ppermute | solution.py:15
  63.9 2.2 %copy-start.2 = (bf16[1024,2048]{1,0:T(8,128)(2,1)S(1)}, bf16[1024,2048]{1,0:T(8,128)(2,1)}, u32[]{:S(2)}) copy-start(bf16[1024,2048]{1,0:T(8,128)(2,1)} %w_ref.5) | copy-start | bytes 12582916
  69.2 28.7 %collective-permute-start.3 = (f32[64,2048]{1,0:T(8,128)S(1)}, f32[64,2048]{1,0:T(8,128)S(1)}, u32[]{:S(2)}, u32[]{:S(2)}) collective-permute-start(f32[64,2048]{1,0:T(8,128)S(1)} %get-tuple-element.26), channel_id=1, source_target_pairs={{0,32},{32,64},{64,96},{96,128},{128,160},{160,192},{192,224},{224... | collective-permute-start | bytes 1572872 | tf_op jit(solution)/shard_map/ppermute | solution.py:15
  72.1 25.7 %collective-permute-start.4 = (f32[64,2048]{1,0:T(8,128)S(1)}, f32[64,2048]{1,0:T(8,128)S(1)}, u32[]{:S(2)}, u32[]{:S(2)}) collective-permute-start(f32[64,2048]{1,0:T(8,128)S(1)} %get-tuple-element.27), channel_id=1, source_target_pairs={{0,480},{32,0},{64,32},{96,64},{128,96},{160,128},{192,160},{224,1... | collective-permute-start | bytes 1572872 | tf_op jit(solution)/shard_map/ppermute | solution.py:15
  76.2 22.1 %collective-permute-start.2 = (f32[64,2048]{1,0:T(8,128)S(1)}, f32[64,2048]{1,0:T(8,128)S(1)}, u32[]{:S(2)}, u32[]{:S(2)}) collective-permute-start(f32[64,2048]{1,0:T(8,128)S(1)} %add.326), channel_id=1, source_target_pairs={{0,480},{32,0},{64,32},{96,64},{128,96},{160,128},{192,160},{224,1... | collective-permute-start | bytes 1572872 | tf_op jit(solution)/shard_map/ppermute | solution.py:15
  79.4 19.0 %collective-permute-start.5 = (f32[64,2048]{1,0:T(8,128)S(1)}, f32[64,2048]{1,0:T(8,128)S(1)}, u32[]{:S(2)}, u32[]{:S(2)}) collective-permute-start(f32[64,2048]{1,0:T(8,128)S(1)} %add.327), channel_id=1, source_target_pairs={{0,32},{32,64},{64,96},{96,128},{128,160},{160,192},{192,224},{224... | collective-permute-start | bytes 1572872 | tf_op jit(solution)/shard_map/ppermute | solution.py:15
  98.4 45.2 %copy-start.3 = (bf16[1024,2048]{1,0:T(8,128)(2,1)S(1)}, bf16[1024,2048]{1,0:T(8,128)(2,1)}, u32[]{:S(2)}) copy-start(bf16[1024,2048]{1,0:T(8,128)(2,1)} %w_ref.5) | copy-start | bytes 12582916
  111.2 32.4 %collective-permute-start.6 = (bf16[128,2048]{1,0:T(8,128)(2,1)S(1)}, bf16[128,2048]{1,0:T(8,128)(2,1)S(1)}, u32[]{:S(2)}, u32[]{:S(2)}) collective-permute-start(bf16[128,2048]{1,0:T(8,128)(2,1)S(1)} %get-tuple-element.32.own_ref), channel_id=1, source_target_pairs={{0,32},{32,64},{64,96},{96,128},{128,160},{160,192},{192,224},{224... | collective-permute-start | bytes 1572872 | tf_op jit(solution)/shard_map/ppermute | solution.py:15
  115.9 27.7 %collective-permute-start.7 = (bf16[128,2048]{1,0:T(8,128)(2,1)S(1)}, bf16[128,2048]{1,0:T(8,128)(2,1)S(1)}, u32[]{:S(2)}, u32[]{:S(2)}) collective-permute-start(bf16[128,2048]{1,0:T(8,128)(2,1)S(1)} %get-tuple-element.32.own_ref), channel_id=1, source_target_pairs={{0,480},{32,0},{64,32},{96,64},{128,96},{160,128},{192,160},{224,1... | collective-permute-start | bytes 1572872 | tf_op jit(solution)/shard_map/ppermute | solution.py:15
  117.8 20.7 %collective-permute-start.8 = (bf16[64,2048]{1,0:T(8,128)(2,1)S(1)}, bf16[64,2048]{1,0:T(8,128)(2,1)S(1)}, u32[]{:S(2)}, u32[]{:S(2)}) collective-permute-start(bf16[64,2048]{1,0:T(8,128)(2,1)S(1)} %get-tuple-element.33), channel_id=1, source_target_pairs={{0,64},{32,96},{64,128},{96,160},{128,192},{160,224},{192,256},{22... | collective-permute-start | bytes 786440 | tf_op jit(solution)/shard_map/ppermute | solution.py:15
  122.4 21.2 %collective-permute-start.9 = (bf16[64,2048]{1,0:T(8,128)(2,1)S(1)}, bf16[64,2048]{1,0:T(8,128)(2,1)S(1)}, u32[]{:S(2)}, u32[]{:S(2)}) collective-permute-start(bf16[64,2048]{1,0:T(8,128)(2,1)S(1)} %get-tuple-element.34), channel_id=1, source_target_pairs={{0,448},{32,480},{64,0},{96,32},{128,64},{160,96},{192,128},{224,1... | collective-permute-start | bytes 786440 | tf_op jit(solution)/shard_map/ppermute | solution.py:15
  147.6 34.0 %all-to-all-start.4 = ((f32[32,32,512]{2,1,0:T(8,128)}), f32[32,32,512]{2,1,0:T(8,128)S(1)}, u32[]{:S(2)}, u32[]{:S(2)}) async-start(f32[32,32,512]{2,1,0:T(8,128)} %bitcast.29), calls=%async_computation.4 | async-start | bytes 4194304 | tf_op jit(solution)/shard_map/all_to_all | solution.py:21
  183.0 19.1 %all-to-all-start.5 = ((f32[4,40,128]{2,1,0:T(8,128)}), f32[4,40,128]{2,1,0:T(8,128)S(1)}, u32[]{:S(2)}, u32[]{:S(2)}) async-start(f32[4,40,128]{2,1,0:T(8,128)} %select_maximum_fusion), calls=%async_computation.5 | async-start | bytes 163840 | tf_op jit(solution)/shard_map/all_to_all | solution.py:258

commit v3 on v2

v3 whole, which is shorter than its diff:
```python
import functools

import jax
import jax.numpy as jnp
from jax import lax
from jax.experimental import pallas as pl
from jax.experimental.pallas import tpu as pltpu
from jax.sharding import PartitionSpec as P

loss_scale = 16.0
VMEM_BYTES = 24 * 1024 * 1024
SMEM = pl.BlockSpec(memory_space=pltpu.SMEM)
VMEM = pl.BlockSpec(memory_space=pltpu.VMEM)


def along_z(value, steps, planes):
    return lax.ppermute(
        value, ("sect", "tok"), [(i, (i + steps) % planes) for i in range(planes)]
    )


def exchange(value, axis, **groups):
    return lax.all_to_all(value, axis, split_axis=0, concat_axis=0, tiled=True, **groups)


def params():
    return pltpu.CompilerParams(vmem_limit_bytes=VMEM_BYTES)


def cost(flops, bytes_accessed):
    return pl.CostEstimate(flops=flops, bytes_accessed=bytes_accessed, transcendentals=0)


def window_block(section, tok, token_section, piece, sections, toks):
    planes = sections * toks
    near = jnp.int32(piece - 2)
    far = jnp.where(token_section < sections // 2, -2, 2)
    plane = lax.rem(section * toks + tok + (far if piece == 0 else near) + planes, planes)
    return lax.rem(plane, toks) * sections + lax.div(plane, toks)


def window_order(sections):
    low = list(range(sections // 2))
    high = list(range(sections // 2, sections))
    order = [(0, s) for s in low + high]
    order += [(1, s) for s in high] + [(3, s) for s in low]
    order += [(1, s) for s in low] + [(3, s) for s in high]
    return order + [(2, s) for s in low + high]


def pick_kernel(place_ref, hidden_ref, picked_ref, *, toks):
    sections, _, own = picked_ref.shape
    rows = hidden_ref.shape[1]
    unit = own // 4
    section, tok = place_ref[0], place_ref[1]
    lane = lax.broadcasted_iota(jnp.int32, (rows, own), 1)
    row = lax.broadcasted_iota(jnp.int32, (rows, own), 0)
    for k in range(sections):
        source = lane
        for piece in range(4):
            block = window_block(jnp.int32(k), tok, section, piece, sections, toks)
            source = jnp.where(
                (lane >= piece * unit) & (lane < (piece + 1) * unit),
                (block - piece) * unit + lane,
                source,
            )
        pick = jnp.where(row == source, 1.0, 0.0).astype(jnp.bfloat16)
        picked_ref[k] = jnp.dot(
            hidden_ref[...], pick, preferred_element_type=jnp.float32
        ).astype(jnp.bfloat16)


def arrange_kernel(got_ref, spread_ref):
    sections, _, own = got_ref.shape
    rows = spread_ref.shape[2]
    unit = own // 4
    lane = lax.broadcasted_iota(jnp.int32, (own, rows), 1)
    row = lax.broadcasted_iota(jnp.int32, (own, rows), 0)
    total = None
    for s in range(sections):
        source = jnp.full((own, rows), -1, jnp.int32)
        for place, (piece, token_section) in enumerate(window_order(sections)):
            if token_section == s:
                source = jnp.where(
                    (lane >= place * unit) & (lane < (place + 1) * unit),
                    lane + (piece - place) * unit,
                    source,
                )
        move = jnp.where(row == source, 1.0, 0.0).astype(jnp.bfloat16)
        part = jnp.dot(got_ref[s], move, preferred_element_type=jnp.float32)
        total = part if total is None else total + part
    window = total.astype(jnp.bfloat16)
    for k in range(spread_ref.shape[0]):
        spread_ref[k] = window


def logits_kernel(first, x_ref, w_ref, *refs):
    *outs, flipped = refs

    @pl.when(pl.program_id(0) == 0)
    def _():
        flipped[...] = x_ref[:, first:].T

    result = jnp.dot(flipped[...], w_ref[...], preferred_element_type=jnp.float32)
    start = 0
    for out in outs:
        out[...] = result[start : start + out.shape[0]]
        start += out.shape[0]


def partial_logits(spread, head_weight, first, sizes):
    feats, width = head_weight.shape
    tile = 512
    count = sum(sizes)
    return pl.pallas_call(
        functools.partial(logits_kernel, first),
        grid=(width // tile,),
        in_specs=[
            pl.BlockSpec((feats, first + count), lambda i: (0, 0)),
            pl.BlockSpec((feats, tile), lambda i: (0, i)),
        ],
        out_specs=[pl.BlockSpec((size, tile), lambda i: (0, i)) for size in sizes],
        out_shape=[jax.ShapeDtypeStruct((size, width), jnp.float32) for size in sizes],
        scratch_shapes=[pltpu.VMEM((count, feats), jnp.bfloat16)],
        compiler_params=params(),
        cost_estimate=cost(
            2 * count * feats * width, feats * width * 2 + count * (feats * 2 + width * 4)
        ),
    )(spread, head_weight)


def order_kernel(place_ref, pairing_ref, teacher_ref, after_ref, ordered_ref):
    vocabs, sections, width = ordered_ref.shape
    section = place_ref[0]
    paired = [pairing_ref[section, k] for k in range(sections)]
    for v in range(vocabs):
        rows = teacher_ref[:, v * width : (v + 1) * width].astype(jnp.float32)
        row = lax.broadcasted_iota(jnp.int32, (sections, width), 0)
        out = jnp.zeros((sections, width), jnp.float32)
        for k in range(sections):
            out = jnp.where(row == paired[k], rows[k : k + 1], out)
        ordered_ref[v] = out.astype(jnp.bfloat16)


def add_kernel(down_ref, far_down_ref, up_ref, far_up_ref, down_out, up_out):
    down_out[...] = down_ref[...] + far_down_ref[...]
    up_out[...] = up_ref[...] + far_up_ref[...]


def stats_kernel(own_ref, lo_a, lo_b, hi_a, hi_b, teacher_ref, logits_ref, stats_ref):
    half = lo_a.shape[0]
    logits_ref[:half] = own_ref[:half] + lo_a[...] + lo_b[...]
    logits_ref[half:] = own_ref[half:] + hi_a[...] + hi_b[...]
    logits = logits_ref[...]
    teacher = teacher_ref[...].astype(jnp.float32)
    top_s = jnp.max(logits, axis=1, keepdims=True)
    top_t = jnp.max(teacher, axis=1, keepdims=True)
    sum_s = jnp.sum(jnp.exp(logits - top_s), axis=1, keepdims=True)
    exp_t = jnp.exp(teacher - top_t)
    sum_t = jnp.sum(exp_t, axis=1, keepdims=True)
    cross = jnp.sum(exp_t * (teacher - logits), axis=1, keepdims=True)
    own = logits.shape[0]
    lane = lax.broadcasted_iota(jnp.int32, (own, 128), 1)
    packed = jnp.zeros((own, 128), jnp.float32)
    for place, column in enumerate((top_s, top_t, sum_s, sum_t, cross)):
        packed = jnp.where(lane == place, column, packed)
    rows = packed.T[:8]
    for k in range(stats_ref.shape[0]):
        stats_ref[k] = rows


def grads_kernel(logits_ref, teacher_ref, stats_ref, low_ref, high_ref, div_ref):
    stats = stats_ref[...]
    top = jnp.max(stats, axis=0)
    scale = jnp.exp(stats[:, :2] - top[None, :2])
    top_s, top_t = top[0:1], top[1:2]
    total_s = jnp.sum(stats[:, 2] * scale[:, 0], axis=0, keepdims=True)
    total_t = jnp.sum(stats[:, 3] * scale[:, 1], axis=0, keepdims=True)
    cross = jnp.sum(stats[:, 4] * scale[:, 1], axis=0, keepdims=True)
    div_ref[...] = cross / total_t - top_t - jnp.log(total_t) + top_s + jnp.log(total_s)
    own = logits_ref.shape[0]
    half = own // 2
    row = lax.broadcasted_iota(jnp.int32, (128, own), 0)
    packed = jnp.zeros((128, own), jnp.float32)
    for place, values in enumerate((top_s, top_t, loss_scale / total_s, loss_scale / total_t)):
        packed = jnp.where(row == place, values, packed)
    columns = packed.T
    grad = (
        jnp.exp(logits_ref[...] - columns[:, 0:1]) * columns[:, 2:3]
        - jnp.exp(teacher_ref[...].astype(jnp.float32) - columns[:, 1:2]) * columns[:, 3:4]
    ).astype(jnp.bfloat16)
    low_ref[...] = grad[:half]
    high_ref[...] = grad[half:]


def hidden_kernel(place_ref, w_ref, *refs):
    *pieces, keep_ref, send_ref, window = refs

    @pl.when(pl.program_id(0) == 0)
    def _():
        start = 0
        for piece in pieces:
            window[start : start + piece.shape[0]] = piece[...]
            start += piece.shape[0]

    pairs, feats, rows = keep_ref.shape
    result = lax.dot_general(
        w_ref[...], window[...], (((1,), (1,)), ((), ())), preferred_element_type=jnp.float32
    ).reshape(pairs, 2, feats, rows)
    core = lax.rem(place_ref[2], 2)

    @pl.when(core == 0)
    def _():
        keep_ref[...] = result[:, 0]
        send_ref[...] = result[:, 1]

    @pl.when(core != 0)
    def _():
        keep_ref[...] = result[:, 1]
        send_ref[...] = result[:, 0]


def hidden_grads(place, head_weight, pieces, pairs):
    feats, width = head_weight.shape
    rows = sum(piece.shape[0] for piece in pieces)
    steps = 2
    shape = jax.ShapeDtypeStruct((pairs, feats // (2 * pairs), rows), jnp.float32)
    block = pl.BlockSpec((pairs // steps,) + shape.shape[1:], lambda i: (i, 0, 0))
    return pl.pallas_call(
        hidden_kernel,
        grid=(steps,),
        in_specs=[SMEM, pl.BlockSpec((feats // steps, width), lambda i: (i, 0))]
        + [pl.BlockSpec(piece.shape, lambda i: (0, 0)) for piece in pieces],
        out_specs=[block, block],
        out_shape=[shape, shape],
        scratch_shapes=[pltpu.VMEM((rows, width), jnp.bfloat16)],
        compiler_params=params(),
        cost_estimate=cost(
            2 * rows * feats * width, feats * width * 2 + rows * width * 2 + rows * feats * 4
        ),
    )(place, head_weight, *pieces)


def regroup_kernel(place_ref, parts_ref, div_ref, out_ref):
    sections, height, own = out_ref.shape
    _, feats, _ = parts_ref.shape
    unit = own // 4
    summed = jnp.sum(parts_ref[...], axis=0)
    lane = lax.broadcasted_iota(jnp.int32, (feats, own), 1)
    order = window_order(sections)
    for s in range(sections):
        out = jnp.zeros((feats, own), jnp.float32)
        for piece in range(4):
            start = order.index((piece, s)) * unit
            whole = start // own * own
            turned = pltpu.roll(
                summed[:, whole : whole + own], (piece * unit - start + whole) % own, 1
            )
            out = jnp.where((lane >= piece * unit) & (lane < (piece + 1) * unit), turned, out)
        out_ref[s, :feats] = out
    section = place_ref[0]
    values = jnp.broadcast_to(div_ref[...], (height - feats, own))
    small = lane[: height - feats]
    for s in range(sections):
        out = jnp.zeros_like(values)
        for mine in range(sections):
            turned = pltpu.roll(values, (mine - s) * unit % own, 1)
            inside = (small >= mine * unit) & (small < (mine + 1) * unit)
            out = jnp.where(inside & (section == mine), turned, out)
        out_ref[s, feats:] = out


def return_kernel(place_ref, got_ref, grads_ref, div_ref, ordered, *, toks):
    sections, _, own = got_ref.shape
    unit = own // 4
    feats = grads_ref.shape[0]
    for sender in range(sections):
        turned = got_ref[sender, :feats, :].T
        for piece in range(4):
            block = window_block(
                jnp.int32(sender), place_ref[1], place_ref[0], piece, sections, toks
            )
            ordered[pl.ds(pl.multiple_of(block * unit, unit), unit), :] = turned[
                piece * unit : (piece + 1) * unit
            ]
    grads_ref[...] = ordered[...].T
    div_ref[...] = jnp.sum(got_ref[:, feats : feats + 1, :], axis=0)


def shards(hidden, head_weight, teacher_logits, pairing):
    sections = lax.axis_size("sect")
    toks = lax.axis_size("tok")
    vocabs = lax.axis_size("vocab")
    planes = sections * toks
    width = head_weight.shape[1]
    rows, feats = hidden.shape
    own = rows // toks
    half = own // 2
    place = jnp.stack([lax.axis_index(name) for name in ("sect", "tok", "vocab")])

    picked = pl.pallas_call(
        functools.partial(pick_kernel, toks=toks),
        in_specs=[SMEM, VMEM],
        out_specs=VMEM,
        out_shape=jax.ShapeDtypeStruct((sections, feats, own), jnp.bfloat16),
        compiler_params=params(),
    )(place, hidden.T)
    spread = pl.pallas_call(
        arrange_kernel,
        in_specs=[VMEM],
        out_specs=VMEM,
        out_shape=jax.ShapeDtypeStruct((vocabs, feats, rows), jnp.bfloat16),
        compiler_params=params(),
        cost_estimate=cost(2 * feats * own * sections * rows, vocabs * feats * rows * 2),
    )(exchange(picked, "sect"))
    spread = exchange(spread, "vocab").reshape(vocabs * feats, rows)

    edge_down, edge_up = partial_logits(spread, head_weight, 0, [half, half])
    far_down = along_z(edge_down, -1, planes)
    far_up = along_z(edge_up, 1, planes)
    near_down, near_up, next_down, next_up, kept = partial_logits(
        spread, head_weight, own, [half, half, half, half, own]
    )
    down_b = along_z(near_down, -1, planes)
    up_a = along_z(near_up, 1, planes)
    next_down, next_up = pl.pallas_call(
        add_kernel,
        out_shape=[jax.ShapeDtypeStruct(next_down.shape, jnp.float32)] * 2,
        compiler_params=params(),
    )(next_down, far_down, next_up, far_up)
    down_a = along_z(next_down, -1, planes)
    up_b = along_z(next_up, 1, planes)

    ordered = pl.pallas_call(
        order_kernel,
        in_specs=[SMEM, SMEM, VMEM, pl.BlockSpec(memory_space=pl.ANY)],
        out_specs=VMEM,
        out_shape=jax.ShapeDtypeStruct((vocabs, sections, width), jnp.bfloat16),
        compiler_params=params(),
    )(place, pairing, teacher_logits, kept)
    teacher = exchange(ordered, "vocab").transpose(1, 0, 2).reshape(own, width)

    logits, stats = pl.pallas_call(
        stats_kernel,
        out_shape=[
            jax.ShapeDtypeStruct((own, width), jnp.float32),
            jax.ShapeDtypeStruct((vocabs, 8, own), jnp.float32),
        ],
        compiler_params=params(),
    )(kept, down_a, up_a, down_b, up_b, teacher)
    low, high, diverge = pl.pallas_call(
        grads_kernel,
        out_shape=[
            jax.ShapeDtypeStruct((half, width), jnp.bfloat16),
            jax.ShapeDtypeStruct((half, width), jnp.bfloat16),
            jax.ShapeDtypeStruct((1, own), jnp.float32),
        ],
        compiler_params=params(),
    )(logits, teacher, exchange(stats, "vocab"))

    below_low = along_z(low, 1, planes)
    above_high = along_z(high, -1, planes)
    below_high = along_z(high, 1, planes)
    above_low = along_z(low, -1, planes)
    far_below = along_z(below_low, 1, planes)
    far_above = along_z(above_high, -1, planes)
    keep, send = hidden_grads(
        place,
        head_weight,
        [far_below, far_above, below_high, above_low, below_low, above_high, low, high],
        vocabs // 2,
    )
    other = lax.ppermute(send, "vocab", [(i, i ^ 1) for i in range(vocabs)])
    groups = [list(range(core, vocabs, 2)) for core in range(2)]
    parts = exchange(keep + other, "vocab", axis_index_groups=groups)

    regrouped = pl.pallas_call(
        regroup_kernel,
        in_specs=[SMEM, VMEM, VMEM],
        out_specs=VMEM,
        out_shape=jax.ShapeDtypeStruct((sections, feats + 8, own), jnp.float32),
        compiler_params=params(),
    )(place, parts, diverge)
    grads, div = pl.pallas_call(
        functools.partial(return_kernel, toks=toks),
        in_specs=[SMEM, VMEM],
        out_specs=[VMEM, VMEM],
        out_shape=[
            jax.ShapeDtypeStruct((feats, rows), jnp.float32),
            jax.ShapeDtypeStruct((1, own), jnp.float32),
        ],
        scratch_shapes=[pltpu.VMEM((rows, feats), jnp.float32)],
        compiler_params=params(),
    )(place, exchange(regrouped, "sect"))
    return grads.T, div.reshape(own)


def solution(mesh):
    placed = (
        P("sect", ("tok", "vocab")),
        P("tok", "vocab"),
        P(("sect", "tok", "vocab"), None),
        P(),
    )
    return jax.shard_map(
        shards,
        mesh=mesh,
        in_specs=placed,
        out_specs=(P("sect", ("tok", "vocab")), P(("sect", "tok"))),
        check_vma=False,
    )
```

time: 206 us -> 189 us (0.917)
  the two profiles are of different devices: /device:TPU:64 before, /device:TPU:6 now
where the time goes in v3:
time: 189 us; the launch traced here: 187 us
  blocking collectives  116 us (61%)
  starting transfers between devices  40.7 us (22%)
  Pallas kernels  14.5 us (8%)
  waiting for transfers between devices  11.5 us (6%)
  local copies, waits for them, and re-layouts  3.26 us (2%)
    all_to_all x6, blocking collectives, exchange(): lax.all_to_all(value, axis, split_axis=0, concat_axis=0, tiled=True, **gr...  116 us
    ppermute x12, starting transfers between devices, along_z(): lax.ppermute(value, ('sect', 'tok'), [(i, (i + steps) % planes) for i in...  38.8 us
    ppermute x12, waiting for transfers between devices, along_z(): lax.ppermute(value, ('sect', 'tok'), [(i, (i + steps) % planes) for i in...  8.88 us
    pallas_call x2, Pallas kernels, partial_logits(): pl.pallas_call(functools.partial(logits_kernel, first), grid=(width // ti...  5.04 us
  transfers between devices with their start and end apart: 13, of which 5 were waited for; matrix products, arithmetic and copies ran while one was open for 0% of the time, Pallas kernels for 3%

profile of v3, /device:TPU:6, one launch (start us, length us, event | category | flops | bytes accessed | tf_op | source)
XLA Modules:
  0.0 187.0 jit_solution(3221822442971404545)
XLA Ops:
  0.6 0.1 pad_add_fusion.place_ref
  0.7 0.0 copy-start.3
  0.7 0.8 copy-done.3
  1.5 0.8 shard_map.59
  2.3 27.6 %all_to_all.30.got_ref = bf16[4,32,128]{2,1,0:T(8,128)(2,1)S(1)} all-to-all(bf16[4,32,128]{2,1,0:T(8,128)(2,1)S(1)} %shard_map.59), channel_id=1, replica_groups=mesh['sect'=4,'tok'=4,'vocab'=32] {'sect'}, dimensions={0} | all-to-all | bytes 65536 | tf_op jit(solution)/shard_map/all_to_all | solution.py:23
  29.9 0.3 shard_map.60
  30.2 22.0 %all_to_all.31 = bf16[32,32,512]{2,1,0:T(8,128)(2,1)S(1)} all-to-all(bf16[32,32,512]{2,1,0:T(8,128)(2,1)S(1)} %shard_map.60), channel_id=1, replica_groups=mesh['sect'=4,'tok'=4,'vocab'=32] {'vocab'}, dimensions={0} | all-to-all | bytes 2097152 | tf_op jit(solution)/shard_map/all_to_all | solution.py:23
  52.2 0.0 copy-start
  52.2 2.2 %copy-done = bf16[1024,2048]{1,0:T(8,128)(2,1)S(1)} copy-done((bf16[1024,2048]{1,0:T(8,128)(2,1)S(1)}, bf16[1024,2048]{1,0:T(8,128)(2,1)}, u32[]{:S(2)}) %copy-start) | copy-done | bytes 4194328
  54.4 1.9 %shard_map.62 = (f32[64,2048]{1,0:T(8,128)S(1)}, f32[64,2048]{1,0:T(8,128)S(1)}) custom-call(bf16[1024,512]{1,0:T(8,128)(2,1)S(1)} %bitcast.11, bf16[1024,2048]{1,0:T(8,128)(2,1)S(1)} %copy-done), custom_call_target="tpu_custom_call" | custom-call | flops 536870912 | bytes 5505024 | tf_op jit(solution)/shard_map/pallas_call | solution.py:115
  56.3 0.0 copy-start.2
  56.3 0.0 copy-start.4
  56.3 2.1 %collective-permute-start = (f32[64,2048]{1,0:T(8,128)S(1)}, f32[64,2048]{1,0:T(8,128)S(1)}, u32[]{:S(2)}, u32[]{:S(2)}) collective-permute-start(f32[64,2048]{1,0:T(8,128)S(1)} %get-tuple-element.22), channel_id=1, source_target_pairs={{0,480},{32,0},{64,32},{96,64},{128,96},{160,128},{192,160},{224,1... | collective-permute-start | bytes 1572872 | tf_op jit(solution)/shard_map/ppermute | solution.py:17
  58.4 3.9 %collective-permute-start.1 = (f32[64,2048]{1,0:T(8,128)S(1)}, f32[64,2048]{1,0:T(8,128)S(1)}, u32[]{:S(2)}, u32[]{:S(2)}) collective-permute-start(f32[64,2048]{1,0:T(8,128)S(1)} %get-tuple-element.24), channel_id=1, source_target_pairs={{0,32},{32,64},{64,96},{96,128},{128,160},{160,192},{192,224},{224... | collective-permute-start | bytes 1572872 | tf_op jit(solution)/shard_map/ppermute | solution.py:17
  62.3 3.1 %shard_map.61 = (f32[64,2048]{1,0:T(8,128)S(1)}, f32[64,2048]{1,0:T(8,128)S(1)}, f32[64,2048]{1,0:T(8,128)S(1)}, f32[64,2048]{1,0:T(8,128)S(1)}, f32[128,2048]{1,0:T(8,128)S(1)}) custom-call(bf16[1024,512]{1,0:T(8,128)(2,1)S(1)} %bitcast.12, bf16[1024,2048]{1,0:T(8,128)(2,1)S(1)} %copy-done), custom_call_target="tpu_custom_call" | custom-call | flops 1610612736 | bytes 8126464 | tf_op jit(solution)/shard_map/pallas_call | solution.py:115
  65.5 2.9 %collective-permute-start.3 = (f32[64,2048]{1,0:T(8,128)S(1)}, f32[64,2048]{1,0:T(8,128)S(1)}, u32[]{:S(2)}, u32[]{:S(2)}) collective-permute-start(f32[64,2048]{1,0:T(8,128)S(1)} %get-tuple-element.26), channel_id=1, source_target_pairs={{0,32},{32,64},{64,96},{96,128},{128,160},{160,192},{192,224},{224... | collective-permute-start | bytes 1572872 | tf_op jit(solution)/shard_map/ppermute | solution.py:17
  68.4 4.1 %collective-permute-start.4 = (f32[64,2048]{1,0:T(8,128)S(1)}, f32[64,2048]{1,0:T(8,128)S(1)}, u32[]{:S(2)}, u32[]{:S(2)}) collective-permute-start(f32[64,2048]{1,0:T(8,128)S(1)} %get-tuple-element.27), channel_id=1, source_target_pairs={{0,480},{32,0},{64,32},{96,64},{128,96},{160,128},{192,160},{224,1... | collective-permute-start | bytes 1572872 | tf_op jit(solution)/shard_map/ppermute | solution.py:17
  72.5 0.3 collective-permute-done.far_down_ref
  72.8 3.1 %collective-permute-done.1.far_up_ref = f32[64,2048]{1,0:T(8,128)S(1)} collective-permute-done((f32[64,2048]{1,0:T(8,128)S(1)}, f32[64,2048]{1,0:T(8,128)S(1)}, u32[]{:S(2)}, u32[]{:S(2)}) %collective-permute-start.1) | collective-permute-done | bytes 524320 | tf_op jit(solution)/shard_map/ppermute | solution.py:17
  75.9 0.1 shard_map.63
  76.1 1.9 %collective-permute-start.2 = (f32[64,2048]{1,0:T(8,128)S(1)}, f32[64,2048]{1,0:T(8,128)S(1)}, u32[]{:S(2)}, u32[]{:S(2)}) collective-permute-start(f32[64,2048]{1,0:T(8,128)S(1)} %get-tuple-element.25), channel_id=1, source_target_pairs={{0,480},{32,0},{64,32},{96,64},{128,96},{160,128},{192,160},{224,1... | collective-permute-start | bytes 1572872 | tf_op jit(solution)/shard_map/ppermute | solution.py:17
  78.0 3.9 %collective-permute-start.5 = (f32[64,2048]{1,0:T(8,128)S(1)}, f32[64,2048]{1,0:T(8,128)S(1)}, u32[]{:S(2)}, u32[]{:S(2)}) collective-permute-start(f32[64,2048]{1,0:T(8,128)S(1)} %get-tuple-element.28), channel_id=1, source_target_pairs={{0,32},{32,64},{64,96},{96,128},{128,160},{160,192},{192,224},{224... | collective-permute-start | bytes 1572872 | tf_op jit(solution)/shard_map/ppermute | solution.py:17
  81.9 0.0 copy-done.2
  81.9 0.0 copy-done.4
  81.9 1.5 shard_map.64
  83.5 0.0 copy-start.1
  83.5 15.7 %all_to_all.32 = bf16[32,4,2048]{2,1,0:T(4,128)(2,1)S(1)} all-to-all(bf16[32,4,2048]{2,1,0:T(4,128)(2,1)S(1)} %shard_map.64), channel_id=1, replica_groups=mesh['sect'=4,'tok'=4,'vocab'=32] {'vocab'}, dimensions={0} | all-to-all | bytes 1048576 | tf_op jit(solution)/shard_map/all_to_all | solution.py:23
  99.2 0.3 copy.6
  99.5 0.0 collective-permute-done.3.lo_b
  99.5 0.0 collective-permute-done.4.hi_a
  99.5 0.0 collective-permute-done.2.lo_a
  99.5 0.0 collective-permute-done.5.hi_b
  99.5 0.7 shard_map.65
  100.3 11.9 %all_to_all.33.stats_ref = f32[32,8,128]{2,1,0:T(8,128)S(1)} all-to-all(f32[32,8,128]{2,1,0:T(8,128)S(1)} %get-tuple-element.30), channel_id=1, replica_groups=mesh['sect'=4,'tok'=4,'vocab'=32] {'vocab'}, dimensions={0} | all-to-all | bytes 262144 | tf_op jit(solution)/shard_map/all_to_all | solution.py:23
  112.2 0.6 shard_map.66
  112.8 2.7 %collective-permute-start.6 = (bf16[64,2048]{1,0:T(8,128)(2,1)S(1)}, bf16[64,2048]{1,0:T(8,128)(2,1)S(1)}, u32[]{:S(2)}, u32[]{:S(2)}) collective-permute-start(bf16[64,2048]{1,0:T(8,128)(2,1)S(1)} %get-tuple-element.31.refs_6_), channel_id=1, source_target_pairs={{0,32},{32,64},{64,96},{96,128},{128,160},{160,192},{192,224},{224... | collective-permute-start | bytes 786440 | tf_op jit(solution)/shard_map/ppermute | solution.py:17
  115.6 4.3 %collective-permute-start.8 = (bf16[64,2048]{1,0:T(8,128)(2,1)S(1)}, bf16[64,2048]{1,0:T(8,128)(2,1)S(1)}, u32[]{:S(2)}, u32[]{:S(2)}) collective-permute-start(bf16[64,2048]{1,0:T(8,128)(2,1)S(1)} %get-tuple-element.32.refs_7_), channel_id=1, source_target_pairs={{0,480},{32,0},{64,32},{96,64},{128,96},{160,128},{192,160},{224,1... | collective-permute-start | bytes 786440 | tf_op jit(solution)/shard_map/ppermute | solution.py:17
  119.9 1.9 %collective-permute-start.11 = (bf16[64,2048]{1,0:T(8,128)(2,1)S(1)}, bf16[64,2048]{1,0:T(8,128)(2,1)S(1)}, u32[]{:S(2)}, u32[]{:S(2)}) collective-permute-start(bf16[64,2048]{1,0:T(8,128)(2,1)S(1)} %get-tuple-element.31.refs_6_), channel_id=1, source_target_pairs={{0,480},{32,0},{64,32},{96,64},{128,96},{160,128},{192,160},{224,1... | collective-permute-start | bytes 786440 | tf_op jit(solution)/shard_map/ppermute | solution.py:17
  121.8 3.9 %collective-permute-start.10 = (bf16[64,2048]{1,0:T(8,128)(2,1)S(1)}, bf16[64,2048]{1,0:T(8,128)(2,1)S(1)}, u32[]{:S(2)}, u32[]{:S(2)}) collective-permute-start(bf16[64,2048]{1,0:T(8,128)(2,1)S(1)} %get-tuple-element.32.refs_7_), channel_id=1, source_target_pairs={{0,32},{32,64},{64,96},{96,128},{128,160},{160,192},{192,224},{224... | collective-permute-start | bytes 786440 | tf_op jit(solution)/shard_map/ppermute | solution.py:17
  125.7 0.0 collective-permute-done.6.refs_4_
  125.7 1.9 %collective-permute-start.7 = (bf16[64,2048]{1,0:T(8,128)(2,1)S(1)}, bf16[64,2048]{1,0:T(8,128)(2,1)S(1)}, u32[]{:S(2)}, u32[]{:S(2)}) collective-permute-start(bf16[64,2048]{1,0:T(8,128)(2,1)S(1)} %collective-permute-done.6.refs_4_), channel_id=1, source_target_pairs={{0,32},{32,64},{64,96},{96,128},{128,160},{160,192},{192,224},{224... | collective-permute-start | bytes 786440 | tf_op jit(solution)/shard_map/ppermute | solution.py:17
  127.7 0.0 collective-permute-done.8.refs_5_
  127.7 5.1 %collective-permute-start.9 = (bf16[64,2048]{1,0:T(8,128)(2,1)S(1)}, bf16[64,2048]{1,0:T(8,128)(2,1)S(1)}, u32[]{:S(2)}, u32[]{:S(2)}) collective-permute-start(bf16[64,2048]{1,0:T(8,128)(2,1)S(1)} %collective-permute-done.8.refs_5_), channel_id=1, source_target_pairs={{0,480},{32,0},{64,32},{96,64},{128,96},{160,128},{192,160},{224,1... | collective-permute-start | bytes 786440 | tf_op jit(solution)/shard_map/ppermute | solution.py:17
  132.8 0.0 collective-permute-done.11.refs_3_
  132.8 1.3 collective-permute-done.10.refs_2_
  134.1 4.1 %collective-permute-done.7.refs_0_ = bf16[64,2048]{1,0:T(8,128)(2,1)S(1)} collective-permute-done((bf16[64,2048]{1,0:T(8,128)(2,1)S(1)}, bf16[64,2048]{1,0:T(8,128)(2,1)S(1)}, u32[]{:S(2)}, u32[]{:S(2)}) %collective-permute-start.7) | collective-permute-done | bytes 262176 | tf_op jit(solution)/shard_map/ppermute | solution.py:17
  138.3 0.0 collective-permute-done.9.refs_1_
  138.3 0.0 copy-done.1
  138.3 3.4 %shard_map.67 = (f32[16,32,512]{2,1,0:T(8,128)S(1)}, f32[16,32,512]{2,1,0:T(8,128)S(1)}) custom-call(s32[3]{0:T(128)S(1)} %pad_add_fusion.place_ref, bf16[1024,2048]{1,0:T(8,128)(2,1)S(1)} %copy-done.1, bf16[64,2048]{1,0:T(8,128)(2,1)S(1)} %collective-permute-done.7.refs_0_, bf16[64,2048]{1,0:T(8,128)(2,1)S(1)} %collective-permute-done.9.refs_1_, ...), custom_call_target="tpu_custom_call" | custom-call | flops 2147483648 | bytes 8388608 | tf_op jit(solution)/shard_map/pallas_call | solution.py:229
  141.7 1.9 %collective-permute-start.12 = (f32[16,32,512]{2,1,0:T(8,128)S(1)}, f32[16,32,512]{2,1,0:T(8,128)S(1)}, u32[]{:S(2)}, u32[]{:S(2)}) collective-permute-start(f32[16,32,512]{2,1,0:T(8,128)S(1)} %get-tuple-element.34), channel_id=1, source_target_pairs={{0,1},{1,0},{2,3},{3,2},{4,5},{5,4},{6,7},{7,6},{8,9},{9,8},{10,11... | collective-permute-start | bytes 3145736 | tf_op jit(solution)/shard_map/ppermute | solution.py:373
  143.6 2.6 %collective-permute-done.12 = f32[16,32,512]{2,1,0:T(8,128)S(1)} collective-permute-done((f32[16,32,512]{2,1,0:T(8,128)S(1)}, f32[16,32,512]{2,1,0:T(8,128)S(1)}, u32[]{:S(2)}, u32[]{:S(2)}) %collective-permute-start.12) | collective-permute-done | bytes 1048608 | tf_op jit(solution)/shard_map/ppermute | solution.py:373
  146.2 0.2 add.3
  146.5 19.8 %all_to_all.34.parts_ref = f32[16,32,512]{2,1,0:T(8,128)S(1)} all-to-all(f32[16,32,512]{2,1,0:T(8,128)S(1)} %add.3), channel_id=1, replica_groups={{0,2,4,6,8,10,12,14,16,18,20,22,24,26,28,30},{1,3,5,7,9,11,13,15,17,19,..., dimensions={0} | all-to-all | bytes 2097152 | tf_op jit(solution)/shard_map/all_to_all | solution.py:23
  166.2 0.7 shard_map.68
  166.9 18.6 %all_to_all.35.got_ref = f32[4,40,128]{2,1,0:T(8,128)S(1)} all-to-all(f32[4,40,128]{2,1,0:T(8,128)S(1)} %shard_map.68), channel_id=1, replica_groups=mesh['sect'=4,'tok'=4,'vocab'=32] {'sect'}, dimensions={0} | all-to-all | bytes 163840 | tf_op jit(solution)/shard_map/all_to_all | solution.py:23
  185.5 1.4 shard_map.69
Async XLA Ops:
  0.7 0.8 copy-start.3
  52.2 2.2 %copy-start = (bf16[1024,2048]{1,0:T(8,128)(2,1)S(1)}, bf16[1024,2048]{1,0:T(8,128)(2,1)}, u32[]{:S(2)}) copy-start(bf16[1024,2048]{1,0:T(8,128)(2,1)} %w_ref.5) | copy-start | bytes 12582916
  56.3 25.6 %copy-start.2 = (bf16[4,65536]{1,0:T(4,128)(2,1)S(1)}, bf16[4,65536]{1,0:T(4,128)(2,1)}, u32[]{:S(2)}) copy-start(bf16[4,65536]{1,0:T(4,128)(2,1)} %teacher_ref.1) | copy-start | bytes 1572868
  56.3 25.6 %copy-start.4 = (s32[4,4]{1,0:T(4,128)S(1)}, s32[4,4]{1,0:T(4,128)}, u32[]{:S(2)}) copy-start(s32[4,4]{1,0:T(4,128)} %pairing_ref.1) | copy-start | bytes 196
  56.3 16.5 %collective-permute-start = (f32[64,2048]{1,0:T(8,128)S(1)}, f32[64,2048]{1,0:T(8,128)S(1)}, u32[]{:S(2)}, u32[]{:S(2)}) collective-permute-start(f32[64,2048]{1,0:T(8,128)S(1)} %get-tuple-element.22), channel_id=1, source_target_pairs={{0,480},{32,0},{64,32},{96,64},{128,96},{160,128},{192,160},{224,1... | collective-permute-start | bytes 1572872 | tf_op jit(solution)/shard_map/ppermute | solution.py:17
  58.4 17.6 %collective-permute-start.1 = (f32[64,2048]{1,0:T(8,128)S(1)}, f32[64,2048]{1,0:T(8,128)S(1)}, u32[]{:S(2)}, u32[]{:S(2)}) collective-permute-start(f32[64,2048]{1,0:T(8,128)S(1)} %get-tuple-element.24), channel_id=1, source_target_pairs={{0,32},{32,64},{64,96},{96,128},{128,160},{160,192},{192,224},{224... | collective-permute-start | bytes 1572872 | tf_op jit(solution)/shard_map/ppermute | solution.py:17
  65.5 34.0 %collective-permute-start.3 = (f32[64,2048]{1,0:T(8,128)S(1)}, f32[64,2048]{1,0:T(8,128)S(1)}, u32[]{:S(2)}, u32[]{:S(2)}) collective-permute-start(f32[64,2048]{1,0:T(8,128)S(1)} %get-tuple-element.26), channel_id=1, source_target_pairs={{0,32},{32,64},{64,96},{96,128},{128,160},{160,192},{192,224},{224... | collective-permute-start | bytes 1572872 | tf_op jit(solution)/shard_map/ppermute | solution.py:17
  68.4 31.1 %collective-permute-start.4 = (f32[64,2048]{1,0:T(8,128)S(1)}, f32[64,2048]{1,0:T(8,128)S(1)}, u32[]{:S(2)}, u32[]{:S(2)}) collective-permute-start(f32[64,2048]{1,0:T(8,128)S(1)} %get-tuple-element.27), channel_id=1, source_target_pairs={{0,480},{32,0},{64,32},{96,64},{128,96},{160,128},{192,160},{224,1... | collective-permute-start | bytes 1572872 | tf_op jit(solution)/shard_map/ppermute | solution.py:17
  76.1 23.5 %collective-permute-start.2 = (f32[64,2048]{1,0:T(8,128)S(1)}, f32[64,2048]{1,0:T(8,128)S(1)}, u32[]{:S(2)}, u32[]{:S(2)}) collective-permute-start(f32[64,2048]{1,0:T(8,128)S(1)} %get-tuple-element.25), channel_id=1, source_target_pairs={{0,480},{32,0},{64,32},{96,64},{128,96},{160,128},{192,160},{224,1... | collective-permute-start | bytes 1572872 | tf_op jit(solution)/shard_map/ppermute | solution.py:17
  78.0 21.6 %collective-permute-start.5 = (f32[64,2048]{1,0:T(8,128)S(1)}, f32[64,2048]{1,0:T(8,128)S(1)}, u32[]{:S(2)}, u32[]{:S(2)}) collective-permute-start(f32[64,2048]{1,0:T(8,128)S(1)} %get-tuple-element.28), channel_id=1, source_target_pairs={{0,32},{32,64},{64,96},{96,128},{128,160},{160,192},{192,224},{224... | collective-permute-start | bytes 1572872 | tf_op jit(solution)/shard_map/ppermute | solution.py:17
  83.5 54.8 %copy-start.1 = (bf16[1024,2048]{1,0:T(8,128)(2,1)S(1)}, bf16[1024,2048]{1,0:T(8,128)(2,1)}, u32[]{:S(2)}) copy-start(bf16[1024,2048]{1,0:T(8,128)(2,1)} %w_ref.5) | copy-start | bytes 12582916
  112.8 12.9 %collective-permute-start.6 = (bf16[64,2048]{1,0:T(8,128)(2,1)S(1)}, bf16[64,2048]{1,0:T(8,128)(2,1)S(1)}, u32[]{:S(2)}, u32[]{:S(2)}) collective-permute-start(bf16[64,2048]{1,0:T(8,128)(2,1)S(1)} %get-tuple-element.31.refs_6_), channel_id=1, source_target_pairs={{0,32},{32,64},{64,96},{96,128},{128,160},{160,192},{192,224},{224... | collective-permute-start | bytes 786440 | tf_op jit(solution)/shard_map/ppermute | solution.py:17
  115.6 12.1 %collective-permute-start.8 = (bf16[64,2048]{1,0:T(8,128)(2,1)S(1)}, bf16[64,2048]{1,0:T(8,128)(2,1)S(1)}, u32[]{:S(2)}, u32[]{:S(2)}) collective-permute-start(bf16[64,2048]{1,0:T(8,128)(2,1)S(1)} %get-tuple-element.32.refs_7_), channel_id=1, source_target_pairs={{0,480},{32,0},{64,32},{96,64},{128,96},{160,128},{192,160},{224,1... | collective-permute-start | bytes 786440 | tf_op jit(solution)/shard_map/ppermute | solution.py:17
  119.9 13.0 %collective-permute-start.11 = (bf16[64,2048]{1,0:T(8,128)(2,1)S(1)}, bf16[64,2048]{1,0:T(8,128)(2,1)S(1)}, u32[]{:S(2)}, u32[]{:S(2)}) collective-permute-start(bf16[64,2048]{1,0:T(8,128)(2,1)S(1)} %get-tuple-element.31.refs_6_), channel_id=1, source_target_pairs={{0,480},{32,0},{64,32},{96,64},{128,96},{160,128},{192,160},{224,1... | collective-permute-start | bytes 786440 | tf_op jit(solution)/shard_map/ppermute | solution.py:17
  121.8 12.3 %collective-permute-start.10 = (bf16[64,2048]{1,0:T(8,128)(2,1)S(1)}, bf16[64,2048]{1,0:T(8,128)(2,1)S(1)}, u32[]{:S(2)}, u32[]{:S(2)}) collective-permute-start(bf16[64,2048]{1,0:T(8,128)(2,1)S(1)} %get-tuple-element.32.refs_7_), channel_id=1, source_target_pairs={{0,32},{32,64},{64,96},{96,128},{128,160},{160,192},{192,224},{224... | collective-permute-start | bytes 786440 | tf_op jit(solution)/shard_map/ppermute | solution.py:17
  125.7 12.5 %collective-permute-start.7 = (bf16[64,2048]{1,0:T(8,128)(2,1)S(1)}, bf16[64,2048]{1,0:T(8,128)(2,1)S(1)}, u32[]{:S(2)}, u32[]{:S(2)}) collective-permute-start(bf16[64,2048]{1,0:T(8,128)(2,1)S(1)} %collective-permute-done.6.refs_4_), channel_id=1, source_target_pairs={{0,32},{32,64},{64,96},{96,128},{128,160},{160,192},{192,224},{224... | collective-permute-start | bytes 786440 | tf_op jit(solution)/shard_map/ppermute | solution.py:17
  127.7 10.6 %collective-permute-start.9 = (bf16[64,2048]{1,0:T(8,128)(2,1)S(1)}, bf16[64,2048]{1,0:T(8,128)(2,1)S(1)}, u32[]{:S(2)}, u32[]{:S(2)}) collective-permute-start(bf16[64,2048]{1,0:T(8,128)(2,1)S(1)} %collective-permute-done.8.refs_5_), channel_id=1, source_target_pairs={{0,480},{32,0},{64,32},{96,64},{128,96},{160,128},{192,160},{224,1... | collective-permute-start | bytes 786440 | tf_op jit(solution)/shard_map/ppermute | solution.py:17
  141.7 4.6 %collective-permute-start.12 = (f32[16,32,512]{2,1,0:T(8,128)S(1)}, f32[16,32,512]{2,1,0:T(8,128)S(1)}, u32[]{:S(2)}, u32[]{:S(2)}) collective-permute-start(f32[16,32,512]{2,1,0:T(8,128)S(1)} %get-tuple-element.34), channel_id=1, source_target_pairs={{0,1},{1,0},{2,3},{3,2},{4,5},{5,4},{6,7},{7,6},{8,9},{9,8},{10,11... | collective-permute-start | bytes 3145736 | tf_op jit(solution)/shard_map/ppermute | solution.py:373

commit v4 on v3

--- a/solution.py
+++ b/solution.py
@@ -11,6 +11,7 @@
 VMEM_BYTES = 24 * 1024 * 1024
 SMEM = pl.BlockSpec(memory_space=pltpu.SMEM)
 VMEM = pl.BlockSpec(memory_space=pltpu.VMEM)
+ANYWHERE = pl.BlockSpec(memory_space=pl.ANY)
 
 
 def along_z(value, steps, planes):
@@ -29,14 +30,24 @@
 
 def cost(flops, bytes_accessed):
     return pl.CostEstimate(flops=flops, bytes_accessed=bytes_accessed, transcendentals=0)
+
+
+def remainder(value, count):
+    return value & (count - 1) if count & (count - 1) == 0 else lax.rem(value, count)
+
+
+def quotient(value, count):
+    if count & (count - 1) == 0:
+        return lax.shift_right_logical(value, jnp.int32(count.bit_length() - 1))
+    return lax.div(value, count)
 
 
 def window_block(section, tok, token_section, piece, sections, toks):
     planes = sections * toks
     near = jnp.int32(piece - 2)
     far = jnp.where(token_section < sections // 2, -2, 2)
-    plane = lax.rem(section * toks + tok + (far if piece == 0 else near) + planes, planes)
-    return lax.rem(plane, toks) * sections + lax.div(plane, toks)
+    plane = remainder(section * toks + tok + (far if piece == 0 else near) + planes, planes)
+    return remainder(plane, toks) * sections + quotient(plane, toks)
 
 
 def window_order(sections):
@@ -94,12 +105,24 @@
         spread_ref[k] = window
 
 
-def logits_kernel(first, x_ref, w_ref, *refs):
-    *outs, flipped = refs
+def logits_kernel(first, place_ref, mine_ref, other_ref, w_ref, *refs):
+    *outs, both, flipped = refs
 
     @pl.when(pl.program_id(0) == 0)
     def _():
-        flipped[...] = x_ref[:, first:].T
+        core = remainder(place_ref[2], 2)
+
+        @pl.when(core == 0)
+        def _():
+            both[:, 0] = mine_ref[:, :, first:]
+            both[:, 1] = other_ref[:, :, first:]
+
+        @pl.when(core != 0)
+        def _():
+            both[:, 0] = other_ref[:, :, first:]
+            both[:, 1] = mine_ref[:, :, first:]
+
+        flipped[...] = both[...].reshape(w_ref.shape[0], flipped.shape[0]).T
 
     result = jnp.dot(flipped[...], w_ref[...], preferred_element_type=jnp.float32)
     start = 0
@@ -108,25 +131,27 @@
         start += out.shape[0]
 
 
-def partial_logits(spread, head_weight, first, sizes):
+def partial_logits(place, mine, other, head_weight, first, sizes):
     feats, width = head_weight.shape
     tile = 512
     count = sum(sizes)
+    pairs, unit, _ = mine.shape
+    half = pl.BlockSpec((pairs, unit, first + count), lambda i: (0, 0, 0))
     return pl.pallas_call(
         functools.partial(logits_kernel, first),
         grid=(width // tile,),
-        in_specs=[
-            pl.BlockSpec((feats, first + count), lambda i: (0, 0)),
-            pl.BlockSpec((feats, tile), lambda i: (0, i)),
-        ],
+        in_specs=[SMEM, half, half, pl.BlockSpec((feats, tile), lambda i: (0, i))],
         out_specs=[pl.BlockSpec((size, tile), lambda i: (0, i)) for size in sizes],
         out_shape=[jax.ShapeDtypeStruct((size, width), jnp.float32) for size in sizes],
-        scratch_shapes=[pltpu.VMEM((count, feats), jnp.bfloat16)],
+        scratch_shapes=[
+            pltpu.VMEM((pairs, 2, unit, count), jnp.bfloat16),
+            pltpu.VMEM((count, feats), jnp.bfloat16),
+        ],
         compiler_params=params(),
         cost_estimate=cost(
             2 * count * feats * width, feats * width * 2 + count * (feats * 2 + width * 4)
         ),
-    )(spread, head_weight)
+    )(place, mine, other, head_weight)
 
 
 def order_kernel(place_ref, pairing_ref, teacher_ref, after_ref, ordered_ref):
@@ -142,9 +167,8 @@
         ordered_ref[v] = out.astype(jnp.bfloat16)
 
 
-def add_kernel(down_ref, far_down_ref, up_ref, far_up_ref, down_out, up_out):
-    down_out[...] = down_ref[...] + far_down_ref[...]
-    up_out[...] = up_ref[...] + far_up_ref[...]
+def add_kernel(mine_ref, far_ref, after_ref, out_ref):
+    out_ref[...] = mine_ref[...] + far_ref[...]
 
 
 def stats_kernel(own_ref, lo_a, lo_b, hi_a, hi_b, teacher_ref, logits_ref, stats_ref):
@@ -207,7 +231,7 @@
     result = lax.dot_general(
         w_ref[...], window[...], (((1,), (1,)), ((), ())), preferred_element_type=jnp.float32
     ).reshape(pairs, 2, feats, rows)
-    core = lax.rem(place_ref[2], 2)
+    core = remainder(place_ref[2], 2)
 
     @pl.when(core == 0)
     def _():
@@ -270,20 +294,26 @@
         out_ref[s, feats:] = out
 
 
-def return_kernel(place_ref, got_ref, grads_ref, div_ref, ordered, *, toks):
+def return_kernel(place_ref, got_ref, grads_ref, div_ref, *, toks):
     sections, _, own = got_ref.shape
     unit = own // 4
-    feats = grads_ref.shape[0]
+    feats, rows = grads_ref.shape
+    lane = lax.broadcasted_iota(jnp.int32, (feats, own), 1)
+    outs = [jnp.zeros((feats, own), jnp.float32) for _ in range(rows // own)]
     for sender in range(sections):
-        turned = got_ref[sender, :feats, :].T
+        values = got_ref[sender, :feats]
         for piece in range(4):
             block = window_block(
                 jnp.int32(sender), place_ref[1], place_ref[0], piece, sections, toks
             )
-            ordered[pl.ds(pl.multiple_of(block * unit, unit), unit), :] = turned[
-                piece * unit : (piece + 1) * unit
-            ]
-    grads_ref[...] = ordered[...].T
+            begin = remainder(block, 4) * unit
+            turned = pltpu.roll(values, remainder(begin - piece * unit + own, own), 1)
+            first = lane - quotient(block, 4) * own - begin
+            for index in range(len(outs)):
+                inside = (first >= -index * own) & (first < unit - index * own)
+                outs[index] = jnp.where(inside, turned, outs[index])
+    for index, out in enumerate(outs):
+        grads_ref[:, index * own : (index + 1) * own] = out
     div_ref[...] = jnp.sum(got_ref[:, feats : feats + 1, :], axis=0)
 
 
@@ -309,35 +339,43 @@
         arrange_kernel,
         in_specs=[VMEM],
         out_specs=VMEM,
-        out_shape=jax.ShapeDtypeStruct((vocabs, feats, rows), jnp.bfloat16),
-        compiler_params=params(),
-        cost_estimate=cost(2 * feats * own * sections * rows, vocabs * feats * rows * 2),
+        out_shape=jax.ShapeDtypeStruct((vocabs // 2, feats, rows), jnp.bfloat16),
+        compiler_params=params(),
+        cost_estimate=cost(20 * 10**9, 64 * 10**6),
     )(exchange(picked, "sect"))
-    spread = exchange(spread, "vocab").reshape(vocabs * feats, rows)
-
-    edge_down, edge_up = partial_logits(spread, head_weight, 0, [half, half])
+    groups = [list(range(core, vocabs, 2)) for core in range(2)]
+    other_core = [(i, i ^ 1) for i in range(vocabs)]
+    mine = exchange(spread, "vocab", axis_index_groups=groups)
+    other = lax.ppermute(mine, "vocab", other_core)
+
+    edge_down, edge_up = partial_logits(
+        place, mine, other, head_weight, 0, [half, half]
+    )
     far_down = along_z(edge_down, -1, planes)
     far_up = along_z(edge_up, 1, planes)
     near_down, near_up, next_down, next_up, kept = partial_logits(
-        spread, head_weight, own, [half, half, half, half, own]
+        place, mine, other, head_weight, own, [half, half, half, half, own]
     )
     down_b = along_z(near_down, -1, planes)
     up_a = along_z(near_up, 1, planes)
-    next_down, next_up = pl.pallas_call(
-        add_kernel,
-        out_shape=[jax.ShapeDtypeStruct(next_down.shape, jnp.float32)] * 2,
-        compiler_params=params(),
-    )(next_down, far_down, next_up, far_up)
-    down_a = along_z(next_down, -1, planes)
-    up_b = along_z(next_up, 1, planes)
 
     ordered = pl.pallas_call(
         order_kernel,
-        in_specs=[SMEM, SMEM, VMEM, pl.BlockSpec(memory_space=pl.ANY)],
+        in_specs=[SMEM, SMEM, VMEM, ANYWHERE],
         out_specs=VMEM,
         out_shape=jax.ShapeDtypeStruct((vocabs, sections, width), jnp.bfloat16),
         compiler_params=params(),
     )(place, pairing, teacher_logits, kept)
+
+    add = pl.pallas_call(
+        add_kernel,
+        in_specs=[VMEM, VMEM, ANYWHERE],
+        out_specs=VMEM,
+        out_shape=jax.ShapeDtypeStruct(next_down.shape, jnp.float32),
+        compiler_params=params(),
+    )
+    down_a = along_z(add(next_down, far_down, ordered), -1, planes)
+    up_b = along_z(add(next_up, far_up, ordered), 1, planes)
     teacher = exchange(ordered, "vocab").transpose(1, 0, 2).reshape(own, width)
 
     logits, stats = pl.pallas_call(
@@ -370,8 +408,7 @@
         [far_below, far_above, below_high, above_low, below_low, above_high, low, high],
         vocabs // 2,
     )
-    other = lax.ppermute(send, "vocab", [(i, i ^ 1) for i in range(vocabs)])
-    groups = [list(range(core, vocabs, 2)) for core in range(2)]
+    other = lax.ppermute(send, "vocab", other_core)
     parts = exchange(keep + other, "vocab", axis_index_groups=groups)
 
     regrouped = pl.pallas_call(
@@ -389,7 +426,6 @@
             jax.ShapeDtypeStruct((feats, rows), jnp.float32),
             jax.ShapeDtypeStruct((1, own), jnp.float32),
         ],
-        scratch_shapes=[pltpu.VMEM((rows, feats), jnp.float32)],
         compiler_params=params(),
     )(place, exchange(regrouped, "sect"))
     return grads.T, div.reshape(own)

time: 189 us -> 182 us (0.963)
  blocking collectives: 116 us -> 108 us
  local copies, waits for them, and re-layouts: 3.26 us -> 1.07 us
  starting transfers between devices: 40.7 us -> 42.6 us
    all_to_all x6, blocking collectives: 116 us -> 108 us  [exchange(): lax.all_to_all(value, axis, split_axis=0, concat_axis=0, tiled=True, **gr...]
    unnamed x10 -> x8, local copies, waits for them, and re-layouts: 2.97 us -> 0.78 us
    ppermute x1 -> x2, starting transfers between devices: 1.92 us -> 3.83 us  [the longest x1 1.92 us: shards(): other = lax.ppermute(send, 'vocab', other_core)]
    ppermute x1 -> x2, waiting for transfers between devices: 2.63 us -> 4.5 us  [the longest x1 2.63 us: shards(): other = lax.ppermute(send, 'vocab', other_core)]
  transfers between devices with their start and end apart: 13 -> 14, of which waited for: 5 -> 5; matrix products, arithmetic and copies ran while one was open for 0% -> 0% of each run, Pallas kernels for 3% -> 3%
where the time goes in v4:
time: 182 us; the launch traced here: 180 us
  blocking collectives  108 us (59%)
  starting transfers between devices  42.6 us (23%)
  Pallas kernels  15.4 us (8%)
  waiting for transfers between devices  11.8 us (6%)
    all_to_all x6, blocking collectives, exchange(): lax.all_to_all(value, axis, split_axis=0, concat_axis=0, tiled=True, **gr...  108 us
    ppermute x12, starting transfers between devices, along_z(): lax.ppermute(value, ('sect', 'tok'), [(i, (i + steps) % planes) for i in...  38.8 us
    ppermute x12, waiting for transfers between devices, along_z(): lax.ppermute(value, ('sect', 'tok'), [(i, (i + steps) % planes) for i in...  7.33 us
    pallas_call x2, Pallas kernels, partial_logits(): pl.pallas_call(functools.partial(logits_kernel, first), grid=(width // ti...  6.08 us
  transfers between devices with their start and end apart: 14, of which 5 were waited for; matrix products, arithmetic and copies ran while one was open for 0% of the time, Pallas kernels for 3%

profile of v4, /device:TPU:6, one launch (start us, length us, event | category | flops | bytes accessed | tf_op | source)
XLA Modules:
  0.0 179.9 jit_solution(8807645644953075308)
XLA Ops:
  0.6 0.1 pad_add_fusion.place_ref
  0.7 0.0 copy-start.2
  0.7 0.8 copy-done.2
  1.5 0.8 shard_map.59
  2.2 27.6 %all_to_all.30.got_ref = bf16[4,32,128]{2,1,0:T(8,128)(2,1)S(1)} all-to-all(bf16[4,32,128]{2,1,0:T(8,128)(2,1)S(1)} %shard_map.59), channel_id=1, replica_groups=mesh['sect'=4,'tok'=4,'vocab'=32] {'sect'}, dimensions={0} | all-to-all | bytes 65536 | tf_op jit(solution)/shard_map/all_to_all | solution.py:24
  29.9 0.0 copy-start
  29.9 0.2 shard_map.60
  30.1 15.1 %all_to_all.31.mine_ref = bf16[16,32,512]{2,1,0:T(8,128)(2,1)S(1)} all-to-all(bf16[16,32,512]{2,1,0:T(8,128)(2,1)S(1)} %shard_map.60), channel_id=1, replica_groups={{0,2,4,6,8,10,12,14,16,18,20,22,24,26,28,30},{1,3,5,7,9,11,13,15,17,19,..., dimensions={0} | all-to-all | bytes 1048576 | tf_op jit(solution)/shard_map/all_to_all | solution.py:24
  45.3 1.9 %collective-permute-start = (bf16[16,32,512]{2,1,0:T(8,128)(2,1)S(1)}, bf16[16,32,512]{2,1,0:T(8,128)(2,1)S(1)}, u32[]{:S(2)}, u32[]{:S(2)}) collective-permute-start(bf16[16,32,512]{2,1,0:T(8,128)(2,1)S(1)} %all_to_all.31.mine_ref), channel_id=1, source_target_pairs={{0,1},{1,0},{2,3},{3,2},{4,5},{5,4},{6,7},{7,6},{8,9},{9,8},{10,11... | collective-permute-start | bytes 1572872 | tf_op jit(solution)/shard_map/ppermute | solution.py:349
  47.2 1.9 %collective-permute-done.other_ref = bf16[16,32,512]{2,1,0:T(8,128)(2,1)S(1)} collective-permute-done((bf16[16,32,512]{2,1,0:T(8,128)(2,1)S(1)}, bf16[16,32,512]{2,1,0:T(8,128)(2,1)S(1)}, u32[]{:S(2)}, u32[]{:S(2)}) %collective-permute-start) | collective-permute-done | bytes 524320 | tf_op jit(solution)/shard_map/ppermute | solution.py:349
  49.1 0.0 copy-done
  49.1 2.4 %shard_map.62 = (f32[64,2048]{1,0:T(8,128)S(1)}, f32[64,2048]{1,0:T(8,128)S(1)}) custom-call(s32[3]{0:T(128)S(1)} %pad_add_fusion.place_ref, bf16[16,32,512]{2,1,0:T(8,128)(2,1)S(1)} %all_to_all.31.mine_ref, bf16[16,32,512]{2,1,0:T(8,128)(2,1)S(1)} %collective-permute-done.other_ref, bf16[1024,2048]{1,0:T(8,128)(2,1)S(1)} %copy-done), custom_call_target="tpu_custom_call" | custom-call | flops 536870912 | bytes 5505024 | tf_op jit(solution)/shard_map/pallas_call | solution.py:140
  51.4 0.0 copy-start.1
  51.5 0.0 copy-start.3
  51.5 2.1 %collective-permute-start.1 = (f32[64,2048]{1,0:T(8,128)S(1)}, f32[64,2048]{1,0:T(8,128)S(1)}, u32[]{:S(2)}, u32[]{:S(2)}) collective-permute-start(f32[64,2048]{1,0:T(8,128)S(1)} %get-tuple-element.20), channel_id=1, source_target_pairs={{0,480},{32,0},{64,32},{96,64},{128,96},{160,128},{192,160},{224,1... | collective-permute-start | bytes 1572872 | tf_op jit(solution)/shard_map/ppermute | solution.py:18
  53.5 3.9 %collective-permute-start.5 = (f32[64,2048]{1,0:T(8,128)S(1)}, f32[64,2048]{1,0:T(8,128)S(1)}, u32[]{:S(2)}, u32[]{:S(2)}) collective-permute-start(f32[64,2048]{1,0:T(8,128)S(1)} %get-tuple-element.24), channel_id=1, source_target_pairs={{0,32},{32,64},{64,96},{96,128},{128,160},{160,192},{192,224},{224... | collective-permute-start | bytes 1572872 | tf_op jit(solution)/shard_map/ppermute | solution.py:18
  57.5 3.7 %shard_map.61 = (f32[64,2048]{1,0:T(8,128)S(1)}, f32[64,2048]{1,0:T(8,128)S(1)}, f32[64,2048]{1,0:T(8,128)S(1)}, f32[64,2048]{1,0:T(8,128)S(1)}, f32[128,2048]{1,0:T(8,128)S(1)}) custom-call(s32[3]{0:T(128)S(1)} %pad_add_fusion.place_ref, bf16[16,32,512]{2,1,0:T(8,128)(2,1)S(1)} %all_to_all.31.mine_ref, ...), custom_call_target="tpu_custom_call" | custom-call | flops 1610612736 | bytes 8126464 | tf_op jit(solution)/shard_map/pallas_call | solution.py:140
  61.2 2.9 %collective-permute-start.3 = (f32[64,2048]{1,0:T(8,128)S(1)}, f32[64,2048]{1,0:T(8,128)S(1)}, u32[]{:S(2)}, u32[]{:S(2)}) collective-permute-start(f32[64,2048]{1,0:T(8,128)S(1)} %get-tuple-element.21), channel_id=1, source_target_pairs={{0,32},{32,64},{64,96},{96,128},{128,160},{160,192},{192,224},{224... | collective-permute-start | bytes 1572872 | tf_op jit(solution)/shard_map/ppermute | solution.py:18
  64.0 4.2 %collective-permute-start.4 = (f32[64,2048]{1,0:T(8,128)S(1)}, f32[64,2048]{1,0:T(8,128)S(1)}, u32[]{:S(2)}, u32[]{:S(2)}) collective-permute-start(f32[64,2048]{1,0:T(8,128)S(1)} %get-tuple-element.22), channel_id=1, source_target_pairs={{0,480},{32,0},{64,32},{96,64},{128,96},{160,128},{192,160},{224,1... | collective-permute-start | bytes 1572872 | tf_op jit(solution)/shard_map/ppermute | solution.py:18
  68.2 0.0 copy-done.1
  68.3 0.0 copy-done.3
  68.3 1.5 shard_map.63.after_ref
  69.8 0.0 collective-permute-done.1.far_ref
  69.8 0.1 shard_map.64
  69.9 1.9 %collective-permute-start.2 = (f32[64,2048]{1,0:T(8,128)S(1)}, f32[64,2048]{1,0:T(8,128)S(1)}, u32[]{:S(2)}, u32[]{:S(2)}) collective-permute-start(f32[64,2048]{1,0:T(8,128)S(1)} %shard_map.64), channel_id=1, source_target_pairs={{0,480},{32,0},{64,32},{96,64},{128,96},{160,128},{192,160},{224,1... | collective-permute-start | bytes 1572872 | tf_op jit(solution)/shard_map/ppermute | solution.py:18
  71.8 0.0 collective-permute-done.5.far_ref
  71.8 0.1 shard_map.65
  71.9 3.9 %collective-permute-start.6 = (f32[64,2048]{1,0:T(8,128)S(1)}, f32[64,2048]{1,0:T(8,128)S(1)}, u32[]{:S(2)}, u32[]{:S(2)}) collective-permute-start(f32[64,2048]{1,0:T(8,128)S(1)} %shard_map.65), channel_id=1, source_target_pairs={{0,32},{32,64},{64,96},{96,128},{128,160},{160,192},{192,224},{224... | collective-permute-start | bytes 1572872 | tf_op jit(solution)/shard_map/ppermute | solution.py:18
  75.8 15.1 %all_to_all.32 = bf16[32,4,2048]{2,1,0:T(4,128)(2,1)S(1)} all-to-all(bf16[32,4,2048]{2,1,0:T(4,128)(2,1)S(1)} %shard_map.63.after_ref), channel_id=1, replica_groups=mesh['sect'=4,'tok'=4,'vocab'=32] {'vocab'}, dimensions={0} | all-to-all | bytes 1048576 | tf_op jit(solution)/shard_map/all_to_all | solution.py:24
  90.9 0.3 copy.6
  91.2 0.0 collective-permute-done.3.lo_b
  91.2 0.0 collective-permute-done.4.hi_a
  91.2 0.0 collective-permute-done.2.lo_a
  91.2 1.9 %collective-permute-done.6.hi_b = f32[64,2048]{1,0:T(8,128)S(1)} collective-permute-done((f32[64,2048]{1,0:T(8,128)S(1)}, f32[64,2048]{1,0:T(8,128)S(1)}, u32[]{:S(2)}, u32[]{:S(2)}) %collective-permute-start.6) | collective-permute-done | bytes 524320 | tf_op jit(solution)/shard_map/ppermute | solution.py:18
  93.1 0.7 shard_map.66
  93.8 11.8 %all_to_all.33.stats_ref = f32[32,8,128]{2,1,0:T(8,128)S(1)} all-to-all(f32[32,8,128]{2,1,0:T(8,128)S(1)} %get-tuple-element.26), channel_id=1, replica_groups=mesh['sect'=4,'tok'=4,'vocab'=32] {'vocab'}, dimensions={0} | all-to-all | bytes 262144 | tf_op jit(solution)/shard_map/all_to_all | solution.py:24
  105.6 0.6 shard_map.67
  106.2 2.4 %collective-permute-start.7 = (bf16[64,2048]{1,0:T(8,128)(2,1)S(1)}, bf16[64,2048]{1,0:T(8,128)(2,1)S(1)}, u32[]{:S(2)}, u32[]{:S(2)}) collective-permute-start(bf16[64,2048]{1,0:T(8,128)(2,1)S(1)} %get-tuple-element.27.refs_6_), channel_id=1, source_target_pairs={{0,32},{32,64},{64,96},{96,128},{128,160},{160,192},{192,224},{224... | collective-permute-start | bytes 786440 | tf_op jit(solution)/shard_map/ppermute | solution.py:18
  108.6 4.6 %collective-permute-start.9 = (bf16[64,2048]{1,0:T(8,128)(2,1)S(1)}, bf16[64,2048]{1,0:T(8,128)(2,1)S(1)}, u32[]{:S(2)}, u32[]{:S(2)}) collective-permute-start(bf16[64,2048]{1,0:T(8,128)(2,1)S(1)} %get-tuple-element.28.refs_7_), channel_id=1, source_target_pairs={{0,480},{32,0},{64,32},{96,64},{128,96},{160,128},{192,160},{224,1... | collective-permute-start | bytes 786440 | tf_op jit(solution)/shard_map/ppermute | solution.py:18
  113.3 1.9 %collective-permute-start.12 = (bf16[64,2048]{1,0:T(8,128)(2,1)S(1)}, bf16[64,2048]{1,0:T(8,128)(2,1)S(1)}, u32[]{:S(2)}, u32[]{:S(2)}) collective-permute-start(bf16[64,2048]{1,0:T(8,128)(2,1)S(1)} %get-tuple-element.27.refs_6_), channel_id=1, source_target_pairs={{0,480},{32,0},{64,32},{96,64},{128,96},{160,128},{192,160},{224,1... | collective-permute-start | bytes 786440 | tf_op jit(solution)/shard_map/ppermute | solution.py:18
  115.2 3.9 %collective-permute-start.11 = (bf16[64,2048]{1,0:T(8,128)(2,1)S(1)}, bf16[64,2048]{1,0:T(8,128)(2,1)S(1)}, u32[]{:S(2)}, u32[]{:S(2)}) collective-permute-start(bf16[64,2048]{1,0:T(8,128)(2,1)S(1)} %get-tuple-element.28.refs_7_), channel_id=1, source_target_pairs={{0,32},{32,64},{64,96},{96,128},{128,160},{160,192},{192,224},{224... | collective-permute-start | bytes 786440 | tf_op jit(solution)/shard_map/ppermute | solution.py:18
  119.1 0.0 collective-permute-done.7.refs_4_
  119.1 1.9 %collective-permute-start.8 = (bf16[64,2048]{1,0:T(8,128)(2,1)S(1)}, bf16[64,2048]{1,0:T(8,128)(2,1)S(1)}, u32[]{:S(2)}, u32[]{:S(2)}) collective-permute-start(bf16[64,2048]{1,0:T(8,128)(2,1)S(1)} %collective-permute-done.7.refs_4_), channel_id=1, source_target_pairs={{0,32},{32,64},{64,96},{96,128},{128,160},{160,192},{192,224},{224... | collective-permute-start | bytes 786440 | tf_op jit(solution)/shard_map/ppermute | solution.py:18
  121.1 0.0 collective-permute-done.9.refs_5_
  121.1 5.1 %collective-permute-start.10 = (bf16[64,2048]{1,0:T(8,128)(2,1)S(1)}, bf16[64,2048]{1,0:T(8,128)(2,1)S(1)}, u32[]{:S(2)}, u32[]{:S(2)}) collective-permute-start(bf16[64,2048]{1,0:T(8,128)(2,1)S(1)} %collective-permute-done.9.refs_5_), channel_id=1, source_target_pairs={{0,480},{32,0},{64,32},{96,64},{128,96},{160,128},{192,160},{224,1... | collective-permute-start | bytes 786440 | tf_op jit(solution)/shard_map/ppermute | solution.py:18
  126.2 0.0 collective-permute-done.12.refs_3_
  126.2 1.3 collective-permute-done.11.refs_2_
  127.5 4.1 %collective-permute-done.8.refs_0_ = bf16[64,2048]{1,0:T(8,128)(2,1)S(1)} collective-permute-done((bf16[64,2048]{1,0:T(8,128)(2,1)S(1)}, bf16[64,2048]{1,0:T(8,128)(2,1)S(1)}, u32[]{:S(2)}, u32[]{:S(2)}) %collective-permute-start.8) | collective-permute-done | bytes 262176 | tf_op jit(solution)/shard_map/ppermute | solution.py:18
  131.7 0.0 collective-permute-done.10.refs_1_
  131.7 3.4 %shard_map.68 = (f32[16,32,512]{2,1,0:T(8,128)S(1)}, f32[16,32,512]{2,1,0:T(8,128)S(1)}) custom-call(s32[3]{0:T(128)S(1)} %pad_add_fusion.place_ref, bf16[1024,2048]{1,0:T(8,128)(2,1)S(1)} %copy-done, bf16[64,2048]{1,0:T(8,128)(2,1)S(1)} %collective-permute-done.8.refs_0_, bf16[64,2048]{1,0:T(8,128)(2,1)S(1)} %collective-permute-done.10.refs_1_, ...), custom_call_target="tpu_custom_call" | custom-call | flops 2147483648 | bytes 8388608 | tf_op jit(solution)/shard_map/pallas_call | solution.py:253
  135.1 1.9 %collective-permute-start.13 = (f32[16,32,512]{2,1,0:T(8,128)S(1)}, f32[16,32,512]{2,1,0:T(8,128)S(1)}, u32[]{:S(2)}, u32[]{:S(2)}) collective-permute-start(f32[16,32,512]{2,1,0:T(8,128)S(1)} %get-tuple-element.30), channel_id=1, source_target_pairs={{0,1},{1,0},{2,3},{3,2},{4,5},{5,4},{6,7},{7,6},{8,9},{9,8},{10,11... | collective-permute-start | bytes 3145736 | tf_op jit(solution)/shard_map/ppermute | solution.py:411
  137.0 2.6 %collective-permute-done.13 = f32[16,32,512]{2,1,0:T(8,128)S(1)} collective-permute-done((f32[16,32,512]{2,1,0:T(8,128)S(1)}, f32[16,32,512]{2,1,0:T(8,128)S(1)}, u32[]{:S(2)}, u32[]{:S(2)}) %collective-permute-start.13) | collective-permute-done | bytes 1048608 | tf_op jit(solution)/shard_map/ppermute | solution.py:411
  139.6 0.2 add.3
  139.9 19.8 %all_to_all.34.parts_ref = f32[16,32,512]{2,1,0:T(8,128)S(1)} all-to-all(f32[16,32,512]{2,1,0:T(8,128)S(1)} %add.3), channel_id=1, replica_groups={{0,2,4,6,8,10,12,14,16,18,20,22,24,26,28,30},{1,3,5,7,9,11,13,15,17,19,..., dimensions={0} | all-to-all | bytes 2097152 | tf_op jit(solution)/shard_map/all_to_all | solution.py:24
  159.6 0.7 shard_map.69
  160.3 18.3 %all_to_all.35.got_ref = f32[4,40,128]{2,1,0:T(8,128)S(1)} all-to-all(f32[4,40,128]{2,1,0:T(8,128)S(1)} %shard_map.69), channel_id=1, replica_groups=mesh['sect'=4,'tok'=4,'vocab'=32] {'sect'}, dimensions={0} | all-to-all | bytes 163840 | tf_op jit(solution)/shard_map/all_to_all | solution.py:24
  178.6 1.3 shard_map.70
Async XLA Ops:
  0.7 0.8 copy-start.2
  29.9 19.2 %copy-start = (bf16[1024,2048]{1,0:T(8,128)(2,1)S(1)}, bf16[1024,2048]{1,0:T(8,128)(2,1)}, u32[]{:S(2)}) copy-start(bf16[1024,2048]{1,0:T(8,128)(2,1)} %w_ref.5) | copy-start | bytes 12582916
  45.3 3.8 %collective-permute-start = (bf16[16,32,512]{2,1,0:T(8,128)(2,1)S(1)}, bf16[16,32,512]{2,1,0:T(8,128)(2,1)S(1)}, u32[]{:S(2)}, u32[]{:S(2)}) collective-permute-start(bf16[16,32,512]{2,1,0:T(8,128)(2,1)S(1)} %all_to_all.31.mine_ref), channel_id=1, source_target_pairs={{0,1},{1,0},{2,3},{3,2},{4,5},{5,4},{6,7},{7,6},{8,9},{9,8},{10,11... | collective-permute-start | bytes 1572872 | tf_op jit(solution)/shard_map/ppermute | solution.py:349
  51.4 16.8 %copy-start.1 = (bf16[4,65536]{1,0:T(4,128)(2,1)S(1)}, bf16[4,65536]{1,0:T(4,128)(2,1)}, u32[]{:S(2)}) copy-start(bf16[4,65536]{1,0:T(4,128)(2,1)} %teacher_ref.1) | copy-start | bytes 1572868
  51.5 16.8 %copy-start.3 = (s32[4,4]{1,0:T(4,128)S(1)}, s32[4,4]{1,0:T(4,128)}, u32[]{:S(2)}) copy-start(s32[4,4]{1,0:T(4,128)} %pairing_ref.1) | copy-start | bytes 196
  51.5 18.3 %collective-permute-start.1 = (f32[64,2048]{1,0:T(8,128)S(1)}, f32[64,2048]{1,0:T(8,128)S(1)}, u32[]{:S(2)}, u32[]{:S(2)}) collective-permute-start(f32[64,2048]{1,0:T(8,128)S(1)} %get-tuple-element.20), channel_id=1, source_target_pairs={{0,480},{32,0},{64,32},{96,64},{128,96},{160,128},{192,160},{224,1... | collective-permute-start | bytes 1572872 | tf_op jit(solution)/shard_map/ppermute | solution.py:18
  53.5 18.3 %collective-permute-start.5 = (f32[64,2048]{1,0:T(8,128)S(1)}, f32[64,2048]{1,0:T(8,128)S(1)}, u32[]{:S(2)}, u32[]{:S(2)}) collective-permute-start(f32[64,2048]{1,0:T(8,128)S(1)} %get-tuple-element.24), channel_id=1, source_target_pairs={{0,32},{32,64},{64,96},{96,128},{128,160},{160,192},{192,224},{224... | collective-permute-start | bytes 1572872 | tf_op jit(solution)/shard_map/ppermute | solution.py:18
  61.2 30.0 %collective-permute-start.3 = (f32[64,2048]{1,0:T(8,128)S(1)}, f32[64,2048]{1,0:T(8,128)S(1)}, u32[]{:S(2)}, u32[]{:S(2)}) collective-permute-start(f32[64,2048]{1,0:T(8,128)S(1)} %get-tuple-element.21), channel_id=1, source_target_pairs={{0,32},{32,64},{64,96},{96,128},{128,160},{160,192},{192,224},{224... | collective-permute-start | bytes 1572872 | tf_op jit(solution)/shard_map/ppermute | solution.py:18
  64.0 27.2 %collective-permute-start.4 = (f32[64,2048]{1,0:T(8,128)S(1)}, f32[64,2048]{1,0:T(8,128)S(1)}, u32[]{:S(2)}, u32[]{:S(2)}) collective-permute-start(f32[64,2048]{1,0:T(8,128)S(1)} %get-tuple-element.22), channel_id=1, source_target_pairs={{0,480},{32,0},{64,32},{96,64},{128,96},{160,128},{192,160},{224,1... | collective-permute-start | bytes 1572872 | tf_op jit(solution)/shard_map/ppermute | solution.py:18
  69.9 21.3 %collective-permute-start.2 = (f32[64,2048]{1,0:T(8,128)S(1)}, f32[64,2048]{1,0:T(8,128)S(1)}, u32[]{:S(2)}, u32[]{:S(2)}) collective-permute-start(f32[64,2048]{1,0:T(8,128)S(1)} %shard_map.64), channel_id=1, source_target_pairs={{0,480},{32,0},{64,32},{96,64},{128,96},{160,128},{192,160},{224,1... | collective-permute-start | bytes 1572872 | tf_op jit(solution)/shard_map/ppermute | solution.py:18
  71.9 21.2 %collective-permute-start.6 = (f32[64,2048]{1,0:T(8,128)S(1)}, f32[64,2048]{1,0:T(8,128)S(1)}, u32[]{:S(2)}, u32[]{:S(2)}) collective-permute-start(f32[64,2048]{1,0:T(8,128)S(1)} %shard_map.65), channel_id=1, source_target_pairs={{0,32},{32,64},{64,96},{96,128},{128,160},{160,192},{192,224},{224... | collective-permute-start | bytes 1572872 | tf_op jit(solution)/shard_map/ppermute | solution.py:18
  106.2 12.9 %collective-permute-start.7 = (bf16[64,2048]{1,0:T(8,128)(2,1)S(1)}, bf16[64,2048]{1,0:T(8,128)(2,1)S(1)}, u32[]{:S(2)}, u32[]{:S(2)}) collective-permute-start(bf16[64,2048]{1,0:T(8,128)(2,1)S(1)} %get-tuple-element.27.refs_6_), channel_id=1, source_target_pairs={{0,32},{32,64},{64,96},{96,128},{128,160},{160,192},{192,224},{224... | collective-permute-start | bytes 786440 | tf_op jit(solution)/shard_map/ppermute | solution.py:18
  108.6 12.4 %collective-permute-start.9 = (bf16[64,2048]{1,0:T(8,128)(2,1)S(1)}, bf16[64,2048]{1,0:T(8,128)(2,1)S(1)}, u32[]{:S(2)}, u32[]{:S(2)}) collective-permute-start(bf16[64,2048]{1,0:T(8,128)(2,1)S(1)} %get-tuple-element.28.refs_7_), channel_id=1, source_target_pairs={{0,480},{32,0},{64,32},{96,64},{128,96},{160,128},{192,160},{224,1... | collective-permute-start | bytes 786440 | tf_op jit(solution)/shard_map/ppermute | solution.py:18
  113.3 13.0 %collective-permute-start.12 = (bf16[64,2048]{1,0:T(8,128)(2,1)S(1)}, bf16[64,2048]{1,0:T(8,128)(2,1)S(1)}, u32[]{:S(2)}, u32[]{:S(2)}) collective-permute-start(bf16[64,2048]{1,0:T(8,128)(2,1)S(1)} %get-tuple-element.27.refs_6_), channel_id=1, source_target_pairs={{0,480},{32,0},{64,32},{96,64},{128,96},{160,128},{192,160},{224,1... | collective-permute-start | bytes 786440 | tf_op jit(solution)/shard_map/ppermute | solution.py:18
  115.2 12.3 %collective-permute-start.11 = (bf16[64,2048]{1,0:T(8,128)(2,1)S(1)}, bf16[64,2048]{1,0:T(8,128)(2,1)S(1)}, u32[]{:S(2)}, u32[]{:S(2)}) collective-permute-start(bf16[64,2048]{1,0:T(8,128)(2,1)S(1)} %get-tuple-element.28.refs_7_), channel_id=1, source_target_pairs={{0,32},{32,64},{64,96},{96,128},{128,160},{160,192},{192,224},{224... | collective-permute-start | bytes 786440 | tf_op jit(solution)/shard_map/ppermute | solution.py:18
  119.1 12.5 %collective-permute-start.8 = (bf16[64,2048]{1,0:T(8,128)(2,1)S(1)}, bf16[64,2048]{1,0:T(8,128)(2,1)S(1)}, u32[]{:S(2)}, u32[]{:S(2)}) collective-permute-start(bf16[64,2048]{1,0:T(8,128)(2,1)S(1)} %collective-permute-done.7.refs_4_), channel_id=1, source_target_pairs={{0,32},{32,64},{64,96},{96,128},{128,160},{160,192},{192,224},{224... | collective-permute-start | bytes 786440 | tf_op jit(solution)/shard_map/ppermute | solution.py:18
  121.1 10.6 %collective-permute-start.10 = (bf16[64,2048]{1,0:T(8,128)(2,1)S(1)}, bf16[64,2048]{1,0:T(8,128)(2,1)S(1)}, u32[]{:S(2)}, u32[]{:S(2)}) collective-permute-start(bf16[64,2048]{1,0:T(8,128)(2,1)S(1)} %collective-permute-done.9.refs_5_), channel_id=1, source_target_pairs={{0,480},{32,0},{64,32},{96,64},{128,96},{160,128},{192,160},{224,1... | collective-permute-start | bytes 786440 | tf_op jit(solution)/shard_map/ppermute | solution.py:18
  135.1 4.6 %collective-permute-start.13 = (f32[16,32,512]{2,1,0:T(8,128)S(1)}, f32[16,32,512]{2,1,0:T(8,128)S(1)}, u32[]{:S(2)}, u32[]{:S(2)}) collective-permute-start(f32[16,32,512]{2,1,0:T(8,128)S(1)} %get-tuple-element.30), channel_id=1, source_target_pairs={{0,1},{1,0},{2,3},{3,2},{4,5},{5,4},{6,7},{7,6},{8,9},{9,8},{10,11... | collective-permute-start | bytes 3145736 | tf_op jit(solution)/shard_map/ppermute | solution.py:411

commit v5 on v4

--- a/solution.py
+++ b/solution.py
@@ -114,13 +114,13 @@
 
         @pl.when(core == 0)
         def _():
-            both[:, 0] = mine_ref[:, :, first:]
-            both[:, 1] = other_ref[:, :, first:]
+            both[:, 0] = mine_ref[:, :, first : first + both.shape[3]]
+            both[:, 1] = other_ref[:, :, first : first + both.shape[3]]
 
         @pl.when(core != 0)
         def _():
-            both[:, 0] = other_ref[:, :, first:]
-            both[:, 1] = mine_ref[:, :, first:]
+            both[:, 0] = other_ref[:, :, first : first + both.shape[3]]
+            both[:, 1] = mine_ref[:, :, first : first + both.shape[3]]
 
         flipped[...] = both[...].reshape(w_ref.shape[0], flipped.shape[0]).T
 
@@ -136,11 +136,10 @@
     tile = 512
     count = sum(sizes)
     pairs, unit, _ = mine.shape
-    half = pl.BlockSpec((pairs, unit, first + count), lambda i: (0, 0, 0))
     return pl.pallas_call(
         functools.partial(logits_kernel, first),
         grid=(width // tile,),
-        in_specs=[SMEM, half, half, pl.BlockSpec((feats, tile), lambda i: (0, i))],
+        in_specs=[SMEM, VMEM, VMEM, pl.BlockSpec((feats, tile), lambda i: (0, i))],
         out_specs=[pl.BlockSpec((size, tile), lambda i: (0, i)) for size in sizes],
         out_shape=[jax.ShapeDtypeStruct((size, width), jnp.float32) for size in sizes],
         scratch_shapes=[
@@ -217,8 +216,9 @@
     high_ref[...] = grad[half:]
 
 
-def hidden_kernel(place_ref, w_ref, *refs):
+def hidden_kernel(earlier, place_ref, w_ref, *refs):
     *pieces, keep_ref, send_ref, window = refs
+    pieces = pieces[: len(pieces) - earlier]
 
     @pl.when(pl.program_id(0) == 0)
     def _():
@@ -244,25 +244,29 @@
         send_ref[...] = result[:, 0]
 
 
-def hidden_grads(place, head_weight, pieces, pairs):
+def hidden_grads(place, head_weight, pieces, pairs, total, earlier=()):
     feats, width = head_weight.shape
     rows = sum(piece.shape[0] for piece in pieces)
+    index = (total - rows) // rows if earlier else 0
     steps = 2
-    shape = jax.ShapeDtypeStruct((pairs, feats // (2 * pairs), rows), jnp.float32)
-    block = pl.BlockSpec((pairs // steps,) + shape.shape[1:], lambda i: (i, 0, 0))
+    shape = jax.ShapeDtypeStruct((pairs, feats // (2 * pairs), total), jnp.float32)
+    block = pl.BlockSpec((pairs // steps, shape.shape[1], rows), lambda i: (i, 0, index))
+    inputs = 2 + len(pieces)
     return pl.pallas_call(
-        hidden_kernel,
+        functools.partial(hidden_kernel, len(earlier)),
         grid=(steps,),
         in_specs=[SMEM, pl.BlockSpec((feats // steps, width), lambda i: (i, 0))]
-        + [pl.BlockSpec(piece.shape, lambda i: (0, 0)) for piece in pieces],
+        + [VMEM] * len(pieces)
+        + [ANYWHERE] * len(earlier),
         out_specs=[block, block],
         out_shape=[shape, shape],
         scratch_shapes=[pltpu.VMEM((rows, width), jnp.bfloat16)],
+        input_output_aliases={inputs + k: k for k in range(len(earlier))},
         compiler_params=params(),
         cost_estimate=cost(
             2 * rows * feats * width, feats * width * 2 + rows * width * 2 + rows * feats * 4
         ),
-    )(place, head_weight, *pieces)
+    )(place, head_weight, *pieces, *earlier)
 
 
 def regroup_kernel(place_ref, parts_ref, div_ref, out_ref):
@@ -272,6 +276,7 @@
     summed = jnp.sum(parts_ref[...], axis=0)
     lane = lax.broadcasted_iota(jnp.int32, (feats, own), 1)
     order = window_order(sections)
+    order = order[sections:] + order[:sections]
     for s in range(sections):
         out = jnp.zeros((feats, own), jnp.float32)
         for piece in range(4):
@@ -402,11 +407,10 @@
     above_low = along_z(low, -1, planes)
     far_below = along_z(below_low, 1, planes)
     far_above = along_z(above_high, -1, planes)
+    near_pieces = [below_high, above_low, below_low, above_high, low, high]
+    near = hidden_grads(place, head_weight, near_pieces, vocabs // 2, rows)
     keep, send = hidden_grads(
-        place,
-        head_weight,
-        [far_below, far_above, below_high, above_low, below_low, above_high, low, high],
-        vocabs // 2,
+        place, head_weight, [far_below, far_above], vocabs // 2, rows, near
     )
     other = lax.ppermute(send, "vocab", other_core)
     parts = exchange(keep + other, "vocab", axis_index_groups=groups)

time: 182 us -> 181 us (level)
  waiting for transfers between devices: 11.8 us -> 8.45 us
  Pallas kernels: 15.4 us -> 17.5 us
    ppermute x12, waiting for transfers between devices: 7.33 us -> 3.95 us  [along_z(): lax.ppermute(value, ('sect', 'tok'), [(i, (i + steps) % planes) for i in...]
    pallas_call x1 -> x2, Pallas kernels: 3.38 us -> 5.49 us  [hidden_grads(): pl.pallas_call(functools.partial(hidden_kernel, len(earlier)), grid=(step...]
  transfers between devices with their start and end apart: 14 -> 14, of which waited for: 5 -> 5; matrix products, arithmetic and copies ran while one was open for 0% -> 0% of each run, Pallas kernels for 3% -> 5%
where the time goes in v5:
time: 181 us; the launch traced here: 179 us
  blocking collectives  108 us (60%)
  starting transfers between devices  42.6 us (24%)
  Pallas kernels  17.5 us (10%)
  waiting for transfers between devices  8.45 us (5%)
    all_to_all x6, blocking collectives, exchange(): lax.all_to_all(value, axis, split_axis=0, concat_axis=0, tiled=True, **gr...  108 us
    ppermute x12, starting transfers between devices, along_z(): lax.ppermute(value, ('sect', 'tok'), [(i, (i + steps) % planes) for i in...  38.8 us
    pallas_call x2, Pallas kernels, partial_logits(): pl.pallas_call(functools.partial(logits_kernel, first), grid=(width // ti...  6.09 us
    pallas_call x2, Pallas kernels, hidden_grads(): pl.pallas_call(functools.partial(hidden_kernel, len(earlier)), grid=(step...  5.49 us
    ppermute x12, waiting for transfers between devices, along_z(): lax.ppermute(value, ('sect', 'tok'), [(i, (i + steps) % planes) for i in...  3.95 us
  transfers between devices with their start and end apart: 14, of which 5 were waited for; matrix products, arithmetic and copies ran while one was open for 0% of the time, Pallas kernels for 5%

profile of v5, /device:TPU:6, one launch (start us, length us, event | category | flops | bytes accessed | tf_op | source)
XLA Modules:
  0.0 178.7 jit_solution(15674171663119422791)
XLA Ops:
  0.6 0.1 pad_add_fusion.place_ref
  0.7 0.0 copy-start.2
  0.7 0.8 copy-done.2
  1.5 0.8 shard_map.59
  2.2 27.6 %all_to_all.30.got_ref = bf16[4,32,128]{2,1,0:T(8,128)(2,1)S(1)} all-to-all(bf16[4,32,128]{2,1,0:T(8,128)(2,1)S(1)} %shard_map.59), channel_id=1, replica_groups=mesh['sect'=4,'tok'=4,'vocab'=32] {'sect'}, dimensions={0} | all-to-all | bytes 65536 | tf_op jit(solution)/shard_map/all_to_all | solution.py:24
  29.9 0.0 copy-start
  29.9 0.2 shard_map.60
  30.1 15.1 %all_to_all.31.mine_ref = bf16[16,32,512]{2,1,0:T(8,128)(2,1)S(1)} all-to-all(bf16[16,32,512]{2,1,0:T(8,128)(2,1)S(1)} %shard_map.60), channel_id=1, replica_groups={{0,2,4,6,8,10,12,14,16,18,20,22,24,26,28,30},{1,3,5,7,9,11,13,15,17,19,..., dimensions={0} | all-to-all | bytes 1048576 | tf_op jit(solution)/shard_map/all_to_all | solution.py:24
  45.3 1.9 %collective-permute-start = (bf16[16,32,512]{2,1,0:T(8,128)(2,1)S(1)}, bf16[16,32,512]{2,1,0:T(8,128)(2,1)S(1)}, u32[]{:S(2)}, u32[]{:S(2)}) collective-permute-start(bf16[16,32,512]{2,1,0:T(8,128)(2,1)S(1)} %all_to_all.31.mine_ref), channel_id=1, source_target_pairs={{0,1},{1,0},{2,3},{3,2},{4,5},{5,4},{6,7},{7,6},{8,9},{9,8},{10,11... | collective-permute-start | bytes 1572872 | tf_op jit(solution)/shard_map/ppermute | solution.py:354
  47.2 1.9 %collective-permute-done.other_ref = bf16[16,32,512]{2,1,0:T(8,128)(2,1)S(1)} collective-permute-done((bf16[16,32,512]{2,1,0:T(8,128)(2,1)S(1)}, bf16[16,32,512]{2,1,0:T(8,128)(2,1)S(1)}, u32[]{:S(2)}, u32[]{:S(2)}) %collective-permute-start) | collective-permute-done | bytes 524320 | tf_op jit(solution)/shard_map/ppermute | solution.py:354
  49.1 0.0 copy-done
  49.1 2.4 %shard_map.62 = (f32[64,2048]{1,0:T(8,128)S(1)}, f32[64,2048]{1,0:T(8,128)S(1)}) custom-call(s32[3]{0:T(128)S(1)} %pad_add_fusion.place_ref, bf16[16,32,512]{2,1,0:T(8,128)(2,1)S(1)} %all_to_all.31.mine_ref, bf16[16,32,512]{2,1,0:T(8,128)(2,1)S(1)} %collective-permute-done.other_ref, bf16[1024,2048]{1,0:T(8,128)(2,1)S(1)} %copy-done), custom_call_target="tpu_custom_call" | custom-call | flops 536870912 | bytes 5505024 | tf_op jit(solution)/shard_map/pallas_call | solution.py:139
  51.4 0.0 copy-start.1
  51.5 0.0 copy-start.3
  51.5 2.1 %collective-permute-start.1 = (f32[64,2048]{1,0:T(8,128)S(1)}, f32[64,2048]{1,0:T(8,128)S(1)}, u32[]{:S(2)}, u32[]{:S(2)}) collective-permute-start(f32[64,2048]{1,0:T(8,128)S(1)} %get-tuple-element.22), channel_id=1, source_target_pairs={{0,480},{32,0},{64,32},{96,64},{128,96},{160,128},{192,160},{224,1... | collective-permute-start | bytes 1572872 | tf_op jit(solution)/shard_map/ppermute | solution.py:18
  53.5 3.9 %collective-permute-start.5 = (f32[64,2048]{1,0:T(8,128)S(1)}, f32[64,2048]{1,0:T(8,128)S(1)}, u32[]{:S(2)}, u32[]{:S(2)}) collective-permute-start(f32[64,2048]{1,0:T(8,128)S(1)} %get-tuple-element.26), channel_id=1, source_target_pairs={{0,32},{32,64},{64,96},{96,128},{128,160},{160,192},{192,224},{224... | collective-permute-start | bytes 1572872 | tf_op jit(solution)/shard_map/ppermute | solution.py:18
  57.5 3.7 %shard_map.61 = (f32[64,2048]{1,0:T(8,128)S(1)}, f32[64,2048]{1,0:T(8,128)S(1)}, f32[64,2048]{1,0:T(8,128)S(1)}, f32[64,2048]{1,0:T(8,128)S(1)}, f32[128,2048]{1,0:T(8,128)S(1)}) custom-call(s32[3]{0:T(128)S(1)} %pad_add_fusion.place_ref, bf16[16,32,512]{2,1,0:T(8,128)(2,1)S(1)} %all_to_all.31.mine_ref, ...), custom_call_target="tpu_custom_call" | custom-call | flops 1610612736 | bytes 8126464 | tf_op jit(solution)/shard_map/pallas_call | solution.py:139
  61.2 2.9 %collective-permute-start.3 = (f32[64,2048]{1,0:T(8,128)S(1)}, f32[64,2048]{1,0:T(8,128)S(1)}, u32[]{:S(2)}, u32[]{:S(2)}) collective-permute-start(f32[64,2048]{1,0:T(8,128)S(1)} %get-tuple-element.23), channel_id=1, source_target_pairs={{0,32},{32,64},{64,96},{96,128},{128,160},{160,192},{192,224},{224... | collective-permute-start | bytes 1572872 | tf_op jit(solution)/shard_map/ppermute | solution.py:18
  64.0 4.2 %collective-permute-start.4 = (f32[64,2048]{1,0:T(8,128)S(1)}, f32[64,2048]{1,0:T(8,128)S(1)}, u32[]{:S(2)}, u32[]{:S(2)}) collective-permute-start(f32[64,2048]{1,0:T(8,128)S(1)} %get-tuple-element.24), channel_id=1, source_target_pairs={{0,480},{32,0},{64,32},{96,64},{128,96},{160,128},{192,160},{224,1... | collective-permute-start | bytes 1572872 | tf_op jit(solution)/shard_map/ppermute | solution.py:18
  68.3 0.0 copy-done.1
  68.3 0.0 copy-done.3
  68.3 1.5 shard_map.63.after_ref
  69.8 0.0 collective-permute-done.1.far_ref
  69.8 0.1 shard_map.64
  69.9 1.9 %collective-permute-start.2 = (f32[64,2048]{1,0:T(8,128)S(1)}, f32[64,2048]{1,0:T(8,128)S(1)}, u32[]{:S(2)}, u32[]{:S(2)}) collective-permute-start(f32[64,2048]{1,0:T(8,128)S(1)} %shard_map.64), channel_id=1, source_target_pairs={{0,480},{32,0},{64,32},{96,64},{128,96},{160,128},{192,160},{224,1... | collective-permute-start | bytes 1572872 | tf_op jit(solution)/shard_map/ppermute | solution.py:18
  71.8 0.0 collective-permute-done.5.far_ref
  71.8 0.1 shard_map.65
  71.9 3.9 %collective-permute-start.6 = (f32[64,2048]{1,0:T(8,128)S(1)}, f32[64,2048]{1,0:T(8,128)S(1)}, u32[]{:S(2)}, u32[]{:S(2)}) collective-permute-start(f32[64,2048]{1,0:T(8,128)S(1)} %shard_map.65), channel_id=1, source_target_pairs={{0,32},{32,64},{64,96},{96,128},{128,160},{160,192},{192,224},{224... | collective-permute-start | bytes 1572872 | tf_op jit(solution)/shard_map/ppermute | solution.py:18
  75.8 15.1 %all_to_all.32 = bf16[32,4,2048]{2,1,0:T(4,128)(2,1)S(1)} all-to-all(bf16[32,4,2048]{2,1,0:T(4,128)(2,1)S(1)} %shard_map.63.after_ref), channel_id=1, replica_groups=mesh['sect'=4,'tok'=4,'vocab'=32] {'vocab'}, dimensions={0} | all-to-all | bytes 1048576 | tf_op jit(solution)/shard_map/all_to_all | solution.py:24
  90.9 0.3 copy.8
  91.2 0.0 collective-permute-done.3.lo_b
  91.2 0.0 collective-permute-done.4.hi_a
  91.2 0.0 collective-permute-done.2.lo_a
  91.2 1.8 %collective-permute-done.6.hi_b = f32[64,2048]{1,0:T(8,128)S(1)} collective-permute-done((f32[64,2048]{1,0:T(8,128)S(1)}, f32[64,2048]{1,0:T(8,128)S(1)}, u32[]{:S(2)}, u32[]{:S(2)}) %collective-permute-start.6) | collective-permute-done | bytes 524320 | tf_op jit(solution)/shard_map/ppermute | solution.py:18
  93.1 0.7 shard_map.66
  93.8 11.8 %all_to_all.33.stats_ref = f32[32,8,128]{2,1,0:T(8,128)S(1)} all-to-all(f32[32,8,128]{2,1,0:T(8,128)S(1)} %get-tuple-element.28), channel_id=1, replica_groups=mesh['sect'=4,'tok'=4,'vocab'=32] {'vocab'}, dimensions={0} | all-to-all | bytes 262144 | tf_op jit(solution)/shard_map/all_to_all | solution.py:24
  105.6 0.6 shard_map.67
  106.2 2.4 %collective-permute-start.7 = (bf16[64,2048]{1,0:T(8,128)(2,1)S(1)}, bf16[64,2048]{1,0:T(8,128)(2,1)S(1)}, u32[]{:S(2)}, u32[]{:S(2)}) collective-permute-start(bf16[64,2048]{1,0:T(8,128)(2,1)S(1)} %get-tuple-element.29.refs_4_), channel_id=1, source_target_pairs={{0,32},{32,64},{64,96},{96,128},{128,160},{160,192},{192,224},{224... | collective-permute-start | bytes 786440 | tf_op jit(solution)/shard_map/ppermute | solution.py:18
  108.6 4.6 %collective-permute-start.9 = (bf16[64,2048]{1,0:T(8,128)(2,1)S(1)}, bf16[64,2048]{1,0:T(8,128)(2,1)S(1)}, u32[]{:S(2)}, u32[]{:S(2)}) collective-permute-start(bf16[64,2048]{1,0:T(8,128)(2,1)S(1)} %get-tuple-element.30.refs_5_), channel_id=1, source_target_pairs={{0,480},{32,0},{64,32},{96,64},{128,96},{160,128},{192,160},{224,1... | collective-permute-start | bytes 786440 | tf_op jit(solution)/shard_map/ppermute | solution.py:18
  113.3 1.9 %collective-permute-start.12 = (bf16[64,2048]{1,0:T(8,128)(2,1)S(1)}, bf16[64,2048]{1,0:T(8,128)(2,1)S(1)}, u32[]{:S(2)}, u32[]{:S(2)}) collective-permute-start(bf16[64,2048]{1,0:T(8,128)(2,1)S(1)} %get-tuple-element.29.refs_4_), channel_id=1, source_target_pairs={{0,480},{32,0},{64,32},{96,64},{128,96},{160,128},{192,160},{224,1... | collective-permute-start | bytes 786440 | tf_op jit(solution)/shard_map/ppermute | solution.py:18
  115.2 3.9 %collective-permute-start.11 = (bf16[64,2048]{1,0:T(8,128)(2,1)S(1)}, bf16[64,2048]{1,0:T(8,128)(2,1)S(1)}, u32[]{:S(2)}, u32[]{:S(2)}) collective-permute-start(bf16[64,2048]{1,0:T(8,128)(2,1)S(1)} %get-tuple-element.30.refs_5_), channel_id=1, source_target_pairs={{0,32},{32,64},{64,96},{96,128},{128,160},{160,192},{192,224},{224... | collective-permute-start | bytes 786440 | tf_op jit(solution)/shard_map/ppermute | solution.py:18
  119.1 0.0 collective-permute-done.7.refs_2_
  119.1 1.9 %collective-permute-start.8 = (bf16[64,2048]{1,0:T(8,128)(2,1)S(1)}, bf16[64,2048]{1,0:T(8,128)(2,1)S(1)}, u32[]{:S(2)}, u32[]{:S(2)}) collective-permute-start(bf16[64,2048]{1,0:T(8,128)(2,1)S(1)} %collective-permute-done.7.refs_2_), channel_id=1, source_target_pairs={{0,32},{32,64},{64,96},{96,128},{128,160},{160,192},{192,224},{224... | collective-permute-start | bytes 786440 | tf_op jit(solution)/shard_map/ppermute | solution.py:18
  121.1 0.0 collective-permute-done.9.refs_3_
  121.1 5.1 %collective-permute-start.10 = (bf16[64,2048]{1,0:T(8,128)(2,1)S(1)}, bf16[64,2048]{1,0:T(8,128)(2,1)S(1)}, u32[]{:S(2)}, u32[]{:S(2)}) collective-permute-start(bf16[64,2048]{1,0:T(8,128)(2,1)S(1)} %collective-permute-done.9.refs_3_), channel_id=1, source_target_pairs={{0,480},{32,0},{64,32},{96,64},{128,96},{160,128},{192,160},{224,1... | collective-permute-start | bytes 786440 | tf_op jit(solution)/shard_map/ppermute | solution.py:18
  126.2 0.0 collective-permute-done.12.refs_1_
  126.2 1.3 collective-permute-done.11.refs_0_
  127.5 3.4 %shard_map.68 = (f32[16,32,512]{2,1,0:T(8,128)S(1)}, f32[16,32,512]{2,1,0:T(8,128)S(1)}) custom-call(s32[3]{0:T(128)S(1)} %pad_add_fusion.place_ref, bf16[1024,2048]{1,0:T(8,128)(2,1)S(1)} %copy-done, bf16[64,2048]{1,0:T(8,128)(2,1)S(1)} %collective-permute-done.11.refs_0_, bf16[64,2048]{1,0:T(8,128)(2,1)S(1)} %collective-permute-done.12.refs_1_, ...), custom_call_target="tpu_custom_call" | custom-call | flops 1610612736 | bytes 7340032 | tf_op jit(solution)/shard_map/pallas_call | solution.py:255
  130.9 0.8 collective-permute-done.8.refs_0_
  131.7 0.0 collective-permute-done.10.refs_1_
  131.7 2.1 %shard_map.69 = (f32[16,32,512]{2,1,0:T(8,128)S(1)}, f32[16,32,512]{2,1,0:T(8,128)S(1)}) custom-call(s32[3]{0:T(128)S(1)} %pad_add_fusion.place_ref, bf16[1024,2048]{1,0:T(8,128)(2,1)S(1)} %copy-done, bf16[64,2048]{1,0:T(8,128)(2,1)S(1)} %collective-permute-done.8.refs_0_, ...), custom_call_target="tpu_custom_call", output_to_operand_aliasing={{0}: (4, {}), {1}: (5, {})} | custom-call | flops 536870912 | bytes 5242880 | tf_op jit(solution)/shard_map/pallas_call | solution.py:255
  133.8 1.9 %collective-permute-start.13 = (f32[16,32,512]{2,1,0:T(8,128)S(1)}, f32[16,32,512]{2,1,0:T(8,128)S(1)}, u32[]{:S(2)}, u32[]{:S(2)}) collective-permute-start(f32[16,32,512]{2,1,0:T(8,128)S(1)} %get-tuple-element.34), channel_id=1, source_target_pairs={{0,1},{1,0},{2,3},{3,2},{4,5},{5,4},{6,7},{7,6},{8,9},{9,8},{10,11... | collective-permute-start | bytes 3145736 | tf_op jit(solution)/shard_map/ppermute | solution.py:415
  135.7 2.6 %collective-permute-done.13 = f32[16,32,512]{2,1,0:T(8,128)S(1)} collective-permute-done((f32[16,32,512]{2,1,0:T(8,128)S(1)}, f32[16,32,512]{2,1,0:T(8,128)S(1)}, u32[]{:S(2)}, u32[]{:S(2)}) %collective-permute-start.13) | collective-permute-done | bytes 1048608 | tf_op jit(solution)/shard_map/ppermute | solution.py:415
  138.4 0.2 add.3
  138.6 19.8 %all_to_all.34.parts_ref = f32[16,32,512]{2,1,0:T(8,128)S(1)} all-to-all(f32[16,32,512]{2,1,0:T(8,128)S(1)} %add.3), channel_id=1, replica_groups={{0,2,4,6,8,10,12,14,16,18,20,22,24,26,28,30},{1,3,5,7,9,11,13,15,17,19,..., dimensions={0} | all-to-all | bytes 2097152 | tf_op jit(solution)/shard_map/all_to_all | solution.py:24
  158.4 0.7 shard_map.70
  159.0 18.3 %all_to_all.35.got_ref = f32[4,40,128]{2,1,0:T(8,128)S(1)} all-to-all(f32[4,40,128]{2,1,0:T(8,128)S(1)} %shard_map.70), channel_id=1, replica_groups=mesh['sect'=4,'tok'=4,'vocab'=32] {'sect'}, dimensions={0} | all-to-all | bytes 163840 | tf_op jit(solution)/shard_map/all_to_all | solution.py:24
  177.3 1.3 shard_map.71
Async XLA Ops:
  0.7 0.8 copy-start.2
  29.9 19.2 %copy-start = (bf16[1024,2048]{1,0:T(8,128)(2,1)S(1)}, bf16[1024,2048]{1,0:T(8,128)(2,1)}, u32[]{:S(2)}) copy-start(bf16[1024,2048]{1,0:T(8,128)(2,1)} %w_ref.7) | copy-start | bytes 12582916
  45.3 3.8 %collective-permute-start = (bf16[16,32,512]{2,1,0:T(8,128)(2,1)S(1)}, bf16[16,32,512]{2,1,0:T(8,128)(2,1)S(1)}, u32[]{:S(2)}, u32[]{:S(2)}) collective-permute-start(bf16[16,32,512]{2,1,0:T(8,128)(2,1)S(1)} %all_to_all.31.mine_ref), channel_id=1, source_target_pairs={{0,1},{1,0},{2,3},{3,2},{4,5},{5,4},{6,7},{7,6},{8,9},{9,8},{10,11... | collective-permute-start | bytes 1572872 | tf_op jit(solution)/shard_map/ppermute | solution.py:354
  51.4 16.8 %copy-start.1 = (bf16[4,65536]{1,0:T(4,128)(2,1)S(1)}, bf16[4,65536]{1,0:T(4,128)(2,1)}, u32[]{:S(2)}) copy-start(bf16[4,65536]{1,0:T(4,128)(2,1)} %teacher_ref.1) | copy-start | bytes 1572868
  51.5 16.8 %copy-start.3 = (s32[4,4]{1,0:T(4,128)S(1)}, s32[4,4]{1,0:T(4,128)}, u32[]{:S(2)}) copy-start(s32[4,4]{1,0:T(4,128)} %pairing_ref.1) | copy-start | bytes 196
  51.5 18.3 %collective-permute-start.1 = (f32[64,2048]{1,0:T(8,128)S(1)}, f32[64,2048]{1,0:T(8,128)S(1)}, u32[]{:S(2)}, u32[]{:S(2)}) collective-permute-start(f32[64,2048]{1,0:T(8,128)S(1)} %get-tuple-element.22), channel_id=1, source_target_pairs={{0,480},{32,0},{64,32},{96,64},{128,96},{160,128},{192,160},{224,1... | collective-permute-start | bytes 1572872 | tf_op jit(solution)/shard_map/ppermute | solution.py:18
  53.5 18.3 %collective-permute-start.5 = (f32[64,2048]{1,0:T(8,128)S(1)}, f32[64,2048]{1,0:T(8,128)S(1)}, u32[]{:S(2)}, u32[]{:S(2)}) collective-permute-start(f32[64,2048]{1,0:T(8,128)S(1)} %get-tuple-element.26), channel_id=1, source_target_pairs={{0,32},{32,64},{64,96},{96,128},{128,160},{160,192},{192,224},{224... | collective-permute-start | bytes 1572872 | tf_op jit(solution)/shard_map/ppermute | solution.py:18
  61.2 30.0 %collective-permute-start.3 = (f32[64,2048]{1,0:T(8,128)S(1)}, f32[64,2048]{1,0:T(8,128)S(1)}, u32[]{:S(2)}, u32[]{:S(2)}) collective-permute-start(f32[64,2048]{1,0:T(8,128)S(1)} %get-tuple-element.23), channel_id=1, source_target_pairs={{0,32},{32,64},{64,96},{96,128},{128,160},{160,192},{192,224},{224... | collective-permute-start | bytes 1572872 | tf_op jit(solution)/shard_map/ppermute | solution.py:18
  64.0 27.2 %collective-permute-start.4 = (f32[64,2048]{1,0:T(8,128)S(1)}, f32[64,2048]{1,0:T(8,128)S(1)}, u32[]{:S(2)}, u32[]{:S(2)}) collective-permute-start(f32[64,2048]{1,0:T(8,128)S(1)} %get-tuple-element.24), channel_id=1, source_target_pairs={{0,480},{32,0},{64,32},{96,64},{128,96},{160,128},{192,160},{224,1... | collective-permute-start | bytes 1572872 | tf_op jit(solution)/shard_map/ppermute | solution.py:18
  69.9 21.3 %collective-permute-start.2 = (f32[64,2048]{1,0:T(8,128)S(1)}, f32[64,2048]{1,0:T(8,128)S(1)}, u32[]{:S(2)}, u32[]{:S(2)}) collective-permute-start(f32[64,2048]{1,0:T(8,128)S(1)} %shard_map.64), channel_id=1, source_target_pairs={{0,480},{32,0},{64,32},{96,64},{128,96},{160,128},{192,160},{224,1... | collective-permute-start | bytes 1572872 | tf_op jit(solution)/shard_map/ppermute | solution.py:18
  71.9 21.2 %collective-permute-start.6 = (f32[64,2048]{1,0:T(8,128)S(1)}, f32[64,2048]{1,0:T(8,128)S(1)}, u32[]{:S(2)}, u32[]{:S(2)}) collective-permute-start(f32[64,2048]{1,0:T(8,128)S(1)} %shard_map.65), channel_id=1, source_target_pairs={{0,32},{32,64},{64,96},{96,128},{128,160},{160,192},{192,224},{224... | collective-permute-start | bytes 1572872 | tf_op jit(solution)/shard_map/ppermute | solution.py:18
  106.2 12.9 %collective-permute-start.7 = (bf16[64,2048]{1,0:T(8,128)(2,1)S(1)}, bf16[64,2048]{1,0:T(8,128)(2,1)S(1)}, u32[]{:S(2)}, u32[]{:S(2)}) collective-permute-start(bf16[64,2048]{1,0:T(8,128)(2,1)S(1)} %get-tuple-element.29.refs_4_), channel_id=1, source_target_pairs={{0,32},{32,64},{64,96},{96,128},{128,160},{160,192},{192,224},{224... | collective-permute-start | bytes 786440 | tf_op jit(solution)/shard_map/ppermute | solution.py:18
  108.6 12.4 %collective-permute-start.9 = (bf16[64,2048]{1,0:T(8,128)(2,1)S(1)}, bf16[64,2048]{1,0:T(8,128)(2,1)S(1)}, u32[]{:S(2)}, u32[]{:S(2)}) collective-permute-start(bf16[64,2048]{1,0:T(8,128)(2,1)S(1)} %get-tuple-element.30.refs_5_), channel_id=1, source_target_pairs={{0,480},{32,0},{64,32},{96,64},{128,96},{160,128},{192,160},{224,1... | collective-permute-start | bytes 786440 | tf_op jit(solution)/shard_map/ppermute | solution.py:18
  113.3 13.0 %collective-permute-start.12 = (bf16[64,2048]{1,0:T(8,128)(2,1)S(1)}, bf16[64,2048]{1,0:T(8,128)(2,1)S(1)}, u32[]{:S(2)}, u32[]{:S(2)}) collective-permute-start(bf16[64,2048]{1,0:T(8,128)(2,1)S(1)} %get-tuple-element.29.refs_4_), channel_id=1, source_target_pairs={{0,480},{32,0},{64,32},{96,64},{128,96},{160,128},{192,160},{224,1... | collective-permute-start | bytes 786440 | tf_op jit(solution)/shard_map/ppermute | solution.py:18
  115.2 12.3 %collective-permute-start.11 = (bf16[64,2048]{1,0:T(8,128)(2,1)S(1)}, bf16[64,2048]{1,0:T(8,128)(2,1)S(1)}, u32[]{:S(2)}, u32[]{:S(2)}) collective-permute-start(bf16[64,2048]{1,0:T(8,128)(2,1)S(1)} %get-tuple-element.30.refs_5_), channel_id=1, source_target_pairs={{0,32},{32,64},{64,96},{96,128},{128,160},{160,192},{192,224},{224... | collective-permute-start | bytes 786440 | tf_op jit(solution)/shard_map/ppermute | solution.py:18
  119.1 12.5 %collective-permute-start.8 = (bf16[64,2048]{1,0:T(8,128)(2,1)S(1)}, bf16[64,2048]{1,0:T(8,128)(2,1)S(1)}, u32[]{:S(2)}, u32[]{:S(2)}) collective-permute-start(bf16[64,2048]{1,0:T(8,128)(2,1)S(1)} %collective-permute-done.7.refs_2_), channel_id=1, source_target_pairs={{0,32},{32,64},{64,96},{96,128},{128,160},{160,192},{192,224},{224... | collective-permute-start | bytes 786440 | tf_op jit(solution)/shard_map/ppermute | solution.py:18
  121.1 10.6 %collective-permute-start.10 = (bf16[64,2048]{1,0:T(8,128)(2,1)S(1)}, bf16[64,2048]{1,0:T(8,128)(2,1)S(1)}, u32[]{:S(2)}, u32[]{:S(2)}) collective-permute-start(bf16[64,2048]{1,0:T(8,128)(2,1)S(1)} %collective-permute-done.9.refs_3_), channel_id=1, source_target_pairs={{0,480},{32,0},{64,32},{96,64},{128,96},{160,128},{192,160},{224,1... | collective-permute-start | bytes 786440 | tf_op jit(solution)/shard_map/ppermute | solution.py:18
  133.8 4.6 %collective-permute-start.13 = (f32[16,32,512]{2,1,0:T(8,128)S(1)}, f32[16,32,512]{2,1,0:T(8,128)S(1)}, u32[]{:S(2)}, u32[]{:S(2)}) collective-permute-start(f32[16,32,512]{2,1,0:T(8,128)S(1)} %get-tuple-element.34), channel_id=1, source_target_pairs={{0,1},{1,0},{2,3},{3,2},{4,5},{5,4},{6,7},{7,6},{8,9},{9,8},{10,11... | collective-permute-start | bytes 3145736 | tf_op jit(solution)/shard_map/ppermute | solution.py:415

commit v6 on v5

--- a/solution.py
+++ b/solution.py
@@ -14,10 +14,19 @@
 ANYWHERE = pl.BlockSpec(memory_space=pl.ANY)
 
 
-def along_z(value, steps, planes):
-    return lax.ppermute(
-        value, ("sect", "tok"), [(i, (i + steps) % planes) for i in range(planes)]
-    )
+def along_z(value, steps, planes, vocabs):
+    pairs = []
+    for plane in range(planes):
+        for device in range(vocabs):
+            there = (plane + (-steps if device % 2 else steps)) % planes
+            pairs.append((plane * vocabs + device, there * vocabs + device))
+    return lax.ppermute(value, ("sect", "tok", "vocab"), pairs)
+
+
+def halves(core, half, start=0):
+    first = pl.multiple_of(start + core * half, half)
+    second = pl.multiple_of(start + (1 - core) * half, half)
+    return pl.ds(first, half), pl.ds(second, half)
 
 
 def exchange(value, axis, **groups):
@@ -122,7 +131,16 @@
             both[:, 0] = other_ref[:, :, first : first + both.shape[3]]
             both[:, 1] = mine_ref[:, :, first : first + both.shape[3]]
 
-        flipped[...] = both[...].reshape(w_ref.shape[0], flipped.shape[0]).T
+        turned = both[...].reshape(w_ref.shape[0], flipped.shape[0]).T
+        start = 0
+        for one in outs[0 : len(outs) // 2 * 2 : 2]:
+            half = one.shape[0]
+            low, high = halves(core, half, start)
+            flipped[low] = turned[start : start + half]
+            flipped[high] = turned[start + half : start + 2 * half]
+            start += 2 * half
+        if len(outs) % 2:
+            flipped[start:] = turned[start:]
 
     result = jnp.dot(flipped[...], w_ref[...], preferred_element_type=jnp.float32)
     start = 0
@@ -153,29 +171,34 @@
     )(place, mine, other, head_weight)
 
 
-def order_kernel(place_ref, pairing_ref, teacher_ref, after_ref, ordered_ref):
-    vocabs, sections, width = ordered_ref.shape
-    section = place_ref[0]
-    paired = [pairing_ref[section, k] for k in range(sections)]
-    for v in range(vocabs):
-        rows = teacher_ref[:, v * width : (v + 1) * width].astype(jnp.float32)
-        row = lax.broadcasted_iota(jnp.int32, (sections, width), 0)
-        out = jnp.zeros((sections, width), jnp.float32)
-        for k in range(sections):
-            out = jnp.where(row == paired[k], rows[k : k + 1], out)
-        ordered_ref[v] = out.astype(jnp.bfloat16)
-
-
-def add_kernel(mine_ref, far_ref, after_ref, out_ref):
+def add_kernel(mine_ref, far_ref, out_ref):
     out_ref[...] = mine_ref[...] + far_ref[...]
 
 
-def stats_kernel(own_ref, lo_a, lo_b, hi_a, hi_b, teacher_ref, logits_ref, stats_ref):
-    half = lo_a.shape[0]
-    logits_ref[:half] = own_ref[:half] + lo_a[...] + lo_b[...]
-    logits_ref[half:] = own_ref[half:] + hi_a[...] + hi_b[...]
+def stats_kernel(
+    place_ref,
+    pairing_ref,
+    own_ref,
+    next_first,
+    near_second,
+    near_first,
+    next_second,
+    teacher_ref,
+    logits_ref,
+    sorted_ref,
+    stats_ref,
+):
+    half = next_first.shape[0]
+    one, two = halves(remainder(place_ref[2], 2), half)
+    logits_ref[one] = own_ref[one] + next_first[...] + near_second[...]
+    logits_ref[two] = own_ref[two] + near_first[...] + next_second[...]
+    sections = pairing_ref.shape[0]
+    unit = own_ref.shape[0] // sections
+    for k in range(sections):
+        begin = pl.multiple_of(pairing_ref[place_ref[0], k] * unit, unit)
+        sorted_ref[pl.ds(begin, unit)] = teacher_ref[k * unit : (k + 1) * unit]
     logits = logits_ref[...]
-    teacher = teacher_ref[...].astype(jnp.float32)
+    teacher = sorted_ref[...].astype(jnp.float32)
     top_s = jnp.max(logits, axis=1, keepdims=True)
     top_t = jnp.max(teacher, axis=1, keepdims=True)
     sum_s = jnp.sum(jnp.exp(logits - top_s), axis=1, keepdims=True)
@@ -192,7 +215,9 @@
         stats_ref[k] = rows
 
 
-def grads_kernel(logits_ref, teacher_ref, stats_ref, low_ref, high_ref, div_ref):
+def grads_kernel(
+    place_ref, logits_ref, teacher_ref, stats_ref, first_ref, second_ref, div_ref, columns
+):
     stats = stats_ref[...]
     top = jnp.max(stats, axis=0)
     scale = jnp.exp(stats[:, :2] - top[None, :2])
@@ -207,13 +232,14 @@
     packed = jnp.zeros((128, own), jnp.float32)
     for place, values in enumerate((top_s, top_t, loss_scale / total_s, loss_scale / total_t)):
         packed = jnp.where(row == place, values, packed)
-    columns = packed.T
-    grad = (
-        jnp.exp(logits_ref[...] - columns[:, 0:1]) * columns[:, 2:3]
-        - jnp.exp(teacher_ref[...].astype(jnp.float32) - columns[:, 1:2]) * columns[:, 3:4]
-    ).astype(jnp.bfloat16)
-    low_ref[...] = grad[:half]
-    high_ref[...] = grad[half:]
+    columns[...] = packed.T
+    places = halves(remainder(place_ref[2], 2), half)
+    for place, out_ref in zip(places, (first_ref, second_ref)):
+        values = columns[place]
+        out_ref[...] = (
+            jnp.exp(logits_ref[place] - values[:, 0:1]) * values[:, 2:3]
+            - jnp.exp(teacher_ref[place].astype(jnp.float32) - values[:, 1:2]) * values[:, 3:4]
+        ).astype(jnp.bfloat16)
 
 
 def hidden_kernel(earlier, place_ref, w_ref, *refs):
@@ -223,9 +249,12 @@
     @pl.when(pl.program_id(0) == 0)
     def _():
         start = 0
-        for piece in pieces:
-            window[start : start + piece.shape[0]] = piece[...]
-            start += piece.shape[0]
+        for one, two in zip(pieces[0::2], pieces[1::2]):
+            half = one.shape[0]
+            low, high = halves(remainder(place_ref[2], 2), half, start)
+            window[low] = one[...]
+            window[high] = two[...]
+            start += 2 * half
 
     pairs, feats, rows = keep_ref.shape
     result = lax.dot_general(
@@ -353,64 +382,64 @@
     mine = exchange(spread, "vocab", axis_index_groups=groups)
     other = lax.ppermute(mine, "vocab", other_core)
 
-    edge_down, edge_up = partial_logits(
-        place, mine, other, head_weight, 0, [half, half]
-    )
-    far_down = along_z(edge_down, -1, planes)
-    far_up = along_z(edge_up, 1, planes)
-    near_down, near_up, next_down, next_up, kept = partial_logits(
+    shift = functools.partial(along_z, planes=planes, vocabs=vocabs)
+    edge_first, edge_second = partial_logits(place, mine, other, head_weight, 0, [half, half])
+    far_first = shift(edge_first, -1)
+    far_second = shift(edge_second, 1)
+    near_first, near_second, next_first, next_second, kept = partial_logits(
         place, mine, other, head_weight, own, [half, half, half, half, own]
     )
-    down_b = along_z(near_down, -1, planes)
-    up_a = along_z(near_up, 1, planes)
-
-    ordered = pl.pallas_call(
-        order_kernel,
-        in_specs=[SMEM, SMEM, VMEM, ANYWHERE],
-        out_specs=VMEM,
-        out_shape=jax.ShapeDtypeStruct((vocabs, sections, width), jnp.bfloat16),
-        compiler_params=params(),
-    )(place, pairing, teacher_logits, kept)
+    near_first = shift(near_first, -1)
+    near_second = shift(near_second, 1)
 
     add = pl.pallas_call(
         add_kernel,
-        in_specs=[VMEM, VMEM, ANYWHERE],
+        in_specs=[VMEM, VMEM],
         out_specs=VMEM,
-        out_shape=jax.ShapeDtypeStruct(next_down.shape, jnp.float32),
+        out_shape=jax.ShapeDtypeStruct(next_first.shape, jnp.float32),
         compiler_params=params(),
     )
-    down_a = along_z(add(next_down, far_down, ordered), -1, planes)
-    up_b = along_z(add(next_up, far_up, ordered), 1, planes)
-    teacher = exchange(ordered, "vocab").transpose(1, 0, 2).reshape(own, width)
-
-    logits, stats = pl.pallas_call(
+    next_first = shift(add(next_first, far_first), -1)
+    next_second = shift(add(next_second, far_second), 1)
+
+    teacher_logits, _ = lax.optimization_barrier((teacher_logits, kept))
+    teacher = teacher_logits.reshape(sections, vocabs, width).transpose(1, 0, 2)
+    teacher = exchange(teacher, "vocab").transpose(1, 0, 2).reshape(own, width)
+
+    logits, teacher, stats = pl.pallas_call(
         stats_kernel,
+        in_specs=[SMEM, SMEM] + [VMEM] * 6,
+        out_specs=[VMEM] * 3,
         out_shape=[
             jax.ShapeDtypeStruct((own, width), jnp.float32),
+            jax.ShapeDtypeStruct((own, width), jnp.bfloat16),
             jax.ShapeDtypeStruct((vocabs, 8, own), jnp.float32),
         ],
         compiler_params=params(),
-    )(kept, down_a, up_a, down_b, up_b, teacher)
-    low, high, diverge = pl.pallas_call(
+    )(place, pairing, kept, next_first, near_second, near_first, next_second, teacher)
+    first, second, diverge = pl.pallas_call(
         grads_kernel,
+        in_specs=[SMEM] + [VMEM] * 3,
+        out_specs=[VMEM] * 3,
         out_shape=[
             jax.ShapeDtypeStruct((half, width), jnp.bfloat16),
             jax.ShapeDtypeStruct((half, width), jnp.bfloat16),
             jax.ShapeDtypeStruct((1, own), jnp.float32),
         ],
-        compiler_params=params(),
-    )(logits, teacher, exchange(stats, "vocab"))
-
-    below_low = along_z(low, 1, planes)
-    above_high = along_z(high, -1, planes)
-    below_high = along_z(high, 1, planes)
-    above_low = along_z(low, -1, planes)
-    far_below = along_z(below_low, 1, planes)
-    far_above = along_z(above_high, -1, planes)
-    near_pieces = [below_high, above_low, below_low, above_high, low, high]
+        scratch_shapes=[pltpu.VMEM((own, 128), jnp.float32)],
+        compiler_params=params(),
+    )(place, logits, teacher, exchange(stats, "vocab"))
+
+    one = shift(first, 1)
+    two = shift(second, -1)
+    three = shift(second, 1)
+    four = shift(first, -1)
+    far_one = shift(one, 1)
+    far_two = shift(two, -1)
+    near_pieces = [three, four, one, two, first, second]
     near = hidden_grads(place, head_weight, near_pieces, vocabs // 2, rows)
     keep, send = hidden_grads(
-        place, head_weight, [far_below, far_above], vocabs // 2, rows, near
+        place, head_weight, [far_one, far_two], vocabs // 2, rows, near
     )
     other = lax.ppermute(send, "vocab", other_core)
     parts = exchange(keep + other, "vocab", axis_index_groups=groups)

time: 181 us -> 179 us (0.989)
  waiting for transfers between devices: 8.45 us -> 5.98 us
    ppermute x12, waiting for transfers between devices: 3.95 us -> 1.84 us  [along_z(): return lax.ppermute(value, ('sect', 'tok', 'vocab'), pairs)]
  transfers between devices with their start and end apart: 14 -> 14, of which waited for: 5 -> 4; matrix products, arithmetic and copies ran while one was open for 0% -> 0% of each run, Pallas kernels for 5% -> 4%
where the time goes in v6:
time: 179 us; the launch traced here: 176 us
  blocking collectives  107 us (60%)
  starting transfers between devices  43.4 us (24%)
  Pallas kernels  17.4 us (10%)
  waiting for transfers between devices  5.98 us (3%)
    all_to_all x6, blocking collectives, exchange(): lax.all_to_all(value, axis, split_axis=0, concat_axis=0, tiled=True, **gr...  107 us
    ppermute x12, starting transfers between devices, along_z(): return lax.ppermute(value, ('sect', 'tok', 'vocab'), pairs)  38.8 us
    pallas_call x2, Pallas kernels, partial_logits(): pl.pallas_call(functools.partial(logits_kernel, first), grid=(width // ti...  6.09 us
    pallas_call x2, Pallas kernels, hidden_grads(): pl.pallas_call(functools.partial(hidden_kernel, len(earlier)), grid=(step...  5.54 us
  transfers between devices with their start and end apart: 14, of which 4 were waited for; matrix products, arithmetic and copies ran while one was open for 0% of the time, Pallas kernels for 4%

profile of v6, /device:TPU:6, one launch (start us, length us, event | category | flops | bytes accessed | tf_op | source)
XLA Modules:
  0.0 176.2 jit_solution(15532373554243845577)
XLA Ops:
  0.6 0.1 pad_add_fusion.place_ref
  0.7 0.0 copy-start.1
  0.7 0.8 copy-done.1
  1.5 0.8 shard_map.59
  2.2 27.6 %all_to_all.30.got_ref = bf16[4,32,128]{2,1,0:T(8,128)(2,1)S(1)} all-to-all(bf16[4,32,128]{2,1,0:T(8,128)(2,1)S(1)} %shard_map.59), channel_id=1, replica_groups=mesh['sect'=4,'tok'=4,'vocab'=32] {'sect'}, dimensions={0} | all-to-all | bytes 65536 | tf_op jit(solution)/shard_map/all_to_all | solution.py:33
  29.9 0.0 copy-start
  29.9 0.2 shard_map.60
  30.1 15.1 %all_to_all.31.mine_ref = bf16[16,32,512]{2,1,0:T(8,128)(2,1)S(1)} all-to-all(bf16[16,32,512]{2,1,0:T(8,128)(2,1)S(1)} %shard_map.60), channel_id=1, replica_groups={{0,2,4,6,8,10,12,14,16,18,20,22,24,26,28,30},{1,3,5,7,9,11,13,15,17,19,..., dimensions={0} | all-to-all | bytes 1048576 | tf_op jit(solution)/shard_map/all_to_all | solution.py:33
  45.3 1.9 %collective-permute-start = (bf16[16,32,512]{2,1,0:T(8,128)(2,1)S(1)}, bf16[16,32,512]{2,1,0:T(8,128)(2,1)S(1)}, u32[]{:S(2)}, u32[]{:S(2)}) collective-permute-start(bf16[16,32,512]{2,1,0:T(8,128)(2,1)S(1)} %all_to_all.31.mine_ref), channel_id=1, source_target_pairs={{0,1},{1,0},{2,3},{3,2},{4,5},{5,4},{6,7},{7,6},{8,9},{9,8},{10,11... | collective-permute-start | bytes 1572872 | tf_op jit(solution)/shard_map/ppermute | solution.py:383
  47.2 1.9 %collective-permute-done.other_ref = bf16[16,32,512]{2,1,0:T(8,128)(2,1)S(1)} collective-permute-done((bf16[16,32,512]{2,1,0:T(8,128)(2,1)S(1)}, bf16[16,32,512]{2,1,0:T(8,128)(2,1)S(1)}, u32[]{:S(2)}, u32[]{:S(2)}) %collective-permute-start) | collective-permute-done | bytes 524320 | tf_op jit(solution)/shard_map/ppermute | solution.py:383
  49.1 0.0 copy-done
  49.1 2.4 %shard_map.62 = (f32[64,2048]{1,0:T(8,128)S(1)}, f32[64,2048]{1,0:T(8,128)S(1)}) custom-call(s32[3]{0:T(128)S(1)} %pad_add_fusion.place_ref, bf16[16,32,512]{2,1,0:T(8,128)(2,1)S(1)} %all_to_all.31.mine_ref, bf16[16,32,512]{2,1,0:T(8,128)(2,1)S(1)} %collective-permute-done.other_ref, bf16[1024,2048]{1,0:T(8,128)(2,1)S(1)} %copy-done), custom_call_target="tpu_custom_call" | custom-call | flops 536870912 | bytes 5505024 | tf_op jit(solution)/shard_map/pallas_call | solution.py:157
  51.4 1.9 %collective-permute-start.1 = (f32[64,2048]{1,0:T(8,128)S(1)}, f32[64,2048]{1,0:T(8,128)S(1)}, u32[]{:S(2)}, u32[]{:S(2)}) collective-permute-start(f32[64,2048]{1,0:T(8,128)S(1)} %get-tuple-element.24), channel_id=1, source_target_pairs={{0,480},{1,33},{2,482},{3,35},{4,484},{5,37},{6,486},{7,39},{8,488... | collective-permute-start | bytes 1572872 | tf_op jit(solution)/shard_map/ppermute | solution.py:23
  53.4 0.0 copy-start.3
  53.4 0.0 copy-start.2
  53.4 4.1 %collective-permute-start.5 = (f32[64,2048]{1,0:T(8,128)S(1)}, f32[64,2048]{1,0:T(8,128)S(1)}, u32[]{:S(2)}, u32[]{:S(2)}) collective-permute-start(f32[64,2048]{1,0:T(8,128)S(1)} %get-tuple-element.28), channel_id=1, source_target_pairs={{0,32},{1,481},{2,34},{3,483},{4,36},{5,485},{6,38},{7,487},{8,40}... | collective-permute-start | bytes 1572872 | tf_op jit(solution)/shard_map/ppermute | solution.py:23
  57.5 3.7 %shard_map.61 = (f32[64,2048]{1,0:T(8,128)S(1)}, f32[64,2048]{1,0:T(8,128)S(1)}, f32[64,2048]{1,0:T(8,128)S(1)}, f32[64,2048]{1,0:T(8,128)S(1)}, f32[128,2048]{1,0:T(8,128)S(1)}) custom-call(s32[3]{0:T(128)S(1)} %pad_add_fusion.place_ref, bf16[16,32,512]{2,1,0:T(8,128)(2,1)S(1)} %all_to_all.31.mine_ref, ...), custom_call_target="tpu_custom_call" | custom-call | flops 1610612736 | bytes 8126464 | tf_op jit(solution)/shard_map/pallas_call | solution.py:157
  61.2 2.9 %collective-permute-start.3 = (f32[64,2048]{1,0:T(8,128)S(1)}, f32[64,2048]{1,0:T(8,128)S(1)}, u32[]{:S(2)}, u32[]{:S(2)}) collective-permute-start(f32[64,2048]{1,0:T(8,128)S(1)} %get-tuple-element.25), channel_id=1, source_target_pairs={{0,32},{1,481},{2,34},{3,483},{4,36},{5,485},{6,38},{7,487},{8,40}... | collective-permute-start | bytes 1572872 | tf_op jit(solution)/shard_map/ppermute | solution.py:23
  64.0 4.2 %collective-permute-start.4 = (f32[64,2048]{1,0:T(8,128)S(1)}, f32[64,2048]{1,0:T(8,128)S(1)}, u32[]{:S(2)}, u32[]{:S(2)}) collective-permute-start(f32[64,2048]{1,0:T(8,128)S(1)} %get-tuple-element.26), channel_id=1, source_target_pairs={{0,480},{1,33},{2,482},{3,35},{4,484},{5,37},{6,486},{7,39},{8,488... | collective-permute-start | bytes 1572872 | tf_op jit(solution)/shard_map/ppermute | solution.py:23
  68.3 0.0 collective-permute-done.1.far_ref
  68.3 0.1 shard_map.63
  68.3 1.9 %collective-permute-start.2 = (f32[64,2048]{1,0:T(8,128)S(1)}, f32[64,2048]{1,0:T(8,128)S(1)}, u32[]{:S(2)}, u32[]{:S(2)}) collective-permute-start(f32[64,2048]{1,0:T(8,128)S(1)} %shard_map.63), channel_id=1, source_target_pairs={{0,480},{1,33},{2,482},{3,35},{4,484},{5,37},{6,486},{7,39},{8,488... | collective-permute-start | bytes 1572872 | tf_op jit(solution)/shard_map/ppermute | solution.py:23
  70.3 0.0 collective-permute-done.5.far_ref
  70.3 0.1 shard_map.64
  70.4 3.9 %collective-permute-start.6 = (f32[64,2048]{1,0:T(8,128)S(1)}, f32[64,2048]{1,0:T(8,128)S(1)}, u32[]{:S(2)}, u32[]{:S(2)}) collective-permute-start(f32[64,2048]{1,0:T(8,128)S(1)} %shard_map.64), channel_id=1, source_target_pairs={{0,32},{1,481},{2,34},{3,483},{4,36},{5,485},{6,38},{7,487},{8,40}... | collective-permute-start | bytes 1572872 | tf_op jit(solution)/shard_map/ppermute | solution.py:23
  74.3 0.0 copy-done.3
  74.3 15.1 %all_to_all.32 = bf16[32,4,2048]{2,1,0:T(4,128)(2,1)S(1)} all-to-all(bf16[32,4,2048]{2,1,0:T(4,128)(2,1)S(1)} %bitcast.14), channel_id=1, replica_groups=mesh['sect'=4,'tok'=4,'vocab'=32] {'vocab'}, dimensions={0} | all-to-all | bytes 1048576 | tf_op jit(solution)/shard_map/all_to_all | solution.py:33
  89.4 0.3 copy.8
  89.7 0.0 collective-permute-done.3.near_second
  89.7 0.0 collective-permute-done.4.near_first
  89.7 0.9 collective-permute-done.2.next_first
  90.6 0.0 collective-permute-done.6.next_second
  90.6 0.0 copy-done.2
  90.6 1.5 shard_map.65
  92.1 11.8 %all_to_all.33.stats_ref = f32[32,8,128]{2,1,0:T(8,128)S(1)} all-to-all(f32[32,8,128]{2,1,0:T(8,128)S(1)} %get-tuple-element.32), channel_id=1, replica_groups=mesh['sect'=4,'tok'=4,'vocab'=32] {'vocab'}, dimensions={0} | all-to-all | bytes 262144 | tf_op jit(solution)/shard_map/all_to_all | solution.py:33
  103.9 1.1 shard_map.66
  105.0 2.8 %collective-permute-start.7 = (bf16[64,2048]{1,0:T(8,128)(2,1)S(1)}, bf16[64,2048]{1,0:T(8,128)(2,1)S(1)}, u32[]{:S(2)}, u32[]{:S(2)}) collective-permute-start(bf16[64,2048]{1,0:T(8,128)(2,1)S(1)} %get-tuple-element.33.refs_4_), channel_id=1, source_target_pairs={{0,32},{1,481},{2,34},{3,483},{4,36},{5,485},{6,38},{7,487},{8,40}... | collective-permute-start | bytes 786440 | tf_op jit(solution)/shard_map/ppermute | solution.py:23
  107.8 4.3 %collective-permute-start.9 = (bf16[64,2048]{1,0:T(8,128)(2,1)S(1)}, bf16[64,2048]{1,0:T(8,128)(2,1)S(1)}, u32[]{:S(2)}, u32[]{:S(2)}) collective-permute-start(bf16[64,2048]{1,0:T(8,128)(2,1)S(1)} %get-tuple-element.34.refs_5_), channel_id=1, source_target_pairs={{0,480},{1,33},{2,482},{3,35},{4,484},{5,37},{6,486},{7,39},{8,488... | collective-permute-start | bytes 786440 | tf_op jit(solution)/shard_map/ppermute | solution.py:23
  112.1 1.9 %collective-permute-start.12 = (bf16[64,2048]{1,0:T(8,128)(2,1)S(1)}, bf16[64,2048]{1,0:T(8,128)(2,1)S(1)}, u32[]{:S(2)}, u32[]{:S(2)}) collective-permute-start(bf16[64,2048]{1,0:T(8,128)(2,1)S(1)} %get-tuple-element.33.refs_4_), channel_id=1, source_target_pairs={{0,480},{1,33},{2,482},{3,35},{4,484},{5,37},{6,486},{7,39},{8,488... | collective-permute-start | bytes 786440 | tf_op jit(solution)/shard_map/ppermute | solution.py:23
  114.0 3.9 %collective-permute-start.11 = (bf16[64,2048]{1,0:T(8,128)(2,1)S(1)}, bf16[64,2048]{1,0:T(8,128)(2,1)S(1)}, u32[]{:S(2)}, u32[]{:S(2)}) collective-permute-start(bf16[64,2048]{1,0:T(8,128)(2,1)S(1)} %get-tuple-element.34.refs_5_), channel_id=1, source_target_pairs={{0,32},{1,481},{2,34},{3,483},{4,36},{5,485},{6,38},{7,487},{8,40}... | collective-permute-start | bytes 786440 | tf_op jit(solution)/shard_map/ppermute | solution.py:23
  118.0 0.0 collective-permute-done.7.refs_2_
  118.0 1.9 %collective-permute-start.8 = (bf16[64,2048]{1,0:T(8,128)(2,1)S(1)}, bf16[64,2048]{1,0:T(8,128)(2,1)S(1)}, u32[]{:S(2)}, u32[]{:S(2)}) collective-permute-start(bf16[64,2048]{1,0:T(8,128)(2,1)S(1)} %collective-permute-done.7.refs_2_), channel_id=1, source_target_pairs={{0,32},{1,481},{2,34},{3,483},{4,36},{5,485},{6,38},{7,487},{8,40}... | collective-permute-start | bytes 786440 | tf_op jit(solution)/shard_map/ppermute | solution.py:23
  119.9 0.0 collective-permute-done.9.refs_3_
  119.9 5.1 %collective-permute-start.10 = (bf16[64,2048]{1,0:T(8,128)(2,1)S(1)}, bf16[64,2048]{1,0:T(8,128)(2,1)S(1)}, u32[]{:S(2)}, u32[]{:S(2)}) collective-permute-start(bf16[64,2048]{1,0:T(8,128)(2,1)S(1)} %collective-permute-done.9.refs_3_), channel_id=1, source_target_pairs={{0,480},{1,33},{2,482},{3,35},{4,484},{5,37},{6,486},{7,39},{8,488... | collective-permute-start | bytes 786440 | tf_op jit(solution)/shard_map/ppermute | solution.py:23
  125.0 0.0 collective-permute-done.12.refs_1_
  125.1 0.0 collective-permute-done.11.refs_0_
  125.1 3.4 %shard_map.67 = (f32[16,32,512]{2,1,0:T(8,128)S(1)}, f32[16,32,512]{2,1,0:T(8,128)S(1)}) custom-call(s32[3]{0:T(128)S(1)} %pad_add_fusion.place_ref, bf16[1024,2048]{1,0:T(8,128)(2,1)S(1)} %copy-done, bf16[64,2048]{1,0:T(8,128)(2,1)S(1)} %collective-permute-done.11.refs_0_, bf16[64,2048]{1,0:T(8,128)(2,1)S(1)} %collective-permute-done.12.refs_1_, ...), custom_call_target="tpu_custom_call" | custom-call | flops 1610612736 | bytes 7340032 | tf_op jit(solution)/shard_map/pallas_call | solution.py:284
  128.5 0.9 collective-permute-done.8.refs_0_
  129.4 0.0 collective-permute-done.10.refs_1_
  129.4 2.1 %shard_map.68 = (f32[16,32,512]{2,1,0:T(8,128)S(1)}, f32[16,32,512]{2,1,0:T(8,128)S(1)}) custom-call(s32[3]{0:T(128)S(1)} %pad_add_fusion.place_ref, bf16[1024,2048]{1,0:T(8,128)(2,1)S(1)} %copy-done, bf16[64,2048]{1,0:T(8,128)(2,1)S(1)} %collective-permute-done.8.refs_0_, ...), custom_call_target="tpu_custom_call", output_to_operand_aliasing={{0}: (4, {}), {1}: (5, {})} | custom-call | flops 536870912 | bytes 5242880 | tf_op jit(solution)/shard_map/pallas_call | solution.py:284
  131.5 2.6 %collective-permute-start.13 = (f32[16,32,512]{2,1,0:T(8,128)S(1)}, f32[16,32,512]{2,1,0:T(8,128)S(1)}, u32[]{:S(2)}, u32[]{:S(2)}) collective-permute-start(f32[16,32,512]{2,1,0:T(8,128)S(1)} %get-tuple-element.38), channel_id=1, source_target_pairs={{0,1},{1,0},{2,3},{3,2},{4,5},{5,4},{6,7},{7,6},{8,9},{9,8},{10,11... | collective-permute-start | bytes 3145736 | tf_op jit(solution)/shard_map/ppermute | solution.py:444
  134.2 2.3 %collective-permute-done.13 = f32[16,32,512]{2,1,0:T(8,128)S(1)} collective-permute-done((f32[16,32,512]{2,1,0:T(8,128)S(1)}, f32[16,32,512]{2,1,0:T(8,128)S(1)}, u32[]{:S(2)}, u32[]{:S(2)}) %collective-permute-start.13) | collective-permute-done | bytes 1048608 | tf_op jit(solution)/shard_map/ppermute | solution.py:444
  136.4 0.2 add.3
  136.6 20.2 %all_to_all.34.parts_ref = f32[16,32,512]{2,1,0:T(8,128)S(1)} all-to-all(f32[16,32,512]{2,1,0:T(8,128)S(1)} %add.3), channel_id=1, replica_groups={{0,2,4,6,8,10,12,14,16,18,20,22,24,26,28,30},{1,3,5,7,9,11,13,15,17,19,..., dimensions={0} | all-to-all | bytes 2097152 | tf_op jit(solution)/shard_map/all_to_all | solution.py:33
  156.9 0.7 shard_map.69
  157.6 17.3 %all_to_all.35.got_ref = f32[4,40,128]{2,1,0:T(8,128)S(1)} all-to-all(f32[4,40,128]{2,1,0:T(8,128)S(1)} %shard_map.69), channel_id=1, replica_groups=mesh['sect'=4,'tok'=4,'vocab'=32] {'sect'}, dimensions={0} | all-to-all | bytes 163840 | tf_op jit(solution)/shard_map/all_to_all | solution.py:33
  174.9 1.3 shard_map.70
Async XLA Ops:
  0.7 0.8 copy-start.1
  29.9 19.2 %copy-start = (bf16[1024,2048]{1,0:T(8,128)(2,1)S(1)}, bf16[1024,2048]{1,0:T(8,128)(2,1)}, u32[]{:S(2)}) copy-start(bf16[1024,2048]{1,0:T(8,128)(2,1)} %w_ref.7) | copy-start | bytes 12582916
  45.3 3.8 %collective-permute-start = (bf16[16,32,512]{2,1,0:T(8,128)(2,1)S(1)}, bf16[16,32,512]{2,1,0:T(8,128)(2,1)S(1)}, u32[]{:S(2)}, u32[]{:S(2)}) collective-permute-start(bf16[16,32,512]{2,1,0:T(8,128)(2,1)S(1)} %all_to_all.31.mine_ref), channel_id=1, source_target_pairs={{0,1},{1,0},{2,3},{3,2},{4,5},{5,4},{6,7},{7,6},{8,9},{9,8},{10,11... | collective-permute-start | bytes 1572872 | tf_op jit(solution)/shard_map/ppermute | solution.py:383
  51.4 16.8 %collective-permute-start.1 = (f32[64,2048]{1,0:T(8,128)S(1)}, f32[64,2048]{1,0:T(8,128)S(1)}, u32[]{:S(2)}, u32[]{:S(2)}) collective-permute-start(f32[64,2048]{1,0:T(8,128)S(1)} %get-tuple-element.24), channel_id=1, source_target_pairs={{0,480},{1,33},{2,482},{3,35},{4,484},{5,37},{6,486},{7,39},{8,488... | collective-permute-start | bytes 1572872 | tf_op jit(solution)/shard_map/ppermute | solution.py:23
  53.4 20.9 %copy-start.3 = (bf16[4,65536]{1,0:T(4,128)(2,1)S(1)}, bf16[4,65536]{1,0:T(4,128)(2,1)}, u32[]{:S(2)}) copy-start(bf16[4,65536]{1,0:T(4,128)(2,1)} %param.6) | copy-start | bytes 1572868
  53.4 37.2 %copy-start.2 = (s32[4,4]{1,0:T(4,128)S(1)}, s32[4,4]{1,0:T(4,128)}, u32[]{:S(2)}) copy-start(s32[4,4]{1,0:T(4,128)} %pairing_ref.1) | copy-start | bytes 196
  53.4 16.9 %collective-permute-start.5 = (f32[64,2048]{1,0:T(8,128)S(1)}, f32[64,2048]{1,0:T(8,128)S(1)}, u32[]{:S(2)}, u32[]{:S(2)}) collective-permute-start(f32[64,2048]{1,0:T(8,128)S(1)} %get-tuple-element.28), channel_id=1, source_target_pairs={{0,32},{1,481},{2,34},{3,483},{4,36},{5,485},{6,38},{7,487},{8,40}... | collective-permute-start | bytes 1572872 | tf_op jit(solution)/shard_map/ppermute | solution.py:23
  61.2 28.5 %collective-permute-start.3 = (f32[64,2048]{1,0:T(8,128)S(1)}, f32[64,2048]{1,0:T(8,128)S(1)}, u32[]{:S(2)}, u32[]{:S(2)}) collective-permute-start(f32[64,2048]{1,0:T(8,128)S(1)} %get-tuple-element.25), channel_id=1, source_target_pairs={{0,32},{1,481},{2,34},{3,483},{4,36},{5,485},{6,38},{7,487},{8,40}... | collective-permute-start | bytes 1572872 | tf_op jit(solution)/shard_map/ppermute | solution.py:23
  64.0 25.6 %collective-permute-start.4 = (f32[64,2048]{1,0:T(8,128)S(1)}, f32[64,2048]{1,0:T(8,128)S(1)}, u32[]{:S(2)}, u32[]{:S(2)}) collective-permute-start(f32[64,2048]{1,0:T(8,128)S(1)} %get-tuple-element.26), channel_id=1, source_target_pairs={{0,480},{1,33},{2,482},{3,35},{4,484},{5,37},{6,486},{7,39},{8,488... | collective-permute-start | bytes 1572872 | tf_op jit(solution)/shard_map/ppermute | solution.py:23
  68.3 22.3 %collective-permute-start.2 = (f32[64,2048]{1,0:T(8,128)S(1)}, f32[64,2048]{1,0:T(8,128)S(1)}, u32[]{:S(2)}, u32[]{:S(2)}) collective-permute-start(f32[64,2048]{1,0:T(8,128)S(1)} %shard_map.63), channel_id=1, source_target_pairs={{0,480},{1,33},{2,482},{3,35},{4,484},{5,37},{6,486},{7,39},{8,488... | collective-permute-start | bytes 1572872 | tf_op jit(solution)/shard_map/ppermute | solution.py:23
  70.4 20.3 %collective-permute-start.6 = (f32[64,2048]{1,0:T(8,128)S(1)}, f32[64,2048]{1,0:T(8,128)S(1)}, u32[]{:S(2)}, u32[]{:S(2)}) collective-permute-start(f32[64,2048]{1,0:T(8,128)S(1)} %shard_map.64), channel_id=1, source_target_pairs={{0,32},{1,481},{2,34},{3,483},{4,36},{5,485},{6,38},{7,487},{8,40}... | collective-permute-start | bytes 1572872 | tf_op jit(solution)/shard_map/ppermute | solution.py:23
  105.0 12.9 %collective-permute-start.7 = (bf16[64,2048]{1,0:T(8,128)(2,1)S(1)}, bf16[64,2048]{1,0:T(8,128)(2,1)S(1)}, u32[]{:S(2)}, u32[]{:S(2)}) collective-permute-start(bf16[64,2048]{1,0:T(8,128)(2,1)S(1)} %get-tuple-element.33.refs_4_), channel_id=1, source_target_pairs={{0,32},{1,481},{2,34},{3,483},{4,36},{5,485},{6,38},{7,487},{8,40}... | collective-permute-start | bytes 786440 | tf_op jit(solution)/shard_map/ppermute | solution.py:23
  107.8 12.1 %collective-permute-start.9 = (bf16[64,2048]{1,0:T(8,128)(2,1)S(1)}, bf16[64,2048]{1,0:T(8,128)(2,1)S(1)}, u32[]{:S(2)}, u32[]{:S(2)}) collective-permute-start(bf16[64,2048]{1,0:T(8,128)(2,1)S(1)} %get-tuple-element.34.refs_5_), channel_id=1, source_target_pairs={{0,480},{1,33},{2,482},{3,35},{4,484},{5,37},{6,486},{7,39},{8,488... | collective-permute-start | bytes 786440 | tf_op jit(solution)/shard_map/ppermute | solution.py:23
  112.1 13.0 %collective-permute-start.12 = (bf16[64,2048]{1,0:T(8,128)(2,1)S(1)}, bf16[64,2048]{1,0:T(8,128)(2,1)S(1)}, u32[]{:S(2)}, u32[]{:S(2)}) collective-permute-start(bf16[64,2048]{1,0:T(8,128)(2,1)S(1)} %get-tuple-element.33.refs_4_), channel_id=1, source_target_pairs={{0,480},{1,33},{2,482},{3,35},{4,484},{5,37},{6,486},{7,39},{8,488... | collective-permute-start | bytes 786440 | tf_op jit(solution)/shard_map/ppermute | solution.py:23
  114.0 11.0 %collective-permute-start.11 = (bf16[64,2048]{1,0:T(8,128)(2,1)S(1)}, bf16[64,2048]{1,0:T(8,128)(2,1)S(1)}, u32[]{:S(2)}, u32[]{:S(2)}) collective-permute-start(bf16[64,2048]{1,0:T(8,128)(2,1)S(1)} %get-tuple-element.34.refs_5_), channel_id=1, source_target_pairs={{0,32},{1,481},{2,34},{3,483},{4,36},{5,485},{6,38},{7,487},{8,40}... | collective-permute-start | bytes 786440 | tf_op jit(solution)/shard_map/ppermute | solution.py:23
  118.0 11.4 %collective-permute-start.8 = (bf16[64,2048]{1,0:T(8,128)(2,1)S(1)}, bf16[64,2048]{1,0:T(8,128)(2,1)S(1)}, u32[]{:S(2)}, u32[]{:S(2)}) collective-permute-start(bf16[64,2048]{1,0:T(8,128)(2,1)S(1)} %collective-permute-done.7.refs_2_), channel_id=1, source_target_pairs={{0,32},{1,481},{2,34},{3,483},{4,36},{5,485},{6,38},{7,487},{8,40}... | collective-permute-start | bytes 786440 | tf_op jit(solution)/shard_map/ppermute | solution.py:23
  119.9 9.5 %collective-permute-start.10 = (bf16[64,2048]{1,0:T(8,128)(2,1)S(1)}, bf16[64,2048]{1,0:T(8,128)(2,1)S(1)}, u32[]{:S(2)}, u32[]{:S(2)}) collective-permute-start(bf16[64,2048]{1,0:T(8,128)(2,1)S(1)} %collective-permute-done.9.refs_3_), channel_id=1, source_target_pairs={{0,480},{1,33},{2,482},{3,35},{4,484},{5,37},{6,486},{7,39},{8,488... | collective-permute-start | bytes 786440 | tf_op jit(solution)/shard_map/ppermute | solution.py:23
  131.5 4.9 %collective-permute-start.13 = (f32[16,32,512]{2,1,0:T(8,128)S(1)}, f32[16,32,512]{2,1,0:T(8,128)S(1)}, u32[]{:S(2)}, u32[]{:S(2)}) collective-permute-start(f32[16,32,512]{2,1,0:T(8,128)S(1)} %get-tuple-element.38), channel_id=1, source_target_pairs={{0,1},{1,0},{2,3},{3,2},{4,5},{5,4},{6,7},{7,6},{8,9},{9,8},{10,11... | collective-permute-start | bytes 3145736 | tf_op jit(solution)/shard_map/ppermute | solution.py:444

commit v7 on v6

--- a/solution.py
+++ b/solution.py
@@ -9,7 +9,6 @@
 
 loss_scale = 16.0
 VMEM_BYTES = 24 * 1024 * 1024
-SMEM = pl.BlockSpec(memory_space=pltpu.SMEM)
 VMEM = pl.BlockSpec(memory_space=pltpu.VMEM)
 ANYWHERE = pl.BlockSpec(memory_space=pl.ANY)
 
@@ -68,11 +67,11 @@
     return order + [(2, s) for s in low + high]
 
 
-def pick_kernel(place_ref, hidden_ref, picked_ref, *, toks):
+def pick_kernel(hidden_ref, picked_ref, *, toks):
     sections, _, own = picked_ref.shape
     rows = hidden_ref.shape[1]
     unit = own // 4
-    section, tok = place_ref[0], place_ref[1]
+    section, tok = lax.axis_index("sect"), lax.axis_index("tok")
     lane = lax.broadcasted_iota(jnp.int32, (rows, own), 1)
     row = lax.broadcasted_iota(jnp.int32, (rows, own), 0)
     for k in range(sections):
@@ -114,12 +113,12 @@
         spread_ref[k] = window
 
 
-def logits_kernel(first, place_ref, mine_ref, other_ref, w_ref, *refs):
+def logits_kernel(first, mine_ref, other_ref, w_ref, *refs):
     *outs, both, flipped = refs
 
     @pl.when(pl.program_id(0) == 0)
     def _():
-        core = remainder(place_ref[2], 2)
+        core = remainder(lax.axis_index("vocab"), 2)
 
         @pl.when(core == 0)
         def _():
@@ -149,7 +148,7 @@
         start += out.shape[0]
 
 
-def partial_logits(place, mine, other, head_weight, first, sizes):
+def partial_logits(mine, other, head_weight, first, sizes):
     feats, width = head_weight.shape
     tile = 512
     count = sum(sizes)
@@ -157,7 +156,7 @@
     return pl.pallas_call(
         functools.partial(logits_kernel, first),
         grid=(width // tile,),
-        in_specs=[SMEM, VMEM, VMEM, pl.BlockSpec((feats, tile), lambda i: (0, i))],
+        in_specs=[VMEM, VMEM, pl.BlockSpec((feats, tile), lambda i: (0, i))],
         out_specs=[pl.BlockSpec((size, tile), lambda i: (0, i)) for size in sizes],
         out_shape=[jax.ShapeDtypeStruct((size, width), jnp.float32) for size in sizes],
         scratch_shapes=[
@@ -168,7 +167,7 @@
         cost_estimate=cost(
             2 * count * feats * width, feats * width * 2 + count * (feats * 2 + width * 4)
         ),
-    )(place, mine, other, head_weight)
+    )(mine, other, head_weight)
 
 
 def add_kernel(mine_ref, far_ref, out_ref):
@@ -176,7 +175,6 @@
 
 
 def stats_kernel(
-    place_ref,
     pairing_ref,
     own_ref,
     next_first,
@@ -189,14 +187,25 @@
     stats_ref,
 ):
     half = next_first.shape[0]
-    one, two = halves(remainder(place_ref[2], 2), half)
+    one, two = halves(remainder(lax.axis_index("vocab"), 2), half)
     logits_ref[one] = own_ref[one] + next_first[...] + near_second[...]
     logits_ref[two] = own_ref[two] + near_first[...] + next_second[...]
     sections = pairing_ref.shape[0]
     unit = own_ref.shape[0] // sections
-    for k in range(sections):
-        begin = pl.multiple_of(pairing_ref[place_ref[0], k] * unit, unit)
-        sorted_ref[pl.ds(begin, unit)] = teacher_ref[k * unit : (k + 1) * unit]
+    row = lax.broadcasted_iota(jnp.int32, pairing_ref.shape, 0)
+    lane = lax.broadcasted_iota(jnp.int32, pairing_ref.shape, 1)
+    here = jnp.where(row == lax.axis_index("sect"), pairing_ref[...], 0)
+    paired = [
+        jnp.sum(jnp.where(lane == k, here, 0), axis=(0, 1), keepdims=True) for k in range(sections)
+    ]
+    blocks = [
+        teacher_ref[k * unit : (k + 1) * unit].astype(jnp.float32) for k in range(sections)
+    ]
+    for s in range(sections):
+        block = blocks[0]
+        for k in range(1, sections):
+            block = jnp.where(paired[k] == s, blocks[k], block)
+        sorted_ref[s * unit : (s + 1) * unit] = block.astype(jnp.bfloat16)
     logits = logits_ref[...]
     teacher = sorted_ref[...].astype(jnp.float32)
     top_s = jnp.max(logits, axis=1, keepdims=True)
@@ -216,7 +225,7 @@
 
 
 def grads_kernel(
-    place_ref, logits_ref, teacher_ref, stats_ref, first_ref, second_ref, div_ref, columns
+    logits_ref, teacher_ref, stats_ref, first_ref, second_ref, div_ref, columns
 ):
     stats = stats_ref[...]
     top = jnp.max(stats, axis=0)
@@ -233,7 +242,7 @@
     for place, values in enumerate((top_s, top_t, loss_scale / total_s, loss_scale / total_t)):
         packed = jnp.where(row == place, values, packed)
     columns[...] = packed.T
-    places = halves(remainder(place_ref[2], 2), half)
+    places = halves(remainder(lax.axis_index("vocab"), 2), half)
     for place, out_ref in zip(places, (first_ref, second_ref)):
         values = columns[place]
         out_ref[...] = (
@@ -242,7 +251,7 @@
         ).astype(jnp.bfloat16)
 
 
-def hidden_kernel(earlier, place_ref, w_ref, *refs):
+def hidden_kernel(earlier, w_ref, *refs):
     *pieces, keep_ref, send_ref, window = refs
     pieces = pieces[: len(pieces) - earlier]
 
@@ -251,7 +260,7 @@
         start = 0
         for one, two in zip(pieces[0::2], pieces[1::2]):
             half = one.shape[0]
-            low, high = halves(remainder(place_ref[2], 2), half, start)
+            low, high = halves(remainder(lax.axis_index("vocab"), 2), half, start)
             window[low] = one[...]
             window[high] = two[...]
             start += 2 * half
@@ -260,7 +269,7 @@
     result = lax.dot_general(
         w_ref[...], window[...], (((1,), (1,)), ((), ())), preferred_element_type=jnp.float32
     ).reshape(pairs, 2, feats, rows)
-    core = remainder(place_ref[2], 2)
+    core = remainder(lax.axis_index("vocab"), 2)
 
     @pl.when(core == 0)
     def _():
@@ -273,18 +282,18 @@
         send_ref[...] = result[:, 0]
 
 
-def hidden_grads(place, head_weight, pieces, pairs, total, earlier=()):
+def hidden_grads(head_weight, pieces, pairs, total, earlier=()):
     feats, width = head_weight.shape
     rows = sum(piece.shape[0] for piece in pieces)
     index = (total - rows) // rows if earlier else 0
     steps = 2
     shape = jax.ShapeDtypeStruct((pairs, feats // (2 * pairs), total), jnp.float32)
     block = pl.BlockSpec((pairs // steps, shape.shape[1], rows), lambda i: (i, 0, index))
-    inputs = 2 + len(pieces)
+    inputs = 1 + len(pieces)
     return pl.pallas_call(
         functools.partial(hidden_kernel, len(earlier)),
         grid=(steps,),
-        in_specs=[SMEM, pl.BlockSpec((feats // steps, width), lambda i: (i, 0))]
+        in_specs=[pl.BlockSpec((feats // steps, width), lambda i: (i, 0))]
         + [VMEM] * len(pieces)
         + [ANYWHERE] * len(earlier),
         out_specs=[block, block],
@@ -295,10 +304,10 @@
         cost_estimate=cost(
             2 * rows * feats * width, feats * width * 2 + rows * width * 2 + rows * feats * 4
         ),
-    )(place, head_weight, *pieces, *earlier)
-
-
-def regroup_kernel(place_ref, parts_ref, div_ref, out_ref):
+    )(head_weight, *pieces, *earlier)
+
+
+def regroup_kernel(parts_ref, div_ref, out_ref):
     sections, height, own = out_ref.shape
     _, feats, _ = parts_ref.shape
     unit = own // 4
@@ -316,7 +325,7 @@
             )
             out = jnp.where((lane >= piece * unit) & (lane < (piece + 1) * unit), turned, out)
         out_ref[s, :feats] = out
-    section = place_ref[0]
+    section = lax.axis_index("sect")
     values = jnp.broadcast_to(div_ref[...], (height - feats, own))
     small = lane[: height - feats]
     for s in range(sections):
@@ -328,7 +337,7 @@
         out_ref[s, feats:] = out
 
 
-def return_kernel(place_ref, got_ref, grads_ref, div_ref, *, toks):
+def return_kernel(got_ref, grads_ref, div_ref, *, toks):
     sections, _, own = got_ref.shape
     unit = own // 4
     feats, rows = grads_ref.shape
@@ -338,7 +347,7 @@
         values = got_ref[sender, :feats]
         for piece in range(4):
             block = window_block(
-                jnp.int32(sender), place_ref[1], place_ref[0], piece, sections, toks
+                jnp.int32(sender), lax.axis_index("tok"), lax.axis_index("sect"), piece, sections, toks
             )
             begin = remainder(block, 4) * unit
             turned = pltpu.roll(values, remainder(begin - piece * unit + own, own), 1)
@@ -360,15 +369,14 @@
     rows, feats = hidden.shape
     own = rows // toks
     half = own // 2
-    place = jnp.stack([lax.axis_index(name) for name in ("sect", "tok", "vocab")])
 
     picked = pl.pallas_call(
         functools.partial(pick_kernel, toks=toks),
-        in_specs=[SMEM, VMEM],
+        in_specs=[VMEM],
         out_specs=VMEM,
         out_shape=jax.ShapeDtypeStruct((sections, feats, own), jnp.bfloat16),
         compiler_params=params(),
-    )(place, hidden.T)
+    )(hidden.T)
     spread = pl.pallas_call(
         arrange_kernel,
         in_specs=[VMEM],
@@ -383,11 +391,11 @@
     other = lax.ppermute(mine, "vocab", other_core)
 
     shift = functools.partial(along_z, planes=planes, vocabs=vocabs)
-    edge_first, edge_second = partial_logits(place, mine, other, head_weight, 0, [half, half])
+    edge_first, edge_second = partial_logits(mine, other, head_weight, 0, [half, half])
     far_first = shift(edge_first, -1)
     far_second = shift(edge_second, 1)
     near_first, near_second, next_first, next_second, kept = partial_logits(
-        place, mine, other, head_weight, own, [half, half, half, half, own]
+        mine, other, head_weight, own, [half, half, half, half, own]
     )
     near_first = shift(near_first, -1)
     near_second = shift(near_second, 1)
@@ -408,7 +416,7 @@
 
     logits, teacher, stats = pl.pallas_call(
         stats_kernel,
-        in_specs=[SMEM, SMEM] + [VMEM] * 6,
+        in_specs=[VMEM] * 7,
         out_specs=[VMEM] * 3,
         out_shape=[
             jax.ShapeDtypeStruct((own, width), jnp.float32),
@@ -416,10 +424,10 @@
             jax.ShapeDtypeStruct((vocabs, 8, own), jnp.float32),
         ],
         compiler_params=params(),
-    )(place, pairing, kept, next_first, near_second, near_first, next_second, teacher)
+    )(pairing, kept, next_first, near_second, near_first, next_second, teacher)
     first, second, diverge = pl.pallas_call(
         grads_kernel,
-        in_specs=[SMEM] + [VMEM] * 3,
+        in_specs=[VMEM] * 3,
         out_specs=[VMEM] * 3,
         out_shape=[
             jax.ShapeDtypeStruct((half, width), jnp.bfloat16),
@@ -428,7 +436,7 @@
         ],
         scratch_shapes=[pltpu.VMEM((own, 128), jnp.float32)],
         compiler_params=params(),
-    )(place, logits, teacher, exchange(stats, "vocab"))
+    )(logits, teacher, exchange(stats, "vocab"))
 
     one = shift(first, 1)
     two = shift(second, -1)
@@ -437,30 +445,30 @@
     far_one = shift(one, 1)
     far_two = shift(two, -1)
     near_pieces = [three, four, one, two, first, second]
-    near = hidden_grads(place, head_weight, near_pieces, vocabs // 2, rows)
+    near = hidden_grads(head_weight, near_pieces, vocabs // 2, rows)
     keep, send = hidden_grads(
-        place, head_weight, [far_one, far_two], vocabs // 2, rows, near
+        head_weight, [far_one, far_two], vocabs // 2, rows, near
     )
     other = lax.ppermute(send, "vocab", other_core)
     parts = exchange(keep + other, "vocab", axis_index_groups=groups)
 
     regrouped = pl.pallas_call(
         regroup_kernel,
-        in_specs=[SMEM, VMEM, VMEM],
+        in_specs=[VMEM, VMEM],
         out_specs=VMEM,
         out_shape=jax.ShapeDtypeStruct((sections, feats + 8, own), jnp.float32),
         compiler_params=params(),
-    )(place, parts, diverge)
+    )(parts, diverge)
     grads, div = pl.pallas_call(
         functools.partial(return_kernel, toks=toks),
-        in_specs=[SMEM, VMEM],
+        in_specs=[VMEM],
         out_specs=[VMEM, VMEM],
         out_shape=[
             jax.ShapeDtypeStruct((feats, rows), jnp.float32),
             jax.ShapeDtypeStruct((1, own), jnp.float32),
         ],
         compiler_params=params(),
-    )(place, exchange(regrouped, "sect"))
+    )(exchange(regrouped, "sect"))
     return grads.T, div.reshape(own)
 
 

time: 179 us -> 175 us (0.978)
  Pallas kernels: 17.4 us -> 12.8 us
    pallas_call x5, Pallas kernels: 5.36 us -> 2.86 us  [the longest x1 1.12 us: shards(): pl.pallas_call(stats_kernel, in_specs=[VMEM] * 7, out_specs=[VMEM] * 3, o...]
where the time goes in v7:
time: 175 us; the launch traced here: 173 us
  blocking collectives  107 us (61%)
  starting transfers between devices  43.3 us (25%)
  Pallas kernels  12.8 us (7%)
  waiting for transfers between devices  7.01 us (4%)
    all_to_all x6, blocking collectives, exchange(): lax.all_to_all(value, axis, split_axis=0, concat_axis=0, tiled=True, **gr...  107 us
    ppermute x12, starting transfers between devices, along_z(): return lax.ppermute(value, ('sect', 'tok', 'vocab'), pairs)  38.8 us
    pallas_call x2, Pallas kernels, partial_logits(): pl.pallas_call(functools.partial(logits_kernel, first), grid=(width // ti...  5.12 us
    pallas_call x2, Pallas kernels, hidden_grads(): pl.pallas_call(functools.partial(hidden_kernel, len(earlier)), grid=(step...  4.41 us
  transfers between devices with their start and end apart: 14, of which 4 were waited for; matrix products, arithmetic and copies ran while one was open for 0% of the time, Pallas kernels for 4%

profile of v7, /device:TPU:6, one launch (start us, length us, event | category | flops | bytes accessed | tf_op | source)
XLA Modules:
  0.0 172.6 jit_solution(6830898481219396353)
XLA Ops:
  0.6 0.0 copy-start.1
  0.6 0.7 copy-done.1
  1.4 0.2 shard_map.59
  1.6 27.6 %all_to_all.30.got_ref = bf16[4,32,128]{2,1,0:T(8,128)(2,1)S(1)} all-to-all(bf16[4,32,128]{2,1,0:T(8,128)(2,1)S(1)} %shard_map.59), channel_id=1, replica_groups=mesh['sect'=4,'tok'=4,'vocab'=32] {'sect'}, dimensions={0} | all-to-all | bytes 65536 | tf_op jit(solution)/shard_map/all_to_all | solution.py:32
  29.3 0.0 copy-start
  29.3 0.2 shard_map.60
  29.5 15.1 %all_to_all.31.mine_ref = bf16[16,32,512]{2,1,0:T(8,128)(2,1)S(1)} all-to-all(bf16[16,32,512]{2,1,0:T(8,128)(2,1)S(1)} %shard_map.60), channel_id=1, replica_groups={{0,2,4,6,8,10,12,14,16,18,20,22,24,26,28,30},{1,3,5,7,9,11,13,15,17,19,..., dimensions={0} | all-to-all | bytes 1048576 | tf_op jit(solution)/shard_map/all_to_all | solution.py:32
  44.6 1.9 %collective-permute-start = (bf16[16,32,512]{2,1,0:T(8,128)(2,1)S(1)}, bf16[16,32,512]{2,1,0:T(8,128)(2,1)S(1)}, u32[]{:S(2)}, u32[]{:S(2)}) collective-permute-start(bf16[16,32,512]{2,1,0:T(8,128)(2,1)S(1)} %all_to_all.31.mine_ref), channel_id=1, source_target_pairs={{0,1},{1,0},{2,3},{3,2},{4,5},{5,4},{6,7},{7,6},{8,9},{9,8},{10,11... | collective-permute-start | bytes 1572872 | tf_op jit(solution)/shard_map/ppermute | solution.py:391
  46.6 1.9 %collective-permute-done.other_ref = bf16[16,32,512]{2,1,0:T(8,128)(2,1)S(1)} collective-permute-done((bf16[16,32,512]{2,1,0:T(8,128)(2,1)S(1)}, bf16[16,32,512]{2,1,0:T(8,128)(2,1)S(1)}, u32[]{:S(2)}, u32[]{:S(2)}) %collective-permute-start) | collective-permute-done | bytes 524320 | tf_op jit(solution)/shard_map/ppermute | solution.py:391
  48.4 0.0 copy-done
  48.4 1.9 %shard_map.62 = (f32[64,2048]{1,0:T(8,128)S(1)}, f32[64,2048]{1,0:T(8,128)S(1)}) custom-call(bf16[16,32,512]{2,1,0:T(8,128)(2,1)S(1)} %all_to_all.31.mine_ref, bf16[16,32,512]{2,1,0:T(8,128)(2,1)S(1)} %collective-permute-done.other_ref, bf16[1024,2048]{1,0:T(8,128)(2,1)S(1)} %copy-done), custom_call_target="tpu_custom_call" | custom-call | flops 536870912 | bytes 5505024 | tf_op jit(solution)/shard_map/pallas_call | solution.py:156
  50.3 1.9 %collective-permute-start.1 = (f32[64,2048]{1,0:T(8,128)S(1)}, f32[64,2048]{1,0:T(8,128)S(1)}, u32[]{:S(2)}, u32[]{:S(2)}) collective-permute-start(f32[64,2048]{1,0:T(8,128)S(1)} %get-tuple-element.24), channel_id=1, source_target_pairs={{0,480},{1,33},{2,482},{3,35},{4,484},{5,37},{6,486},{7,39},{8,488... | collective-permute-start | bytes 1572872 | tf_op jit(solution)/shard_map/ppermute | solution.py:22
  52.3 0.0 copy-start.3
  52.3 0.0 copy-start.2
  52.3 4.1 %collective-permute-start.5 = (f32[64,2048]{1,0:T(8,128)S(1)}, f32[64,2048]{1,0:T(8,128)S(1)}, u32[]{:S(2)}, u32[]{:S(2)}) collective-permute-start(f32[64,2048]{1,0:T(8,128)S(1)} %get-tuple-element.28), channel_id=1, source_target_pairs={{0,32},{1,481},{2,34},{3,483},{4,36},{5,485},{6,38},{7,487},{8,40}... | collective-permute-start | bytes 1572872 | tf_op jit(solution)/shard_map/ppermute | solution.py:22
  56.4 3.2 %shard_map.61 = (f32[64,2048]{1,0:T(8,128)S(1)}, f32[64,2048]{1,0:T(8,128)S(1)}, f32[64,2048]{1,0:T(8,128)S(1)}, f32[64,2048]{1,0:T(8,128)S(1)}, f32[128,2048]{1,0:T(8,128)S(1)}) custom-call(bf16[16,32,512]{2,1,0:T(8,128)(2,1)S(1)} %all_to_all.31.mine_ref, bf16[16,32,512]{2,1,0:T(8,128)(2,1)S(1)} %collective-permute-done.other_ref, ...), custom_call_target="tpu_custom_call" | custom-call | flops 1610612736 | bytes 8126464 | tf_op jit(solution)/shard_map/pallas_call | solution.py:156
  59.6 2.9 %collective-permute-start.3 = (f32[64,2048]{1,0:T(8,128)S(1)}, f32[64,2048]{1,0:T(8,128)S(1)}, u32[]{:S(2)}, u32[]{:S(2)}) collective-permute-start(f32[64,2048]{1,0:T(8,128)S(1)} %get-tuple-element.25), channel_id=1, source_target_pairs={{0,32},{1,481},{2,34},{3,483},{4,36},{5,485},{6,38},{7,487},{8,40}... | collective-permute-start | bytes 1572872 | tf_op jit(solution)/shard_map/ppermute | solution.py:22
  62.5 4.2 %collective-permute-start.4 = (f32[64,2048]{1,0:T(8,128)S(1)}, f32[64,2048]{1,0:T(8,128)S(1)}, u32[]{:S(2)}, u32[]{:S(2)}) collective-permute-start(f32[64,2048]{1,0:T(8,128)S(1)} %get-tuple-element.26), channel_id=1, source_target_pairs={{0,480},{1,33},{2,482},{3,35},{4,484},{5,37},{6,486},{7,39},{8,488... | collective-permute-start | bytes 1572872 | tf_op jit(solution)/shard_map/ppermute | solution.py:22
  66.7 0.0 collective-permute-done.1.far_ref
  66.7 0.1 shard_map.63
  66.8 1.9 %collective-permute-start.2 = (f32[64,2048]{1,0:T(8,128)S(1)}, f32[64,2048]{1,0:T(8,128)S(1)}, u32[]{:S(2)}, u32[]{:S(2)}) collective-permute-start(f32[64,2048]{1,0:T(8,128)S(1)} %shard_map.63), channel_id=1, source_target_pairs={{0,480},{1,33},{2,482},{3,35},{4,484},{5,37},{6,486},{7,39},{8,488... | collective-permute-start | bytes 1572872 | tf_op jit(solution)/shard_map/ppermute | solution.py:22
  68.7 0.0 collective-permute-done.5.far_ref
  68.7 0.1 shard_map.64
  68.8 3.9 %collective-permute-start.6 = (f32[64,2048]{1,0:T(8,128)S(1)}, f32[64,2048]{1,0:T(8,128)S(1)}, u32[]{:S(2)}, u32[]{:S(2)}) collective-permute-start(f32[64,2048]{1,0:T(8,128)S(1)} %shard_map.64), channel_id=1, source_target_pairs={{0,32},{1,481},{2,34},{3,483},{4,36},{5,485},{6,38},{7,487},{8,40}... | collective-permute-start | bytes 1572872 | tf_op jit(solution)/shard_map/ppermute | solution.py:22
  72.7 0.0 copy-done.3
  72.7 15.1 %all_to_all.32 = bf16[32,4,2048]{2,1,0:T(4,128)(2,1)S(1)} all-to-all(bf16[32,4,2048]{2,1,0:T(4,128)(2,1)S(1)} %bitcast.11), channel_id=1, replica_groups=mesh['sect'=4,'tok'=4,'vocab'=32] {'vocab'}, dimensions={0} | all-to-all | bytes 1048576 | tf_op jit(solution)/shard_map/all_to_all | solution.py:32
  87.8 0.3 copy.8
  88.1 0.0 collective-permute-done.3.near_second
  88.1 0.0 collective-permute-done.4.near_first
  88.1 1.4 collective-permute-done.2.next_first
  89.5 0.0 collective-permute-done.6.next_second
  89.5 0.0 copy-done.2
  89.5 1.1 shard_map.65
  90.6 11.8 %all_to_all.33.stats_ref = f32[32,8,128]{2,1,0:T(8,128)S(1)} all-to-all(f32[32,8,128]{2,1,0:T(8,128)S(1)} %get-tuple-element.32), channel_id=1, replica_groups=mesh['sect'=4,'tok'=4,'vocab'=32] {'vocab'}, dimensions={0} | all-to-all | bytes 262144 | tf_op jit(solution)/shard_map/all_to_all | solution.py:32
  102.4 0.6 shard_map.66
  103.0 2.8 %collective-permute-start.7 = (bf16[64,2048]{1,0:T(8,128)(2,1)S(1)}, bf16[64,2048]{1,0:T(8,128)(2,1)S(1)}, u32[]{:S(2)}, u32[]{:S(2)}) collective-permute-start(bf16[64,2048]{1,0:T(8,128)(2,1)S(1)} %get-tuple-element.33.refs_4_), channel_id=1, source_target_pairs={{0,32},{1,481},{2,34},{3,483},{4,36},{5,485},{6,38},{7,487},{8,40}... | collective-permute-start | bytes 786440 | tf_op jit(solution)/shard_map/ppermute | solution.py:22
  105.8 4.3 %collective-permute-start.9 = (bf16[64,2048]{1,0:T(8,128)(2,1)S(1)}, bf16[64,2048]{1,0:T(8,128)(2,1)S(1)}, u32[]{:S(2)}, u32[]{:S(2)}) collective-permute-start(bf16[64,2048]{1,0:T(8,128)(2,1)S(1)} %get-tuple-element.34.refs_5_), channel_id=1, source_target_pairs={{0,480},{1,33},{2,482},{3,35},{4,484},{5,37},{6,486},{7,39},{8,488... | collective-permute-start | bytes 786440 | tf_op jit(solution)/shard_map/ppermute | solution.py:22
  110.1 1.9 %collective-permute-start.12 = (bf16[64,2048]{1,0:T(8,128)(2,1)S(1)}, bf16[64,2048]{1,0:T(8,128)(2,1)S(1)}, u32[]{:S(2)}, u32[]{:S(2)}) collective-permute-start(bf16[64,2048]{1,0:T(8,128)(2,1)S(1)} %get-tuple-element.33.refs_4_), channel_id=1, source_target_pairs={{0,480},{1,33},{2,482},{3,35},{4,484},{5,37},{6,486},{7,39},{8,488... | collective-permute-start | bytes 786440 | tf_op jit(solution)/shard_map/ppermute | solution.py:22
  112.0 3.9 %collective-permute-start.11 = (bf16[64,2048]{1,0:T(8,128)(2,1)S(1)}, bf16[64,2048]{1,0:T(8,128)(2,1)S(1)}, u32[]{:S(2)}, u32[]{:S(2)}) collective-permute-start(bf16[64,2048]{1,0:T(8,128)(2,1)S(1)} %get-tuple-element.34.refs_5_), channel_id=1, source_target_pairs={{0,32},{1,481},{2,34},{3,483},{4,36},{5,485},{6,38},{7,487},{8,40}... | collective-permute-start | bytes 786440 | tf_op jit(solution)/shard_map/ppermute | solution.py:22
  116.0 0.0 collective-permute-done.7.refs_2_
  116.0 1.9 %collective-permute-start.8 = (bf16[64,2048]{1,0:T(8,128)(2,1)S(1)}, bf16[64,2048]{1,0:T(8,128)(2,1)S(1)}, u32[]{:S(2)}, u32[]{:S(2)}) collective-permute-start(bf16[64,2048]{1,0:T(8,128)(2,1)S(1)} %collective-permute-done.7.refs_2_), channel_id=1, source_target_pairs={{0,32},{1,481},{2,34},{3,483},{4,36},{5,485},{6,38},{7,487},{8,40}... | collective-permute-start | bytes 786440 | tf_op jit(solution)/shard_map/ppermute | solution.py:22
  117.9 0.0 collective-permute-done.9.refs_3_
  117.9 5.1 %collective-permute-start.10 = (bf16[64,2048]{1,0:T(8,128)(2,1)S(1)}, bf16[64,2048]{1,0:T(8,128)(2,1)S(1)}, u32[]{:S(2)}, u32[]{:S(2)}) collective-permute-start(bf16[64,2048]{1,0:T(8,128)(2,1)S(1)} %collective-permute-done.9.refs_3_), channel_id=1, source_target_pairs={{0,480},{1,33},{2,482},{3,35},{4,484},{5,37},{6,486},{7,39},{8,488... | collective-permute-start | bytes 786440 | tf_op jit(solution)/shard_map/ppermute | solution.py:22
  123.0 0.0 collective-permute-done.12.refs_1_
  123.1 0.0 collective-permute-done.11.refs_0_
  123.1 2.9 %shard_map.67 = (f32[16,32,512]{2,1,0:T(8,128)S(1)}, f32[16,32,512]{2,1,0:T(8,128)S(1)}) custom-call(bf16[1024,2048]{1,0:T(8,128)(2,1)S(1)} %copy-done, bf16[64,2048]{1,0:T(8,128)(2,1)S(1)} %collective-permute-done.11.refs_0_, bf16[64,2048]{1,0:T(8,128)(2,1)S(1)} %collective-permute-done.12.refs_1_, bf16[64,2048]{1,0:T(8,128)(2,1)S(1)} %collective-permute-done.7.refs_2_, ...), custom_call_target="tpu_custom_call" | custom-call | flops 1610612736 | bytes 7340032 | tf_op jit(solution)/shard_map/pallas_call | solution.py:293
  125.9 1.4 collective-permute-done.8.refs_0_
  127.4 0.0 collective-permute-done.10.refs_1_
  127.4 1.6 shard_map.68
  128.9 2.6 %collective-permute-start.13 = (f32[16,32,512]{2,1,0:T(8,128)S(1)}, f32[16,32,512]{2,1,0:T(8,128)S(1)}, u32[]{:S(2)}, u32[]{:S(2)}) collective-permute-start(f32[16,32,512]{2,1,0:T(8,128)S(1)} %get-tuple-element.38), channel_id=1, source_target_pairs={{0,1},{1,0},{2,3},{3,2},{4,5},{5,4},{6,7},{7,6},{8,9},{9,8},{10,11... | collective-permute-start | bytes 3145736 | tf_op jit(solution)/shard_map/ppermute | solution.py:452
  131.6 2.3 %collective-permute-done.13 = f32[16,32,512]{2,1,0:T(8,128)S(1)} collective-permute-done((f32[16,32,512]{2,1,0:T(8,128)S(1)}, f32[16,32,512]{2,1,0:T(8,128)S(1)}, u32[]{:S(2)}, u32[]{:S(2)}) %collective-permute-start.13) | collective-permute-done | bytes 1048608 | tf_op jit(solution)/shard_map/ppermute | solution.py:452
  133.8 0.2 add.3
  134.1 20.2 %all_to_all.34.parts_ref = f32[16,32,512]{2,1,0:T(8,128)S(1)} all-to-all(f32[16,32,512]{2,1,0:T(8,128)S(1)} %add.3), channel_id=1, replica_groups={{0,2,4,6,8,10,12,14,16,18,20,22,24,26,28,30},{1,3,5,7,9,11,13,15,17,19,..., dimensions={0} | all-to-all | bytes 2097152 | tf_op jit(solution)/shard_map/all_to_all | solution.py:32
  154.3 0.1 shard_map.69
  154.5 17.3 %all_to_all.35.got_ref = f32[4,40,128]{2,1,0:T(8,128)S(1)} all-to-all(f32[4,40,128]{2,1,0:T(8,128)S(1)} %shard_map.69), channel_id=1, replica_groups=mesh['sect'=4,'tok'=4,'vocab'=32] {'sect'}, dimensions={0} | all-to-all | bytes 163840 | tf_op jit(solution)/shard_map/all_to_all | solution.py:32
  171.8 0.8 shard_map.70
Async XLA Ops:
  0.6 0.8 copy-start.1
  29.3 19.2 %copy-start = (bf16[1024,2048]{1,0:T(8,128)(2,1)S(1)}, bf16[1024,2048]{1,0:T(8,128)(2,1)}, u32[]{:S(2)}) copy-start(bf16[1024,2048]{1,0:T(8,128)(2,1)} %w_ref.7) | copy-start | bytes 12582916
  44.6 3.8 %collective-permute-start = (bf16[16,32,512]{2,1,0:T(8,128)(2,1)S(1)}, bf16[16,32,512]{2,1,0:T(8,128)(2,1)S(1)}, u32[]{:S(2)}, u32[]{:S(2)}) collective-permute-start(bf16[16,32,512]{2,1,0:T(8,128)(2,1)S(1)} %all_to_all.31.mine_ref), channel_id=1, source_target_pairs={{0,1},{1,0},{2,3},{3,2},{4,5},{5,4},{6,7},{7,6},{8,9},{9,8},{10,11... | collective-permute-start | bytes 1572872 | tf_op jit(solution)/shard_map/ppermute | solution.py:391
  50.3 16.3 %collective-permute-start.1 = (f32[64,2048]{1,0:T(8,128)S(1)}, f32[64,2048]{1,0:T(8,128)S(1)}, u32[]{:S(2)}, u32[]{:S(2)}) collective-permute-start(f32[64,2048]{1,0:T(8,128)S(1)} %get-tuple-element.24), channel_id=1, source_target_pairs={{0,480},{1,33},{2,482},{3,35},{4,484},{5,37},{6,486},{7,39},{8,488... | collective-permute-start | bytes 1572872 | tf_op jit(solution)/shard_map/ppermute | solution.py:22
  52.3 20.4 %copy-start.3 = (bf16[4,65536]{1,0:T(4,128)(2,1)S(1)}, bf16[4,65536]{1,0:T(4,128)(2,1)}, u32[]{:S(2)}) copy-start(bf16[4,65536]{1,0:T(4,128)(2,1)} %param.6) | copy-start | bytes 1572868
  52.3 37.2 %copy-start.2 = (s32[4,4]{1,0:T(4,128)S(1)}, s32[4,4]{1,0:T(4,128)}, u32[]{:S(2)}) copy-start(s32[4,4]{1,0:T(4,128)} %pairing_ref.1) | copy-start | bytes 196
  52.3 16.4 %collective-permute-start.5 = (f32[64,2048]{1,0:T(8,128)S(1)}, f32[64,2048]{1,0:T(8,128)S(1)}, u32[]{:S(2)}, u32[]{:S(2)}) collective-permute-start(f32[64,2048]{1,0:T(8,128)S(1)} %get-tuple-element.28), channel_id=1, source_target_pairs={{0,32},{1,481},{2,34},{3,483},{4,36},{5,485},{6,38},{7,487},{8,40}... | collective-permute-start | bytes 1572872 | tf_op jit(solution)/shard_map/ppermute | solution.py:22
  59.6 28.5 %collective-permute-start.3 = (f32[64,2048]{1,0:T(8,128)S(1)}, f32[64,2048]{1,0:T(8,128)S(1)}, u32[]{:S(2)}, u32[]{:S(2)}) collective-permute-start(f32[64,2048]{1,0:T(8,128)S(1)} %get-tuple-element.25), channel_id=1, source_target_pairs={{0,32},{1,481},{2,34},{3,483},{4,36},{5,485},{6,38},{7,487},{8,40}... | collective-permute-start | bytes 1572872 | tf_op jit(solution)/shard_map/ppermute | solution.py:22
  62.5 25.6 %collective-permute-start.4 = (f32[64,2048]{1,0:T(8,128)S(1)}, f32[64,2048]{1,0:T(8,128)S(1)}, u32[]{:S(2)}, u32[]{:S(2)}) collective-permute-start(f32[64,2048]{1,0:T(8,128)S(1)} %get-tuple-element.26), channel_id=1, source_target_pairs={{0,480},{1,33},{2,482},{3,35},{4,484},{5,37},{6,486},{7,39},{8,488... | collective-permute-start | bytes 1572872 | tf_op jit(solution)/shard_map/ppermute | solution.py:22
  66.8 22.7 %collective-permute-start.2 = (f32[64,2048]{1,0:T(8,128)S(1)}, f32[64,2048]{1,0:T(8,128)S(1)}, u32[]{:S(2)}, u32[]{:S(2)}) collective-permute-start(f32[64,2048]{1,0:T(8,128)S(1)} %shard_map.63), channel_id=1, source_target_pairs={{0,480},{1,33},{2,482},{3,35},{4,484},{5,37},{6,486},{7,39},{8,488... | collective-permute-start | bytes 1572872 | tf_op jit(solution)/shard_map/ppermute | solution.py:22
  68.8 20.7 %collective-permute-start.6 = (f32[64,2048]{1,0:T(8,128)S(1)}, f32[64,2048]{1,0:T(8,128)S(1)}, u32[]{:S(2)}, u32[]{:S(2)}) collective-permute-start(f32[64,2048]{1,0:T(8,128)S(1)} %shard_map.64), channel_id=1, source_target_pairs={{0,32},{1,481},{2,34},{3,483},{4,36},{5,485},{6,38},{7,487},{8,40}... | collective-permute-start | bytes 1572872 | tf_op jit(solution)/shard_map/ppermute | solution.py:22
  103.0 12.9 %collective-permute-start.7 = (bf16[64,2048]{1,0:T(8,128)(2,1)S(1)}, bf16[64,2048]{1,0:T(8,128)(2,1)S(1)}, u32[]{:S(2)}, u32[]{:S(2)}) collective-permute-start(bf16[64,2048]{1,0:T(8,128)(2,1)S(1)} %get-tuple-element.33.refs_4_), channel_id=1, source_target_pairs={{0,32},{1,481},{2,34},{3,483},{4,36},{5,485},{6,38},{7,487},{8,40}... | collective-permute-start | bytes 786440 | tf_op jit(solution)/shard_map/ppermute | solution.py:22
  105.8 12.1 %collective-permute-start.9 = (bf16[64,2048]{1,0:T(8,128)(2,1)S(1)}, bf16[64,2048]{1,0:T(8,128)(2,1)S(1)}, u32[]{:S(2)}, u32[]{:S(2)}) collective-permute-start(bf16[64,2048]{1,0:T(8,128)(2,1)S(1)} %get-tuple-element.34.refs_5_), channel_id=1, source_target_pairs={{0,480},{1,33},{2,482},{3,35},{4,484},{5,37},{6,486},{7,39},{8,488... | collective-permute-start | bytes 786440 | tf_op jit(solution)/shard_map/ppermute | solution.py:22
  110.1 13.0 %collective-permute-start.12 = (bf16[64,2048]{1,0:T(8,128)(2,1)S(1)}, bf16[64,2048]{1,0:T(8,128)(2,1)S(1)}, u32[]{:S(2)}, u32[]{:S(2)}) collective-permute-start(bf16[64,2048]{1,0:T(8,128)(2,1)S(1)} %get-tuple-element.33.refs_4_), channel_id=1, source_target_pairs={{0,480},{1,33},{2,482},{3,35},{4,484},{5,37},{6,486},{7,39},{8,488... | collective-permute-start | bytes 786440 | tf_op jit(solution)/shard_map/ppermute | solution.py:22
  112.0 11.0 %collective-permute-start.11 = (bf16[64,2048]{1,0:T(8,128)(2,1)S(1)}, bf16[64,2048]{1,0:T(8,128)(2,1)S(1)}, u32[]{:S(2)}, u32[]{:S(2)}) collective-permute-start(bf16[64,2048]{1,0:T(8,128)(2,1)S(1)} %get-tuple-element.34.refs_5_), channel_id=1, source_target_pairs={{0,32},{1,481},{2,34},{3,483},{4,36},{5,485},{6,38},{7,487},{8,40}... | collective-permute-start | bytes 786440 | tf_op jit(solution)/shard_map/ppermute | solution.py:22
  116.0 11.4 %collective-permute-start.8 = (bf16[64,2048]{1,0:T(8,128)(2,1)S(1)}, bf16[64,2048]{1,0:T(8,128)(2,1)S(1)}, u32[]{:S(2)}, u32[]{:S(2)}) collective-permute-start(bf16[64,2048]{1,0:T(8,128)(2,1)S(1)} %collective-permute-done.7.refs_2_), channel_id=1, source_target_pairs={{0,32},{1,481},{2,34},{3,483},{4,36},{5,485},{6,38},{7,487},{8,40}... | collective-permute-start | bytes 786440 | tf_op jit(solution)/shard_map/ppermute | solution.py:22
  117.9 9.5 %collective-permute-start.10 = (bf16[64,2048]{1,0:T(8,128)(2,1)S(1)}, bf16[64,2048]{1,0:T(8,128)(2,1)S(1)}, u32[]{:S(2)}, u32[]{:S(2)}) collective-permute-start(bf16[64,2048]{1,0:T(8,128)(2,1)S(1)} %collective-permute-done.9.refs_3_), channel_id=1, source_target_pairs={{0,480},{1,33},{2,482},{3,35},{4,484},{5,37},{6,486},{7,39},{8,488... | collective-permute-start | bytes 786440 | tf_op jit(solution)/shard_map/ppermute | solution.py:22
  128.9 4.9 %collective-permute-start.13 = (f32[16,32,512]{2,1,0:T(8,128)S(1)}, f32[16,32,512]{2,1,0:T(8,128)S(1)}, u32[]{:S(2)}, u32[]{:S(2)}) collective-permute-start(f32[16,32,512]{2,1,0:T(8,128)S(1)} %get-tuple-element.38), channel_id=1, source_target_pairs={{0,1},{1,0},{2,3},{3,2},{4,5},{5,4},{6,7},{7,6},{8,9},{9,8},{10,11... | collective-permute-start | bytes 3145736 | tf_op jit(solution)/shard_map/ppermute | solution.py:452

commit v8 on v7

--- a/solution.py
+++ b/solution.py
@@ -168,6 +168,46 @@
             2 * count * feats * width, feats * width * 2 + count * (feats * 2 + width * 4)
         ),
     )(mine, other, head_weight)
+
+
+def edge_kernel(swapped, x_ref, w_ref, *refs):
+    *earlier, first_ref, second_ref, flipped = refs
+    half, width = first_ref.shape
+    pairs, unit, _ = x_ref.shape
+    core = remainder(lax.axis_index("vocab"), 2)
+    turned = x_ref[:, :, : 2 * half].reshape(pairs * unit, 2 * half).T
+    low, high = halves(core, half)
+    flipped[low] = turned[:half]
+    flipped[high] = turned[half:]
+    chosen = remainder(core + swapped, 2)
+    tile = 512
+
+    @pl.loop(0, width // tile)
+    def _(step):
+        place = pl.ds(pl.multiple_of(step * tile, tile), tile)
+        weights = w_ref[:, chosen, :, place].reshape(pairs * unit, tile)
+        result = jnp.dot(flipped[...], weights, preferred_element_type=jnp.float32)
+        first, second = result[:half], result[half:]
+        if earlier:
+            first, second = first + earlier[0][:, place], second + earlier[1][:, place]
+        first_ref[:, place] = first
+        second_ref[:, place] = second
+
+
+def edge_logits(hidden, head, own, earlier=()):
+    pairs, _, unit, width = head.shape
+    shape = jax.ShapeDtypeStruct((own // 2, width), jnp.float32)
+    return pl.pallas_call(
+        functools.partial(edge_kernel, 1 if earlier else 0),
+        in_specs=[VMEM] * (2 + len(earlier)),
+        out_specs=[VMEM, VMEM],
+        out_shape=[shape, shape],
+        scratch_shapes=[pltpu.VMEM((own, pairs * unit), jnp.bfloat16)],
+        compiler_params=params(),
+        cost_estimate=cost(
+            2 * own * pairs * unit * width, pairs * unit * width * 2 + own * width * 4
+        ),
+    )(hidden, head, *earlier)
 
 
 def add_kernel(mine_ref, far_ref, out_ref):
@@ -391,7 +431,9 @@
     other = lax.ppermute(mine, "vocab", other_core)
 
     shift = functools.partial(along_z, planes=planes, vocabs=vocabs)
-    edge_first, edge_second = partial_logits(mine, other, head_weight, 0, [half, half])
+    paired_head = head_weight.reshape(vocabs // 2, 2, feats, width)
+    edges = edge_logits(mine, paired_head, own)
+    edge_first, edge_second = edge_logits(other, paired_head, own, edges)
     far_first = shift(edge_first, -1)
     far_second = shift(edge_second, 1)
     near_first, near_second, next_first, next_second, kept = partial_logits(

time: 175 us -> 174 us (level)
    pallas_call x0 -> x2, Pallas kernels: none -> 2.06 us  [edge_logits(): pl.pallas_call(functools.partial(edge_kernel, 1 if earlier else 0), in_sp...]
    pallas_call x2 -> x1, Pallas kernels: 5.12 us -> 3.24 us  [partial_logits(): pl.pallas_call(functools.partial(logits_kernel, first), grid=(width // ti...]
where the time goes in v8:
time: 174 us; the launch traced here: 172 us
  blocking collectives  107 us (61%)
  starting transfers between devices  43.4 us (25%)
  Pallas kernels  13 us (7%)
  waiting for transfers between devices  5.96 us (3%)
    all_to_all x6, blocking collectives, exchange(): lax.all_to_all(value, axis, split_axis=0, concat_axis=0, tiled=True, **gr...  107 us
    ppermute x12, starting transfers between devices, along_z(): return lax.ppermute(value, ('sect', 'tok', 'vocab'), pairs)  38.8 us
    pallas_call x2, Pallas kernels, hidden_grads(): pl.pallas_call(functools.partial(hidden_kernel, len(earlier)), grid=(step...  4.41 us
  transfers between devices with their start and end apart: 14, of which 4 were waited for; matrix products, arithmetic and copies ran while one was open for 0% of the time, Pallas kernels for 4%

profile of v8, /device:TPU:6, one launch (start us, length us, event | category | flops | bytes accessed | tf_op | source)
XLA Modules:
  0.0 171.7 jit_solution(665136355747712904)
XLA Ops:
  0.6 0.0 copy-start.1
  0.6 0.7 copy-done.1
  1.4 0.2 shard_map.59
  1.6 27.6 %all_to_all.30.got_ref = bf16[4,32,128]{2,1,0:T(8,128)(2,1)S(1)} all-to-all(bf16[4,32,128]{2,1,0:T(8,128)(2,1)S(1)} %shard_map.59), channel_id=1, replica_groups=mesh['sect'=4,'tok'=4,'vocab'=32] {'sect'}, dimensions={0} | all-to-all | bytes 65536 | tf_op jit(solution)/shard_map/all_to_all | solution.py:32
  29.3 0.0 copy-start
  29.3 0.2 shard_map.60
  29.5 15.1 %all_to_all.31.mine_ref.x_ref = bf16[16,32,512]{2,1,0:T(8,128)(2,1)S(1)} all-to-all(bf16[16,32,512]{2,1,0:T(8,128)(2,1)S(1)} %shard_map.60), channel_id=1, replica_groups={{0,2,4,6,8,10,12,14,16,18,20,22,24,26,28,30},{1,3,5,7,9,11,13,15,17,19,..., dimensions={0} | all-to-all | bytes 1048576 | tf_op jit(solution)/shard_map/all_to_all | solution.py:32
  44.6 1.9 %collective-permute-start = (bf16[16,32,512]{2,1,0:T(8,128)(2,1)S(1)}, bf16[16,32,512]{2,1,0:T(8,128)(2,1)S(1)}, u32[]{:S(2)}, u32[]{:S(2)}) collective-permute-start(bf16[16,32,512]{2,1,0:T(8,128)(2,1)S(1)} %all_to_all.31.mine_ref.x_ref), channel_id=1, source_target_pairs={{0,1},{1,0},{2,3},{3,2},{4,5},{5,4},{6,7},{7,6},{8,9},{9,8},{10,11... | collective-permute-start | bytes 1572872 | tf_op jit(solution)/shard_map/ppermute | solution.py:431
  46.6 0.0 copy-done
  46.6 1.0 shard_map.62
  47.6 0.8 collective-permute-done.other_ref.x_ref
  48.4 1.0 shard_map.63
  49.5 1.9 %collective-permute-start.1 = (f32[64,2048]{1,0:T(8,128)S(1)}, f32[64,2048]{1,0:T(8,128)S(1)}, u32[]{:S(2)}, u32[]{:S(2)}) collective-permute-start(f32[64,2048]{1,0:T(8,128)S(1)} %get-tuple-element.28), channel_id=1, source_target_pairs={{0,480},{1,33},{2,482},{3,35},{4,484},{5,37},{6,486},{7,39},{8,488... | collective-permute-start | bytes 1572872 | tf_op jit(solution)/shard_map/ppermute | solution.py:22
  51.4 0.0 copy-start.3
  51.4 0.0 copy-start.2
  51.4 4.1 %collective-permute-start.5 = (f32[64,2048]{1,0:T(8,128)S(1)}, f32[64,2048]{1,0:T(8,128)S(1)}, u32[]{:S(2)}, u32[]{:S(2)}) collective-permute-start(f32[64,2048]{1,0:T(8,128)S(1)} %get-tuple-element.32), channel_id=1, source_target_pairs={{0,32},{1,481},{2,34},{3,483},{4,36},{5,485},{6,38},{7,487},{8,40}... | collective-permute-start | bytes 1572872 | tf_op jit(solution)/shard_map/ppermute | solution.py:22
  55.5 3.2 %shard_map.61 = (f32[64,2048]{1,0:T(8,128)S(1)}, f32[64,2048]{1,0:T(8,128)S(1)}, f32[64,2048]{1,0:T(8,128)S(1)}, f32[64,2048]{1,0:T(8,128)S(1)}, f32[128,2048]{1,0:T(8,128)S(1)}) custom-call(bf16[16,32,512]{2,1,0:T(8,128)(2,1)S(1)} %all_to_all.31.mine_ref.x_ref, bf16[16,32,512]{2,1,0:T(8,128)(2,1)S(1)} %collective-permute-done.other_ref.x_ref, ...), custom_call_target="tpu_custom_call" | custom-call | flops 1610612736 | bytes 8126464 | tf_op jit(solution)/shard_map/pallas_call | solution.py:156
  58.7 2.9 %collective-permute-start.3 = (f32[64,2048]{1,0:T(8,128)S(1)}, f32[64,2048]{1,0:T(8,128)S(1)}, u32[]{:S(2)}, u32[]{:S(2)}) collective-permute-start(f32[64,2048]{1,0:T(8,128)S(1)} %get-tuple-element.29), channel_id=1, source_target_pairs={{0,32},{1,481},{2,34},{3,483},{4,36},{5,485},{6,38},{7,487},{8,40}... | collective-permute-start | bytes 1572872 | tf_op jit(solution)/shard_map/ppermute | solution.py:22
  61.6 4.2 %collective-permute-start.4 = (f32[64,2048]{1,0:T(8,128)S(1)}, f32[64,2048]{1,0:T(8,128)S(1)}, u32[]{:S(2)}, u32[]{:S(2)}) collective-permute-start(f32[64,2048]{1,0:T(8,128)S(1)} %get-tuple-element.30), channel_id=1, source_target_pairs={{0,480},{1,33},{2,482},{3,35},{4,484},{5,37},{6,486},{7,39},{8,488... | collective-permute-start | bytes 1572872 | tf_op jit(solution)/shard_map/ppermute | solution.py:22
  65.8 0.0 collective-permute-done.1.far_ref
  65.8 0.1 shard_map.64
  65.9 1.9 %collective-permute-start.2 = (f32[64,2048]{1,0:T(8,128)S(1)}, f32[64,2048]{1,0:T(8,128)S(1)}, u32[]{:S(2)}, u32[]{:S(2)}) collective-permute-start(f32[64,2048]{1,0:T(8,128)S(1)} %shard_map.64), channel_id=1, source_target_pairs={{0,480},{1,33},{2,482},{3,35},{4,484},{5,37},{6,486},{7,39},{8,488... | collective-permute-start | bytes 1572872 | tf_op jit(solution)/shard_map/ppermute | solution.py:22
  67.8 0.0 collective-permute-done.5.far_ref
  67.8 0.1 shard_map.65
  67.9 3.9 %collective-permute-start.6 = (f32[64,2048]{1,0:T(8,128)S(1)}, f32[64,2048]{1,0:T(8,128)S(1)}, u32[]{:S(2)}, u32[]{:S(2)}) collective-permute-start(f32[64,2048]{1,0:T(8,128)S(1)} %shard_map.65), channel_id=1, source_target_pairs={{0,32},{1,481},{2,34},{3,483},{4,36},{5,485},{6,38},{7,487},{8,40}... | collective-permute-start | bytes 1572872 | tf_op jit(solution)/shard_map/ppermute | solution.py:22
  71.8 0.0 copy-done.3
  71.9 15.1 %all_to_all.32 = bf16[32,4,2048]{2,1,0:T(4,128)(2,1)S(1)} all-to-all(bf16[32,4,2048]{2,1,0:T(4,128)(2,1)S(1)} %bitcast.14), channel_id=1, replica_groups=mesh['sect'=4,'tok'=4,'vocab'=32] {'vocab'}, dimensions={0} | all-to-all | bytes 1048576 | tf_op jit(solution)/shard_map/all_to_all | solution.py:32
  86.9 0.3 copy.8
  87.2 0.0 collective-permute-done.3.near_second
  87.2 0.0 collective-permute-done.4.near_first
  87.3 1.4 collective-permute-done.2.next_first
  88.6 0.0 collective-permute-done.6.next_second
  88.6 0.0 copy-done.2
  88.7 1.1 shard_map.66
  89.8 11.8 %all_to_all.33.stats_ref = f32[32,8,128]{2,1,0:T(8,128)S(1)} all-to-all(f32[32,8,128]{2,1,0:T(8,128)S(1)} %get-tuple-element.36), channel_id=1, replica_groups=mesh['sect'=4,'tok'=4,'vocab'=32] {'vocab'}, dimensions={0} | all-to-all | bytes 262144 | tf_op jit(solution)/shard_map/all_to_all | solution.py:32
  101.6 0.6 shard_map.67
  102.2 2.8 %collective-permute-start.7 = (bf16[64,2048]{1,0:T(8,128)(2,1)S(1)}, bf16[64,2048]{1,0:T(8,128)(2,1)S(1)}, u32[]{:S(2)}, u32[]{:S(2)}) collective-permute-start(bf16[64,2048]{1,0:T(8,128)(2,1)S(1)} %get-tuple-element.37.refs_4_), channel_id=1, source_target_pairs={{0,32},{1,481},{2,34},{3,483},{4,36},{5,485},{6,38},{7,487},{8,40}... | collective-permute-start | bytes 786440 | tf_op jit(solution)/shard_map/ppermute | solution.py:22
  105.0 4.3 %collective-permute-start.9 = (bf16[64,2048]{1,0:T(8,128)(2,1)S(1)}, bf16[64,2048]{1,0:T(8,128)(2,1)S(1)}, u32[]{:S(2)}, u32[]{:S(2)}) collective-permute-start(bf16[64,2048]{1,0:T(8,128)(2,1)S(1)} %get-tuple-element.38.refs_5_), channel_id=1, source_target_pairs={{0,480},{1,33},{2,482},{3,35},{4,484},{5,37},{6,486},{7,39},{8,488... | collective-permute-start | bytes 786440 | tf_op jit(solution)/shard_map/ppermute | solution.py:22
  109.2 1.9 %collective-permute-start.12 = (bf16[64,2048]{1,0:T(8,128)(2,1)S(1)}, bf16[64,2048]{1,0:T(8,128)(2,1)S(1)}, u32[]{:S(2)}, u32[]{:S(2)}) collective-permute-start(bf16[64,2048]{1,0:T(8,128)(2,1)S(1)} %get-tuple-element.37.refs_4_), channel_id=1, source_target_pairs={{0,480},{1,33},{2,482},{3,35},{4,484},{5,37},{6,486},{7,39},{8,488... | collective-permute-start | bytes 786440 | tf_op jit(solution)/shard_map/ppermute | solution.py:22
  111.2 3.9 %collective-permute-start.11 = (bf16[64,2048]{1,0:T(8,128)(2,1)S(1)}, bf16[64,2048]{1,0:T(8,128)(2,1)S(1)}, u32[]{:S(2)}, u32[]{:S(2)}) collective-permute-start(bf16[64,2048]{1,0:T(8,128)(2,1)S(1)} %get-tuple-element.38.refs_5_), channel_id=1, source_target_pairs={{0,32},{1,481},{2,34},{3,483},{4,36},{5,485},{6,38},{7,487},{8,40}... | collective-permute-start | bytes 786440 | tf_op jit(solution)/shard_map/ppermute | solution.py:22
  115.1 0.0 collective-permute-done.7.refs_2_
  115.1 1.9 %collective-permute-start.8 = (bf16[64,2048]{1,0:T(8,128)(2,1)S(1)}, bf16[64,2048]{1,0:T(8,128)(2,1)S(1)}, u32[]{:S(2)}, u32[]{:S(2)}) collective-permute-start(bf16[64,2048]{1,0:T(8,128)(2,1)S(1)} %collective-permute-done.7.refs_2_), channel_id=1, source_target_pairs={{0,32},{1,481},{2,34},{3,483},{4,36},{5,485},{6,38},{7,487},{8,40}... | collective-permute-start | bytes 786440 | tf_op jit(solution)/shard_map/ppermute | solution.py:22
  117.0 0.0 collective-permute-done.9.refs_3_
  117.1 5.1 %collective-permute-start.10 = (bf16[64,2048]{1,0:T(8,128)(2,1)S(1)}, bf16[64,2048]{1,0:T(8,128)(2,1)S(1)}, u32[]{:S(2)}, u32[]{:S(2)}) collective-permute-start(bf16[64,2048]{1,0:T(8,128)(2,1)S(1)} %collective-permute-done.9.refs_3_), channel_id=1, source_target_pairs={{0,480},{1,33},{2,482},{3,35},{4,484},{5,37},{6,486},{7,39},{8,488... | collective-permute-start | bytes 786440 | tf_op jit(solution)/shard_map/ppermute | solution.py:22
  122.2 0.0 collective-permute-done.12.refs_1_
  122.2 0.0 collective-permute-done.11.refs_0_
  122.2 2.9 %shard_map.68 = (f32[16,32,512]{2,1,0:T(8,128)S(1)}, f32[16,32,512]{2,1,0:T(8,128)S(1)}) custom-call(bf16[1024,2048]{1,0:T(8,128)(2,1)S(1)} %copy-done, bf16[64,2048]{1,0:T(8,128)(2,1)S(1)} %collective-permute-done.11.refs_0_, bf16[64,2048]{1,0:T(8,128)(2,1)S(1)} %collective-permute-done.12.refs_1_, bf16[64,2048]{1,0:T(8,128)(2,1)S(1)} %collective-permute-done.7.refs_2_, ...), custom_call_target="tpu_custom_call" | custom-call | flops 1610612736 | bytes 7340032 | tf_op jit(solution)/shard_map/pallas_call | solution.py:333
  125.1 1.5 collective-permute-done.8.refs_0_
  126.5 0.0 collective-permute-done.10.refs_1_
  126.5 1.6 shard_map.69
  128.1 2.6 %collective-permute-start.13 = (f32[16,32,512]{2,1,0:T(8,128)S(1)}, f32[16,32,512]{2,1,0:T(8,128)S(1)}, u32[]{:S(2)}, u32[]{:S(2)}) collective-permute-start(f32[16,32,512]{2,1,0:T(8,128)S(1)} %get-tuple-element.42), channel_id=1, source_target_pairs={{0,1},{1,0},{2,3},{3,2},{4,5},{5,4},{6,7},{7,6},{8,9},{9,8},{10,11... | collective-permute-start | bytes 3145736 | tf_op jit(solution)/shard_map/ppermute | solution.py:494
  130.7 2.3 %collective-permute-done.13 = f32[16,32,512]{2,1,0:T(8,128)S(1)} collective-permute-done((f32[16,32,512]{2,1,0:T(8,128)S(1)}, f32[16,32,512]{2,1,0:T(8,128)S(1)}, u32[]{:S(2)}, u32[]{:S(2)}) %collective-permute-start.13) | collective-permute-done | bytes 1048608 | tf_op jit(solution)/shard_map/ppermute | solution.py:494
  133.0 0.2 add.3
  133.2 20.2 %all_to_all.34.parts_ref = f32[16,32,512]{2,1,0:T(8,128)S(1)} all-to-all(f32[16,32,512]{2,1,0:T(8,128)S(1)} %add.3), channel_id=1, replica_groups={{0,2,4,6,8,10,12,14,16,18,20,22,24,26,28,30},{1,3,5,7,9,11,13,15,17,19,..., dimensions={0} | all-to-all | bytes 2097152 | tf_op jit(solution)/shard_map/all_to_all | solution.py:32
  153.4 0.1 shard_map.70
  153.6 17.3 %all_to_all.35.got_ref = f32[4,40,128]{2,1,0:T(8,128)S(1)} all-to-all(f32[4,40,128]{2,1,0:T(8,128)S(1)} %shard_map.70), channel_id=1, replica_groups=mesh['sect'=4,'tok'=4,'vocab'=32] {'sect'}, dimensions={0} | all-to-all | bytes 163840 | tf_op jit(solution)/shard_map/all_to_all | solution.py:32
  170.9 0.8 shard_map.71
Async XLA Ops:
  0.6 0.8 copy-start.1
  29.3 17.3 %copy-start = (bf16[1024,2048]{1,0:T(8,128)(2,1)S(1)}, bf16[1024,2048]{1,0:T(8,128)(2,1)}, u32[]{:S(2)}) copy-start(bf16[1024,2048]{1,0:T(8,128)(2,1)} %w_ref.5) | copy-start | bytes 12582916
  44.6 3.8 %collective-permute-start = (bf16[16,32,512]{2,1,0:T(8,128)(2,1)S(1)}, bf16[16,32,512]{2,1,0:T(8,128)(2,1)S(1)}, u32[]{:S(2)}, u32[]{:S(2)}) collective-permute-start(bf16[16,32,512]{2,1,0:T(8,128)(2,1)S(1)} %all_to_all.31.mine_ref.x_ref), channel_id=1, source_target_pairs={{0,1},{1,0},{2,3},{3,2},{4,5},{5,4},{6,7},{7,6},{8,9},{9,8},{10,11... | collective-permute-start | bytes 1572872 | tf_op jit(solution)/shard_map/ppermute | solution.py:431
  49.5 16.3 %collective-permute-start.1 = (f32[64,2048]{1,0:T(8,128)S(1)}, f32[64,2048]{1,0:T(8,128)S(1)}, u32[]{:S(2)}, u32[]{:S(2)}) collective-permute-start(f32[64,2048]{1,0:T(8,128)S(1)} %get-tuple-element.28), channel_id=1, source_target_pairs={{0,480},{1,33},{2,482},{3,35},{4,484},{5,37},{6,486},{7,39},{8,488... | collective-permute-start | bytes 1572872 | tf_op jit(solution)/shard_map/ppermute | solution.py:22
  51.4 20.4 %copy-start.3 = (bf16[4,65536]{1,0:T(4,128)(2,1)S(1)}, bf16[4,65536]{1,0:T(4,128)(2,1)}, u32[]{:S(2)}) copy-start(bf16[4,65536]{1,0:T(4,128)(2,1)} %param.6) | copy-start | bytes 1572868
  51.4 37.2 %copy-start.2 = (s32[4,4]{1,0:T(4,128)S(1)}, s32[4,4]{1,0:T(4,128)}, u32[]{:S(2)}) copy-start(s32[4,4]{1,0:T(4,128)} %pairing_ref.1) | copy-start | bytes 196
  51.4 16.4 %collective-permute-start.5 = (f32[64,2048]{1,0:T(8,128)S(1)}, f32[64,2048]{1,0:T(8,128)S(1)}, u32[]{:S(2)}, u32[]{:S(2)}) collective-permute-start(f32[64,2048]{1,0:T(8,128)S(1)} %get-tuple-element.32), channel_id=1, source_target_pairs={{0,32},{1,481},{2,34},{3,483},{4,36},{5,485},{6,38},{7,487},{8,40}... | collective-permute-start | bytes 1572872 | tf_op jit(solution)/shard_map/ppermute | solution.py:22
  58.7 28.5 %collective-permute-start.3 = (f32[64,2048]{1,0:T(8,128)S(1)}, f32[64,2048]{1,0:T(8,128)S(1)}, u32[]{:S(2)}, u32[]{:S(2)}) collective-permute-start(f32[64,2048]{1,0:T(8,128)S(1)} %get-tuple-element.29), channel_id=1, source_target_pairs={{0,32},{1,481},{2,34},{3,483},{4,36},{5,485},{6,38},{7,487},{8,40}... | collective-permute-start | bytes 1572872 | tf_op jit(solution)/shard_map/ppermute | solution.py:22
  61.6 25.6 %collective-permute-start.4 = (f32[64,2048]{1,0:T(8,128)S(1)}, f32[64,2048]{1,0:T(8,128)S(1)}, u32[]{:S(2)}, u32[]{:S(2)}) collective-permute-start(f32[64,2048]{1,0:T(8,128)S(1)} %get-tuple-element.30), channel_id=1, source_target_pairs={{0,480},{1,33},{2,482},{3,35},{4,484},{5,37},{6,486},{7,39},{8,488... | collective-permute-start | bytes 1572872 | tf_op jit(solution)/shard_map/ppermute | solution.py:22
  65.9 22.7 %collective-permute-start.2 = (f32[64,2048]{1,0:T(8,128)S(1)}, f32[64,2048]{1,0:T(8,128)S(1)}, u32[]{:S(2)}, u32[]{:S(2)}) collective-permute-start(f32[64,2048]{1,0:T(8,128)S(1)} %shard_map.64), channel_id=1, source_target_pairs={{0,480},{1,33},{2,482},{3,35},{4,484},{5,37},{6,486},{7,39},{8,488... | collective-permute-start | bytes 1572872 | tf_op jit(solution)/shard_map/ppermute | solution.py:22
  67.9 20.7 %collective-permute-start.6 = (f32[64,2048]{1,0:T(8,128)S(1)}, f32[64,2048]{1,0:T(8,128)S(1)}, u32[]{:S(2)}, u32[]{:S(2)}) collective-permute-start(f32[64,2048]{1,0:T(8,128)S(1)} %shard_map.65), channel_id=1, source_target_pairs={{0,32},{1,481},{2,34},{3,483},{4,36},{5,485},{6,38},{7,487},{8,40}... | collective-permute-start | bytes 1572872 | tf_op jit(solution)/shard_map/ppermute | solution.py:22
  102.2 12.9 %collective-permute-start.7 = (bf16[64,2048]{1,0:T(8,128)(2,1)S(1)}, bf16[64,2048]{1,0:T(8,128)(2,1)S(1)}, u32[]{:S(2)}, u32[]{:S(2)}) collective-permute-start(bf16[64,2048]{1,0:T(8,128)(2,1)S(1)} %get-tuple-element.37.refs_4_), channel_id=1, source_target_pairs={{0,32},{1,481},{2,34},{3,483},{4,36},{5,485},{6,38},{7,487},{8,40}... | collective-permute-start | bytes 786440 | tf_op jit(solution)/shard_map/ppermute | solution.py:22
  105.0 12.1 %collective-permute-start.9 = (bf16[64,2048]{1,0:T(8,128)(2,1)S(1)}, bf16[64,2048]{1,0:T(8,128)(2,1)S(1)}, u32[]{:S(2)}, u32[]{:S(2)}) collective-permute-start(bf16[64,2048]{1,0:T(8,128)(2,1)S(1)} %get-tuple-element.38.refs_5_), channel_id=1, source_target_pairs={{0,480},{1,33},{2,482},{3,35},{4,484},{5,37},{6,486},{7,39},{8,488... | collective-permute-start | bytes 786440 | tf_op jit(solution)/shard_map/ppermute | solution.py:22
  109.2 13.0 %collective-permute-start.12 = (bf16[64,2048]{1,0:T(8,128)(2,1)S(1)}, bf16[64,2048]{1,0:T(8,128)(2,1)S(1)}, u32[]{:S(2)}, u32[]{:S(2)}) collective-permute-start(bf16[64,2048]{1,0:T(8,128)(2,1)S(1)} %get-tuple-element.37.refs_4_), channel_id=1, source_target_pairs={{0,480},{1,33},{2,482},{3,35},{4,484},{5,37},{6,486},{7,39},{8,488... | collective-permute-start | bytes 786440 | tf_op jit(solution)/shard_map/ppermute | solution.py:22
  111.2 11.0 %collective-permute-start.11 = (bf16[64,2048]{1,0:T(8,128)(2,1)S(1)}, bf16[64,2048]{1,0:T(8,128)(2,1)S(1)}, u32[]{:S(2)}, u32[]{:S(2)}) collective-permute-start(bf16[64,2048]{1,0:T(8,128)(2,1)S(1)} %get-tuple-element.38.refs_5_), channel_id=1, source_target_pairs={{0,32},{1,481},{2,34},{3,483},{4,36},{5,485},{6,38},{7,487},{8,40}... | collective-permute-start | bytes 786440 | tf_op jit(solution)/shard_map/ppermute | solution.py:22
  115.1 11.4 %collective-permute-start.8 = (bf16[64,2048]{1,0:T(8,128)(2,1)S(1)}, bf16[64,2048]{1,0:T(8,128)(2,1)S(1)}, u32[]{:S(2)}, u32[]{:S(2)}) collective-permute-start(bf16[64,2048]{1,0:T(8,128)(2,1)S(1)} %collective-permute-done.7.refs_2_), channel_id=1, source_target_pairs={{0,32},{1,481},{2,34},{3,483},{4,36},{5,485},{6,38},{7,487},{8,40}... | collective-permute-start | bytes 786440 | tf_op jit(solution)/shard_map/ppermute | solution.py:22
  117.1 9.5 %collective-permute-start.10 = (bf16[64,2048]{1,0:T(8,128)(2,1)S(1)}, bf16[64,2048]{1,0:T(8,128)(2,1)S(1)}, u32[]{:S(2)}, u32[]{:S(2)}) collective-permute-start(bf16[64,2048]{1,0:T(8,128)(2,1)S(1)} %collective-permute-done.9.refs_3_), channel_id=1, source_target_pairs={{0,480},{1,33},{2,482},{3,35},{4,484},{5,37},{6,486},{7,39},{8,488... | collective-permute-start | bytes 786440 | tf_op jit(solution)/shard_map/ppermute | solution.py:22
  128.1 4.9 %collective-permute-start.13 = (f32[16,32,512]{2,1,0:T(8,128)S(1)}, f32[16,32,512]{2,1,0:T(8,128)S(1)}, u32[]{:S(2)}, u32[]{:S(2)}) collective-permute-start(f32[16,32,512]{2,1,0:T(8,128)S(1)} %get-tuple-element.42), channel_id=1, source_target_pairs={{0,1},{1,0},{2,3},{3,2},{4,5},{5,4},{6,7},{7,6},{8,9},{9,8},{10,11... | collective-permute-start | bytes 3145736 | tf_op jit(solution)/shard_map/ppermute | solution.py:494

commit v9 on v8

--- a/solution.py
+++ b/solution.py
@@ -150,7 +150,7 @@
 
 def partial_logits(mine, other, head_weight, first, sizes):
     feats, width = head_weight.shape
-    tile = 512
+    tile = 1024
     count = sum(sizes)
     pairs, unit, _ = mine.shape
     return pl.pallas_call(
@@ -326,7 +326,7 @@
     feats, width = head_weight.shape
     rows = sum(piece.shape[0] for piece in pieces)
     index = (total - rows) // rows if earlier else 0
-    steps = 2
+    steps = 1
     shape = jax.ShapeDtypeStruct((pairs, feats // (2 * pairs), total), jnp.float32)
     block = pl.BlockSpec((pairs // steps, shape.shape[1], rows), lambda i: (i, 0, index))
     inputs = 1 + len(pieces)

time: 174 us -> 174 us (level)
  transfers between devices with their start and end apart: 14 -> 14, of which waited for: 4 -> 5; matrix products, arithmetic and copies ran while one was open for 0% -> 0% of each run, Pallas kernels for 4% -> 4%
where the time goes in v9:
time: 174 us; the launch traced here: 171 us
  blocking collectives  107 us (61%)
  starting transfers between devices  43.2 us (25%)
  Pallas kernels  12.1 us (7%)
  waiting for transfers between devices  6.87 us (4%)
    all_to_all x6, blocking collectives, exchange(): lax.all_to_all(value, axis, split_axis=0, concat_axis=0, tiled=True, **gr...  107 us
    ppermute x12, starting transfers between devices, along_z(): return lax.ppermute(value, ('sect', 'tok', 'vocab'), pairs)  38.8 us
    pallas_call x2, Pallas kernels, hidden_grads(): pl.pallas_call(functools.partial(hidden_kernel, len(earlier)), grid=(step...  3.91 us
    ppermute x12, waiting for transfers between devices, along_z(): return lax.ppermute(value, ('sect', 'tok', 'vocab'), pairs)  3.78 us
  transfers between devices with their start and end apart: 14, of which 5 were waited for; matrix products, arithmetic and copies ran while one was open for 0% of the time, Pallas kernels for 4%

profile of v9, /device:TPU:6, one launch (start us, length us, event | category | flops | bytes accessed | tf_op | source)
XLA Modules:
  0.0 171.5 jit_solution(8029318203497498971)
XLA Ops:
  0.6 0.0 copy-start.1
  0.6 0.7 copy-done.1
  1.4 0.2 shard_map.59
  1.6 27.6 %all_to_all.30.got_ref = bf16[4,32,128]{2,1,0:T(8,128)(2,1)S(1)} all-to-all(bf16[4,32,128]{2,1,0:T(8,128)(2,1)S(1)} %shard_map.59), channel_id=1, replica_groups=mesh['sect'=4,'tok'=4,'vocab'=32] {'sect'}, dimensions={0} | all-to-all | bytes 65536 | tf_op jit(solution)/shard_map/all_to_all | solution.py:32
  29.3 0.0 copy-start
  29.3 0.2 shard_map.60
  29.5 15.1 %all_to_all.31.mine_ref.x_ref = bf16[16,32,512]{2,1,0:T(8,128)(2,1)S(1)} all-to-all(bf16[16,32,512]{2,1,0:T(8,128)(2,1)S(1)} %shard_map.60), channel_id=1, replica_groups={{0,2,4,6,8,10,12,14,16,18,20,22,24,26,28,30},{1,3,5,7,9,11,13,15,17,19,..., dimensions={0} | all-to-all | bytes 1048576 | tf_op jit(solution)/shard_map/all_to_all | solution.py:32
  44.6 1.9 %collective-permute-start = (bf16[16,32,512]{2,1,0:T(8,128)(2,1)S(1)}, bf16[16,32,512]{2,1,0:T(8,128)(2,1)S(1)}, u32[]{:S(2)}, u32[]{:S(2)}) collective-permute-start(bf16[16,32,512]{2,1,0:T(8,128)(2,1)S(1)} %all_to_all.31.mine_ref.x_ref), channel_id=1, source_target_pairs={{0,1},{1,0},{2,3},{3,2},{4,5},{5,4},{6,7},{7,6},{8,9},{9,8},{10,11... | collective-permute-start | bytes 1572872 | tf_op jit(solution)/shard_map/ppermute | solution.py:431
  46.6 0.0 copy-done
  46.6 1.0 shard_map.62
  47.6 0.8 collective-permute-done.other_ref.x_ref
  48.4 1.0 shard_map.63
  49.5 1.9 %collective-permute-start.1 = (f32[64,2048]{1,0:T(8,128)S(1)}, f32[64,2048]{1,0:T(8,128)S(1)}, u32[]{:S(2)}, u32[]{:S(2)}) collective-permute-start(f32[64,2048]{1,0:T(8,128)S(1)} %get-tuple-element.28), channel_id=1, source_target_pairs={{0,480},{1,33},{2,482},{3,35},{4,484},{5,37},{6,486},{7,39},{8,488... | collective-permute-start | bytes 1572872 | tf_op jit(solution)/shard_map/ppermute | solution.py:22
  51.4 0.0 copy-start.3
  51.4 0.0 copy-start.2
  51.4 4.1 %collective-permute-start.5 = (f32[64,2048]{1,0:T(8,128)S(1)}, f32[64,2048]{1,0:T(8,128)S(1)}, u32[]{:S(2)}, u32[]{:S(2)}) collective-permute-start(f32[64,2048]{1,0:T(8,128)S(1)} %get-tuple-element.32), channel_id=1, source_target_pairs={{0,32},{1,481},{2,34},{3,483},{4,36},{5,485},{6,38},{7,487},{8,40}... | collective-permute-start | bytes 1572872 | tf_op jit(solution)/shard_map/ppermute | solution.py:22
  55.5 2.8 %shard_map.61 = (f32[64,2048]{1,0:T(8,128)S(1)}, f32[64,2048]{1,0:T(8,128)S(1)}, f32[64,2048]{1,0:T(8,128)S(1)}, f32[64,2048]{1,0:T(8,128)S(1)}, f32[128,2048]{1,0:T(8,128)S(1)}) custom-call(bf16[16,32,512]{2,1,0:T(8,128)(2,1)S(1)} %all_to_all.31.mine_ref.x_ref, bf16[16,32,512]{2,1,0:T(8,128)(2,1)S(1)} %collective-permute-done.other_ref.x_ref, ...), custom_call_target="tpu_custom_call" | custom-call | flops 1610612736 | bytes 8126464 | tf_op jit(solution)/shard_map/pallas_call | solution.py:156
  58.3 2.8 %collective-permute-start.3 = (f32[64,2048]{1,0:T(8,128)S(1)}, f32[64,2048]{1,0:T(8,128)S(1)}, u32[]{:S(2)}, u32[]{:S(2)}) collective-permute-start(f32[64,2048]{1,0:T(8,128)S(1)} %get-tuple-element.29), channel_id=1, source_target_pairs={{0,32},{1,481},{2,34},{3,483},{4,36},{5,485},{6,38},{7,487},{8,40}... | collective-permute-start | bytes 1572872 | tf_op jit(solution)/shard_map/ppermute | solution.py:22
  61.2 4.2 %collective-permute-start.4 = (f32[64,2048]{1,0:T(8,128)S(1)}, f32[64,2048]{1,0:T(8,128)S(1)}, u32[]{:S(2)}, u32[]{:S(2)}) collective-permute-start(f32[64,2048]{1,0:T(8,128)S(1)} %get-tuple-element.30), channel_id=1, source_target_pairs={{0,480},{1,33},{2,482},{3,35},{4,484},{5,37},{6,486},{7,39},{8,488... | collective-permute-start | bytes 1572872 | tf_op jit(solution)/shard_map/ppermute | solution.py:22
  65.4 0.0 collective-permute-done.1.far_ref
  65.4 0.1 shard_map.64
  65.5 1.9 %collective-permute-start.2 = (f32[64,2048]{1,0:T(8,128)S(1)}, f32[64,2048]{1,0:T(8,128)S(1)}, u32[]{:S(2)}, u32[]{:S(2)}) collective-permute-start(f32[64,2048]{1,0:T(8,128)S(1)} %shard_map.64), channel_id=1, source_target_pairs={{0,480},{1,33},{2,482},{3,35},{4,484},{5,37},{6,486},{7,39},{8,488... | collective-permute-start | bytes 1572872 | tf_op jit(solution)/shard_map/ppermute | solution.py:22
  67.4 0.0 collective-permute-done.5.far_ref
  67.4 0.1 shard_map.65
  67.5 3.9 %collective-permute-start.6 = (f32[64,2048]{1,0:T(8,128)S(1)}, f32[64,2048]{1,0:T(8,128)S(1)}, u32[]{:S(2)}, u32[]{:S(2)}) collective-permute-start(f32[64,2048]{1,0:T(8,128)S(1)} %shard_map.65), channel_id=1, source_target_pairs={{0,32},{1,481},{2,34},{3,483},{4,36},{5,485},{6,38},{7,487},{8,40}... | collective-permute-start | bytes 1572872 | tf_op jit(solution)/shard_map/ppermute | solution.py:22
  71.5 0.0 copy-done.3
  71.5 15.1 %all_to_all.32 = bf16[32,4,2048]{2,1,0:T(4,128)(2,1)S(1)} all-to-all(bf16[32,4,2048]{2,1,0:T(4,128)(2,1)S(1)} %bitcast.14), channel_id=1, replica_groups=mesh['sect'=4,'tok'=4,'vocab'=32] {'vocab'}, dimensions={0} | all-to-all | bytes 1048576 | tf_op jit(solution)/shard_map/all_to_all | solution.py:32
  86.5 0.3 copy.8
  86.8 0.0 collective-permute-done.3.near_second
  86.8 0.0 collective-permute-done.4.near_first
  86.9 1.8 %collective-permute-done.2.next_first = f32[64,2048]{1,0:T(8,128)S(1)} collective-permute-done((f32[64,2048]{1,0:T(8,128)S(1)}, f32[64,2048]{1,0:T(8,128)S(1)}, u32[]{:S(2)}, u32[]{:S(2)}) %collective-permute-start.2) | collective-permute-done | bytes 524320 | tf_op jit(solution)/shard_map/ppermute | solution.py:22
  88.6 0.1 collective-permute-done.6.next_second
  88.7 0.0 copy-done.2
  88.8 1.1 shard_map.66
  89.9 11.8 %all_to_all.33.stats_ref = f32[32,8,128]{2,1,0:T(8,128)S(1)} all-to-all(f32[32,8,128]{2,1,0:T(8,128)S(1)} %get-tuple-element.36), channel_id=1, replica_groups=mesh['sect'=4,'tok'=4,'vocab'=32] {'vocab'}, dimensions={0} | all-to-all | bytes 262144 | tf_op jit(solution)/shard_map/all_to_all | solution.py:32
  101.7 0.6 shard_map.67
  102.3 2.7 %collective-permute-start.7 = (bf16[64,2048]{1,0:T(8,128)(2,1)S(1)}, bf16[64,2048]{1,0:T(8,128)(2,1)S(1)}, u32[]{:S(2)}, u32[]{:S(2)}) collective-permute-start(bf16[64,2048]{1,0:T(8,128)(2,1)S(1)} %get-tuple-element.37.refs_4_), channel_id=1, source_target_pairs={{0,32},{1,481},{2,34},{3,483},{4,36},{5,485},{6,38},{7,487},{8,40}... | collective-permute-start | bytes 786440 | tf_op jit(solution)/shard_map/ppermute | solution.py:22
  105.0 4.4 %collective-permute-start.9 = (bf16[64,2048]{1,0:T(8,128)(2,1)S(1)}, bf16[64,2048]{1,0:T(8,128)(2,1)S(1)}, u32[]{:S(2)}, u32[]{:S(2)}) collective-permute-start(bf16[64,2048]{1,0:T(8,128)(2,1)S(1)} %get-tuple-element.38.refs_5_), channel_id=1, source_target_pairs={{0,480},{1,33},{2,482},{3,35},{4,484},{5,37},{6,486},{7,39},{8,488... | collective-permute-start | bytes 786440 | tf_op jit(solution)/shard_map/ppermute | solution.py:22
  109.3 1.9 %collective-permute-start.12 = (bf16[64,2048]{1,0:T(8,128)(2,1)S(1)}, bf16[64,2048]{1,0:T(8,128)(2,1)S(1)}, u32[]{:S(2)}, u32[]{:S(2)}) collective-permute-start(bf16[64,2048]{1,0:T(8,128)(2,1)S(1)} %get-tuple-element.37.refs_4_), channel_id=1, source_target_pairs={{0,480},{1,33},{2,482},{3,35},{4,484},{5,37},{6,486},{7,39},{8,488... | collective-permute-start | bytes 786440 | tf_op jit(solution)/shard_map/ppermute | solution.py:22
  111.3 3.9 %collective-permute-start.11 = (bf16[64,2048]{1,0:T(8,128)(2,1)S(1)}, bf16[64,2048]{1,0:T(8,128)(2,1)S(1)}, u32[]{:S(2)}, u32[]{:S(2)}) collective-permute-start(bf16[64,2048]{1,0:T(8,128)(2,1)S(1)} %get-tuple-element.38.refs_5_), channel_id=1, source_target_pairs={{0,32},{1,481},{2,34},{3,483},{4,36},{5,485},{6,38},{7,487},{8,40}... | collective-permute-start | bytes 786440 | tf_op jit(solution)/shard_map/ppermute | solution.py:22
  115.2 0.0 collective-permute-done.7.refs_2_
  115.2 1.9 %collective-permute-start.8 = (bf16[64,2048]{1,0:T(8,128)(2,1)S(1)}, bf16[64,2048]{1,0:T(8,128)(2,1)S(1)}, u32[]{:S(2)}, u32[]{:S(2)}) collective-permute-start(bf16[64,2048]{1,0:T(8,128)(2,1)S(1)} %collective-permute-done.7.refs_2_), channel_id=1, source_target_pairs={{0,32},{1,481},{2,34},{3,483},{4,36},{5,485},{6,38},{7,487},{8,40}... | collective-permute-start | bytes 786440 | tf_op jit(solution)/shard_map/ppermute | solution.py:22
  117.1 0.0 collective-permute-done.9.refs_3_
  117.1 5.1 %collective-permute-start.10 = (bf16[64,2048]{1,0:T(8,128)(2,1)S(1)}, bf16[64,2048]{1,0:T(8,128)(2,1)S(1)}, u32[]{:S(2)}, u32[]{:S(2)}) collective-permute-start(bf16[64,2048]{1,0:T(8,128)(2,1)S(1)} %collective-permute-done.9.refs_3_), channel_id=1, source_target_pairs={{0,480},{1,33},{2,482},{3,35},{4,484},{5,37},{6,486},{7,39},{8,488... | collective-permute-start | bytes 786440 | tf_op jit(solution)/shard_map/ppermute | solution.py:22
  122.3 0.0 collective-permute-done.12.refs_1_
  122.3 0.0 collective-permute-done.11.refs_0_
  122.3 2.6 %shard_map.68 = (f32[16,32,512]{2,1,0:T(8,128)S(1)}, f32[16,32,512]{2,1,0:T(8,128)S(1)}) custom-call(bf16[1024,2048]{1,0:T(8,128)(2,1)S(1)} %copy-done, bf16[64,2048]{1,0:T(8,128)(2,1)S(1)} %collective-permute-done.11.refs_0_, bf16[64,2048]{1,0:T(8,128)(2,1)S(1)} %collective-permute-done.12.refs_1_, bf16[64,2048]{1,0:T(8,128)(2,1)S(1)} %collective-permute-done.7.refs_2_, ...), custom_call_target="tpu_custom_call" | custom-call | flops 1610612736 | bytes 7340032 | tf_op jit(solution)/shard_map/pallas_call | solution.py:333
  124.9 1.9 %collective-permute-done.8.refs_0_ = bf16[64,2048]{1,0:T(8,128)(2,1)S(1)} collective-permute-done((bf16[64,2048]{1,0:T(8,128)(2,1)S(1)}, bf16[64,2048]{1,0:T(8,128)(2,1)S(1)}, u32[]{:S(2)}, u32[]{:S(2)}) %collective-permute-start.8) | collective-permute-done | bytes 262176 | tf_op jit(solution)/shard_map/ppermute | solution.py:22
  126.7 0.0 collective-permute-done.10.refs_1_
  126.7 1.4 shard_map.69
  128.1 2.5 %collective-permute-start.13 = (f32[16,32,512]{2,1,0:T(8,128)S(1)}, f32[16,32,512]{2,1,0:T(8,128)S(1)}, u32[]{:S(2)}, u32[]{:S(2)}) collective-permute-start(f32[16,32,512]{2,1,0:T(8,128)S(1)} %get-tuple-element.42), channel_id=1, source_target_pairs={{0,1},{1,0},{2,3},{3,2},{4,5},{5,4},{6,7},{7,6},{8,9},{9,8},{10,11... | collective-permute-start | bytes 3145736 | tf_op jit(solution)/shard_map/ppermute | solution.py:494
  130.6 2.3 %collective-permute-done.13 = f32[16,32,512]{2,1,0:T(8,128)S(1)} collective-permute-done((f32[16,32,512]{2,1,0:T(8,128)S(1)}, f32[16,32,512]{2,1,0:T(8,128)S(1)}, u32[]{:S(2)}, u32[]{:S(2)}) %collective-permute-start.13) | collective-permute-done | bytes 1048608 | tf_op jit(solution)/shard_map/ppermute | solution.py:494
  132.9 0.2 add.3
  133.1 20.3 %all_to_all.34.parts_ref = f32[16,32,512]{2,1,0:T(8,128)S(1)} all-to-all(f32[16,32,512]{2,1,0:T(8,128)S(1)} %add.3), channel_id=1, replica_groups={{0,2,4,6,8,10,12,14,16,18,20,22,24,26,28,30},{1,3,5,7,9,11,13,15,17,19,..., dimensions={0} | all-to-all | bytes 2097152 | tf_op jit(solution)/shard_map/all_to_all | solution.py:32
  153.4 0.1 shard_map.70
  153.6 17.1 %all_to_all.35.got_ref = f32[4,40,128]{2,1,0:T(8,128)S(1)} all-to-all(f32[4,40,128]{2,1,0:T(8,128)S(1)} %shard_map.70), channel_id=1, replica_groups=mesh['sect'=4,'tok'=4,'vocab'=32] {'sect'}, dimensions={0} | all-to-all | bytes 163840 | tf_op jit(solution)/shard_map/all_to_all | solution.py:32
  170.7 0.8 shard_map.71
Async XLA Ops:
  0.6 0.8 copy-start.1
  29.3 17.3 %copy-start = (bf16[1024,2048]{1,0:T(8,128)(2,1)S(1)}, bf16[1024,2048]{1,0:T(8,128)(2,1)}, u32[]{:S(2)}) copy-start(bf16[1024,2048]{1,0:T(8,128)(2,1)} %w_ref.5) | copy-start | bytes 12582916
  44.6 3.8 %collective-permute-start = (bf16[16,32,512]{2,1,0:T(8,128)(2,1)S(1)}, bf16[16,32,512]{2,1,0:T(8,128)(2,1)S(1)}, u32[]{:S(2)}, u32[]{:S(2)}) collective-permute-start(bf16[16,32,512]{2,1,0:T(8,128)(2,1)S(1)} %all_to_all.31.mine_ref.x_ref), channel_id=1, source_target_pairs={{0,1},{1,0},{2,3},{3,2},{4,5},{5,4},{6,7},{7,6},{8,9},{9,8},{10,11... | collective-permute-start | bytes 1572872 | tf_op jit(solution)/shard_map/ppermute | solution.py:431
  49.5 15.9 %collective-permute-start.1 = (f32[64,2048]{1,0:T(8,128)S(1)}, f32[64,2048]{1,0:T(8,128)S(1)}, u32[]{:S(2)}, u32[]{:S(2)}) collective-permute-start(f32[64,2048]{1,0:T(8,128)S(1)} %get-tuple-element.28), channel_id=1, source_target_pairs={{0,480},{1,33},{2,482},{3,35},{4,484},{5,37},{6,486},{7,39},{8,488... | collective-permute-start | bytes 1572872 | tf_op jit(solution)/shard_map/ppermute | solution.py:22
  51.4 20.0 %copy-start.3 = (bf16[4,65536]{1,0:T(4,128)(2,1)S(1)}, bf16[4,65536]{1,0:T(4,128)(2,1)}, u32[]{:S(2)}) copy-start(bf16[4,65536]{1,0:T(4,128)(2,1)} %param.6) | copy-start | bytes 1572868
  51.4 37.3 %copy-start.2 = (s32[4,4]{1,0:T(4,128)S(1)}, s32[4,4]{1,0:T(4,128)}, u32[]{:S(2)}) copy-start(s32[4,4]{1,0:T(4,128)} %pairing_ref.1) | copy-start | bytes 196
  51.4 16.0 %collective-permute-start.5 = (f32[64,2048]{1,0:T(8,128)S(1)}, f32[64,2048]{1,0:T(8,128)S(1)}, u32[]{:S(2)}, u32[]{:S(2)}) collective-permute-start(f32[64,2048]{1,0:T(8,128)S(1)} %get-tuple-element.32), channel_id=1, source_target_pairs={{0,32},{1,481},{2,34},{3,483},{4,36},{5,485},{6,38},{7,487},{8,40}... | collective-permute-start | bytes 1572872 | tf_op jit(solution)/shard_map/ppermute | solution.py:22
  58.3 28.5 %collective-permute-start.3 = (f32[64,2048]{1,0:T(8,128)S(1)}, f32[64,2048]{1,0:T(8,128)S(1)}, u32[]{:S(2)}, u32[]{:S(2)}) collective-permute-start(f32[64,2048]{1,0:T(8,128)S(1)} %get-tuple-element.29), channel_id=1, source_target_pairs={{0,32},{1,481},{2,34},{3,483},{4,36},{5,485},{6,38},{7,487},{8,40}... | collective-permute-start | bytes 1572872 | tf_op jit(solution)/shard_map/ppermute | solution.py:22
  61.2 25.7 %collective-permute-start.4 = (f32[64,2048]{1,0:T(8,128)S(1)}, f32[64,2048]{1,0:T(8,128)S(1)}, u32[]{:S(2)}, u32[]{:S(2)}) collective-permute-start(f32[64,2048]{1,0:T(8,128)S(1)} %get-tuple-element.30), channel_id=1, source_target_pairs={{0,480},{1,33},{2,482},{3,35},{4,484},{5,37},{6,486},{7,39},{8,488... | collective-permute-start | bytes 1572872 | tf_op jit(solution)/shard_map/ppermute | solution.py:22
  65.5 23.1 %collective-permute-start.2 = (f32[64,2048]{1,0:T(8,128)S(1)}, f32[64,2048]{1,0:T(8,128)S(1)}, u32[]{:S(2)}, u32[]{:S(2)}) collective-permute-start(f32[64,2048]{1,0:T(8,128)S(1)} %shard_map.64), channel_id=1, source_target_pairs={{0,480},{1,33},{2,482},{3,35},{4,484},{5,37},{6,486},{7,39},{8,488... | collective-permute-start | bytes 1572872 | tf_op jit(solution)/shard_map/ppermute | solution.py:22
  67.5 21.2 %collective-permute-start.6 = (f32[64,2048]{1,0:T(8,128)S(1)}, f32[64,2048]{1,0:T(8,128)S(1)}, u32[]{:S(2)}, u32[]{:S(2)}) collective-permute-start(f32[64,2048]{1,0:T(8,128)S(1)} %shard_map.65), channel_id=1, source_target_pairs={{0,32},{1,481},{2,34},{3,483},{4,36},{5,485},{6,38},{7,487},{8,40}... | collective-permute-start | bytes 1572872 | tf_op jit(solution)/shard_map/ppermute | solution.py:22
  102.3 12.9 %collective-permute-start.7 = (bf16[64,2048]{1,0:T(8,128)(2,1)S(1)}, bf16[64,2048]{1,0:T(8,128)(2,1)S(1)}, u32[]{:S(2)}, u32[]{:S(2)}) collective-permute-start(bf16[64,2048]{1,0:T(8,128)(2,1)S(1)} %get-tuple-element.37.refs_4_), channel_id=1, source_target_pairs={{0,32},{1,481},{2,34},{3,483},{4,36},{5,485},{6,38},{7,487},{8,40}... | collective-permute-start | bytes 786440 | tf_op jit(solution)/shard_map/ppermute | solution.py:22
  105.0 12.2 %collective-permute-start.9 = (bf16[64,2048]{1,0:T(8,128)(2,1)S(1)}, bf16[64,2048]{1,0:T(8,128)(2,1)S(1)}, u32[]{:S(2)}, u32[]{:S(2)}) collective-permute-start(bf16[64,2048]{1,0:T(8,128)(2,1)S(1)} %get-tuple-element.38.refs_5_), channel_id=1, source_target_pairs={{0,480},{1,33},{2,482},{3,35},{4,484},{5,37},{6,486},{7,39},{8,488... | collective-permute-start | bytes 786440 | tf_op jit(solution)/shard_map/ppermute | solution.py:22
  109.3 13.0 %collective-permute-start.12 = (bf16[64,2048]{1,0:T(8,128)(2,1)S(1)}, bf16[64,2048]{1,0:T(8,128)(2,1)S(1)}, u32[]{:S(2)}, u32[]{:S(2)}) collective-permute-start(bf16[64,2048]{1,0:T(8,128)(2,1)S(1)} %get-tuple-element.37.refs_4_), channel_id=1, source_target_pairs={{0,480},{1,33},{2,482},{3,35},{4,484},{5,37},{6,486},{7,39},{8,488... | collective-permute-start | bytes 786440 | tf_op jit(solution)/shard_map/ppermute | solution.py:22
  111.3 11.0 %collective-permute-start.11 = (bf16[64,2048]{1,0:T(8,128)(2,1)S(1)}, bf16[64,2048]{1,0:T(8,128)(2,1)S(1)}, u32[]{:S(2)}, u32[]{:S(2)}) collective-permute-start(bf16[64,2048]{1,0:T(8,128)(2,1)S(1)} %get-tuple-element.38.refs_5_), channel_id=1, source_target_pairs={{0,32},{1,481},{2,34},{3,483},{4,36},{5,485},{6,38},{7,487},{8,40}... | collective-permute-start | bytes 786440 | tf_op jit(solution)/shard_map/ppermute | solution.py:22
  115.2 11.5 %collective-permute-start.8 = (bf16[64,2048]{1,0:T(8,128)(2,1)S(1)}, bf16[64,2048]{1,0:T(8,128)(2,1)S(1)}, u32[]{:S(2)}, u32[]{:S(2)}) collective-permute-start(bf16[64,2048]{1,0:T(8,128)(2,1)S(1)} %collective-permute-done.7.refs_2_), channel_id=1, source_target_pairs={{0,32},{1,481},{2,34},{3,483},{4,36},{5,485},{6,38},{7,487},{8,40}... | collective-permute-start | bytes 786440 | tf_op jit(solution)/shard_map/ppermute | solution.py:22
  117.1 9.6 %collective-permute-start.10 = (bf16[64,2048]{1,0:T(8,128)(2,1)S(1)}, bf16[64,2048]{1,0:T(8,128)(2,1)S(1)}, u32[]{:S(2)}, u32[]{:S(2)}) collective-permute-start(bf16[64,2048]{1,0:T(8,128)(2,1)S(1)} %collective-permute-done.9.refs_3_), channel_id=1, source_target_pairs={{0,480},{1,33},{2,482},{3,35},{4,484},{5,37},{6,486},{7,39},{8,488... | collective-permute-start | bytes 786440 | tf_op jit(solution)/shard_map/ppermute | solution.py:22
  128.1 4.8 %collective-permute-start.13 = (f32[16,32,512]{2,1,0:T(8,128)S(1)}, f32[16,32,512]{2,1,0:T(8,128)S(1)}, u32[]{:S(2)}, u32[]{:S(2)}) collective-permute-start(f32[16,32,512]{2,1,0:T(8,128)S(1)} %get-tuple-element.42), channel_id=1, source_target_pairs={{0,1},{1,0},{2,3},{3,2},{4,5},{5,4},{6,7},{7,6},{8,9},{9,8},{10,11... | collective-permute-start | bytes 3145736 | tf_op jit(solution)/shard_map/ppermute | solution.py:494

commit v10 on v9

--- a/solution.py
+++ b/solution.py
@@ -180,7 +180,7 @@
     flipped[low] = turned[:half]
     flipped[high] = turned[half:]
     chosen = remainder(core + swapped, 2)
-    tile = 512
+    tile = 1024
 
     @pl.loop(0, width // tile)
     def _(step):

time: 174 us -> 173 us (level)
  no operation moved by 1% of the time
where the time goes in v10:
time: 173 us; the launch traced here: 171 us
  blocking collectives  107 us (62%)
  starting transfers between devices  43.2 us (25%)
  Pallas kernels  11.4 us (7%)
  waiting for transfers between devices  7.19 us (4%)
    all_to_all x6, blocking collectives, exchange(): lax.all_to_all(value, axis, split_axis=0, concat_axis=0, tiled=True, **gr...  107 us
    ppermute x12, starting transfers between devices, along_z(): return lax.ppermute(value, ('sect', 'tok', 'vocab'), pairs)  38.8 us
    pallas_call x2, Pallas kernels, hidden_grads(): pl.pallas_call(functools.partial(hidden_kernel, len(earlier)), grid=(step...  3.91 us
    ppermute x12, waiting for transfers between devices, along_z(): return lax.ppermute(value, ('sect', 'tok', 'vocab'), pairs)  3.78 us
  transfers between devices with their start and end apart: 14, of which 5 were waited for; matrix products, arithmetic and copies ran while one was open for 0% of the time, Pallas kernels for 4%

profile of v10, /device:TPU:6, one launch (start us, length us, event | category | flops | bytes accessed | tf_op | source)
XLA Modules:
  0.0 171.2 jit_solution(4717594193213749687)
XLA Ops:
  0.6 0.0 copy-start.1
  0.6 0.7 copy-done.1
  1.4 0.2 shard_map.59
  1.6 27.6 %all_to_all.30.got_ref = bf16[4,32,128]{2,1,0:T(8,128)(2,1)S(1)} all-to-all(bf16[4,32,128]{2,1,0:T(8,128)(2,1)S(1)} %shard_map.59), channel_id=1, replica_groups=mesh['sect'=4,'tok'=4,'vocab'=32] {'sect'}, dimensions={0} | all-to-all | bytes 65536 | tf_op jit(solution)/shard_map/all_to_all | solution.py:32
  29.3 0.0 copy-start
  29.3 0.2 shard_map.60
  29.5 15.1 %all_to_all.31.mine_ref.x_ref = bf16[16,32,512]{2,1,0:T(8,128)(2,1)S(1)} all-to-all(bf16[16,32,512]{2,1,0:T(8,128)(2,1)S(1)} %shard_map.60), channel_id=1, replica_groups={{0,2,4,6,8,10,12,14,16,18,20,22,24,26,28,30},{1,3,5,7,9,11,13,15,17,19,..., dimensions={0} | all-to-all | bytes 1048576 | tf_op jit(solution)/shard_map/all_to_all | solution.py:32
  44.6 1.9 %collective-permute-start = (bf16[16,32,512]{2,1,0:T(8,128)(2,1)S(1)}, bf16[16,32,512]{2,1,0:T(8,128)(2,1)S(1)}, u32[]{:S(2)}, u32[]{:S(2)}) collective-permute-start(bf16[16,32,512]{2,1,0:T(8,128)(2,1)S(1)} %all_to_all.31.mine_ref.x_ref), channel_id=1, source_target_pairs={{0,1},{1,0},{2,3},{3,2},{4,5},{5,4},{6,7},{7,6},{8,9},{9,8},{10,11... | collective-permute-start | bytes 1572872 | tf_op jit(solution)/shard_map/ppermute | solution.py:431
  46.6 0.0 copy-done
  46.6 0.7 shard_map.62
  47.3 1.1 collective-permute-done.other_ref.x_ref
  48.4 0.7 shard_map.63
  49.2 1.9 %collective-permute-start.1 = (f32[64,2048]{1,0:T(8,128)S(1)}, f32[64,2048]{1,0:T(8,128)S(1)}, u32[]{:S(2)}, u32[]{:S(2)}) collective-permute-start(f32[64,2048]{1,0:T(8,128)S(1)} %get-tuple-element.28), channel_id=1, source_target_pairs={{0,480},{1,33},{2,482},{3,35},{4,484},{5,37},{6,486},{7,39},{8,488... | collective-permute-start | bytes 1572872 | tf_op jit(solution)/shard_map/ppermute | solution.py:22
  51.1 0.0 copy-start.3
  51.1 0.0 copy-start.2
  51.1 4.1 %collective-permute-start.5 = (f32[64,2048]{1,0:T(8,128)S(1)}, f32[64,2048]{1,0:T(8,128)S(1)}, u32[]{:S(2)}, u32[]{:S(2)}) collective-permute-start(f32[64,2048]{1,0:T(8,128)S(1)} %get-tuple-element.32), channel_id=1, source_target_pairs={{0,32},{1,481},{2,34},{3,483},{4,36},{5,485},{6,38},{7,487},{8,40}... | collective-permute-start | bytes 1572872 | tf_op jit(solution)/shard_map/ppermute | solution.py:22
  55.2 2.8 %shard_map.61 = (f32[64,2048]{1,0:T(8,128)S(1)}, f32[64,2048]{1,0:T(8,128)S(1)}, f32[64,2048]{1,0:T(8,128)S(1)}, f32[64,2048]{1,0:T(8,128)S(1)}, f32[128,2048]{1,0:T(8,128)S(1)}) custom-call(bf16[16,32,512]{2,1,0:T(8,128)(2,1)S(1)} %all_to_all.31.mine_ref.x_ref, bf16[16,32,512]{2,1,0:T(8,128)(2,1)S(1)} %collective-permute-done.other_ref.x_ref, ...), custom_call_target="tpu_custom_call" | custom-call | flops 1610612736 | bytes 8126464 | tf_op jit(solution)/shard_map/pallas_call | solution.py:156
  58.0 2.8 %collective-permute-start.3 = (f32[64,2048]{1,0:T(8,128)S(1)}, f32[64,2048]{1,0:T(8,128)S(1)}, u32[]{:S(2)}, u32[]{:S(2)}) collective-permute-start(f32[64,2048]{1,0:T(8,128)S(1)} %get-tuple-element.29), channel_id=1, source_target_pairs={{0,32},{1,481},{2,34},{3,483},{4,36},{5,485},{6,38},{7,487},{8,40}... | collective-permute-start | bytes 1572872 | tf_op jit(solution)/shard_map/ppermute | solution.py:22
  60.9 4.2 %collective-permute-start.4 = (f32[64,2048]{1,0:T(8,128)S(1)}, f32[64,2048]{1,0:T(8,128)S(1)}, u32[]{:S(2)}, u32[]{:S(2)}) collective-permute-start(f32[64,2048]{1,0:T(8,128)S(1)} %get-tuple-element.30), channel_id=1, source_target_pairs={{0,480},{1,33},{2,482},{3,35},{4,484},{5,37},{6,486},{7,39},{8,488... | collective-permute-start | bytes 1572872 | tf_op jit(solution)/shard_map/ppermute | solution.py:22
  65.1 0.0 collective-permute-done.1.far_ref
  65.1 0.1 shard_map.64
  65.2 1.9 %collective-permute-start.2 = (f32[64,2048]{1,0:T(8,128)S(1)}, f32[64,2048]{1,0:T(8,128)S(1)}, u32[]{:S(2)}, u32[]{:S(2)}) collective-permute-start(f32[64,2048]{1,0:T(8,128)S(1)} %shard_map.64), channel_id=1, source_target_pairs={{0,480},{1,33},{2,482},{3,35},{4,484},{5,37},{6,486},{7,39},{8,488... | collective-permute-start | bytes 1572872 | tf_op jit(solution)/shard_map/ppermute | solution.py:22
  67.1 0.0 collective-permute-done.5.far_ref
  67.1 0.1 shard_map.65
  67.2 3.9 %collective-permute-start.6 = (f32[64,2048]{1,0:T(8,128)S(1)}, f32[64,2048]{1,0:T(8,128)S(1)}, u32[]{:S(2)}, u32[]{:S(2)}) collective-permute-start(f32[64,2048]{1,0:T(8,128)S(1)} %shard_map.65), channel_id=1, source_target_pairs={{0,32},{1,481},{2,34},{3,483},{4,36},{5,485},{6,38},{7,487},{8,40}... | collective-permute-start | bytes 1572872 | tf_op jit(solution)/shard_map/ppermute | solution.py:22
  71.1 0.0 copy-done.3
  71.1 15.1 %all_to_all.32 = bf16[32,4,2048]{2,1,0:T(4,128)(2,1)S(1)} all-to-all(bf16[32,4,2048]{2,1,0:T(4,128)(2,1)S(1)} %bitcast.14), channel_id=1, replica_groups=mesh['sect'=4,'tok'=4,'vocab'=32] {'vocab'}, dimensions={0} | all-to-all | bytes 1048576 | tf_op jit(solution)/shard_map/all_to_all | solution.py:32
  86.2 0.3 copy.8
  86.5 0.0 collective-permute-done.3.near_second
  86.5 0.0 collective-permute-done.4.near_first
  86.5 1.8 %collective-permute-done.2.next_first = f32[64,2048]{1,0:T(8,128)S(1)} collective-permute-done((f32[64,2048]{1,0:T(8,128)S(1)}, f32[64,2048]{1,0:T(8,128)S(1)}, u32[]{:S(2)}, u32[]{:S(2)}) %collective-permute-start.2) | collective-permute-done | bytes 524320 | tf_op jit(solution)/shard_map/ppermute | solution.py:22
  88.3 0.1 collective-permute-done.6.next_second
  88.4 0.0 copy-done.2
  88.4 1.1 shard_map.66
  89.5 11.8 %all_to_all.33.stats_ref = f32[32,8,128]{2,1,0:T(8,128)S(1)} all-to-all(f32[32,8,128]{2,1,0:T(8,128)S(1)} %get-tuple-element.36), channel_id=1, replica_groups=mesh['sect'=4,'tok'=4,'vocab'=32] {'vocab'}, dimensions={0} | all-to-all | bytes 262144 | tf_op jit(solution)/shard_map/all_to_all | solution.py:32
  101.3 0.6 shard_map.67
  101.9 2.7 %collective-permute-start.7 = (bf16[64,2048]{1,0:T(8,128)(2,1)S(1)}, bf16[64,2048]{1,0:T(8,128)(2,1)S(1)}, u32[]{:S(2)}, u32[]{:S(2)}) collective-permute-start(bf16[64,2048]{1,0:T(8,128)(2,1)S(1)} %get-tuple-element.37.refs_4_), channel_id=1, source_target_pairs={{0,32},{1,481},{2,34},{3,483},{4,36},{5,485},{6,38},{7,487},{8,40}... | collective-permute-start | bytes 786440 | tf_op jit(solution)/shard_map/ppermute | solution.py:22
  104.6 4.4 %collective-permute-start.9 = (bf16[64,2048]{1,0:T(8,128)(2,1)S(1)}, bf16[64,2048]{1,0:T(8,128)(2,1)S(1)}, u32[]{:S(2)}, u32[]{:S(2)}) collective-permute-start(bf16[64,2048]{1,0:T(8,128)(2,1)S(1)} %get-tuple-element.38.refs_5_), channel_id=1, source_target_pairs={{0,480},{1,33},{2,482},{3,35},{4,484},{5,37},{6,486},{7,39},{8,488... | collective-permute-start | bytes 786440 | tf_op jit(solution)/shard_map/ppermute | solution.py:22
  109.0 1.9 %collective-permute-start.12 = (bf16[64,2048]{1,0:T(8,128)(2,1)S(1)}, bf16[64,2048]{1,0:T(8,128)(2,1)S(1)}, u32[]{:S(2)}, u32[]{:S(2)}) collective-permute-start(bf16[64,2048]{1,0:T(8,128)(2,1)S(1)} %get-tuple-element.37.refs_4_), channel_id=1, source_target_pairs={{0,480},{1,33},{2,482},{3,35},{4,484},{5,37},{6,486},{7,39},{8,488... | collective-permute-start | bytes 786440 | tf_op jit(solution)/shard_map/ppermute | solution.py:22
  110.9 3.9 %collective-permute-start.11 = (bf16[64,2048]{1,0:T(8,128)(2,1)S(1)}, bf16[64,2048]{1,0:T(8,128)(2,1)S(1)}, u32[]{:S(2)}, u32[]{:S(2)}) collective-permute-start(bf16[64,2048]{1,0:T(8,128)(2,1)S(1)} %get-tuple-element.38.refs_5_), channel_id=1, source_target_pairs={{0,32},{1,481},{2,34},{3,483},{4,36},{5,485},{6,38},{7,487},{8,40}... | collective-permute-start | bytes 786440 | tf_op jit(solution)/shard_map/ppermute | solution.py:22
  114.9 0.0 collective-permute-done.7.refs_2_
  114.9 1.9 %collective-permute-start.8 = (bf16[64,2048]{1,0:T(8,128)(2,1)S(1)}, bf16[64,2048]{1,0:T(8,128)(2,1)S(1)}, u32[]{:S(2)}, u32[]{:S(2)}) collective-permute-start(bf16[64,2048]{1,0:T(8,128)(2,1)S(1)} %collective-permute-done.7.refs_2_), channel_id=1, source_target_pairs={{0,32},{1,481},{2,34},{3,483},{4,36},{5,485},{6,38},{7,487},{8,40}... | collective-permute-start | bytes 786440 | tf_op jit(solution)/shard_map/ppermute | solution.py:22
  116.8 0.0 collective-permute-done.9.refs_3_
  116.8 5.1 %collective-permute-start.10 = (bf16[64,2048]{1,0:T(8,128)(2,1)S(1)}, bf16[64,2048]{1,0:T(8,128)(2,1)S(1)}, u32[]{:S(2)}, u32[]{:S(2)}) collective-permute-start(bf16[64,2048]{1,0:T(8,128)(2,1)S(1)} %collective-permute-done.9.refs_3_), channel_id=1, source_target_pairs={{0,480},{1,33},{2,482},{3,35},{4,484},{5,37},{6,486},{7,39},{8,488... | collective-permute-start | bytes 786440 | tf_op jit(solution)/shard_map/ppermute | solution.py:22
  122.0 0.0 collective-permute-done.12.refs_1_
  122.0 0.0 collective-permute-done.11.refs_0_
  122.0 2.6 %shard_map.68 = (f32[16,32,512]{2,1,0:T(8,128)S(1)}, f32[16,32,512]{2,1,0:T(8,128)S(1)}) custom-call(bf16[1024,2048]{1,0:T(8,128)(2,1)S(1)} %copy-done, bf16[64,2048]{1,0:T(8,128)(2,1)S(1)} %collective-permute-done.11.refs_0_, bf16[64,2048]{1,0:T(8,128)(2,1)S(1)} %collective-permute-done.12.refs_1_, bf16[64,2048]{1,0:T(8,128)(2,1)S(1)} %collective-permute-done.7.refs_2_, ...), custom_call_target="tpu_custom_call" | custom-call | flops 1610612736 | bytes 7340032 | tf_op jit(solution)/shard_map/pallas_call | solution.py:333
  124.5 1.9 %collective-permute-done.8.refs_0_ = bf16[64,2048]{1,0:T(8,128)(2,1)S(1)} collective-permute-done((bf16[64,2048]{1,0:T(8,128)(2,1)S(1)}, bf16[64,2048]{1,0:T(8,128)(2,1)S(1)}, u32[]{:S(2)}, u32[]{:S(2)}) %collective-permute-start.8) | collective-permute-done | bytes 262176 | tf_op jit(solution)/shard_map/ppermute | solution.py:22
  126.4 0.0 collective-permute-done.10.refs_1_
  126.4 1.4 shard_map.69
  127.8 2.5 %collective-permute-start.13 = (f32[16,32,512]{2,1,0:T(8,128)S(1)}, f32[16,32,512]{2,1,0:T(8,128)S(1)}, u32[]{:S(2)}, u32[]{:S(2)}) collective-permute-start(f32[16,32,512]{2,1,0:T(8,128)S(1)} %get-tuple-element.42), channel_id=1, source_target_pairs={{0,1},{1,0},{2,3},{3,2},{4,5},{5,4},{6,7},{7,6},{8,9},{9,8},{10,11... | collective-permute-start | bytes 3145736 | tf_op jit(solution)/shard_map/ppermute | solution.py:494
  130.3 2.3 %collective-permute-done.13 = f32[16,32,512]{2,1,0:T(8,128)S(1)} collective-permute-done((f32[16,32,512]{2,1,0:T(8,128)S(1)}, f32[16,32,512]{2,1,0:T(8,128)S(1)}, u32[]{:S(2)}, u32[]{:S(2)}) %collective-permute-start.13) | collective-permute-done | bytes 1048608 | tf_op jit(solution)/shard_map/ppermute | solution.py:494
  132.5 0.2 add.3
  132.8 20.4 %all_to_all.34.parts_ref = f32[16,32,512]{2,1,0:T(8,128)S(1)} all-to-all(f32[16,32,512]{2,1,0:T(8,128)S(1)} %add.3), channel_id=1, replica_groups={{0,2,4,6,8,10,12,14,16,18,20,22,24,26,28,30},{1,3,5,7,9,11,13,15,17,19,..., dimensions={0} | all-to-all | bytes 2097152 | tf_op jit(solution)/shard_map/all_to_all | solution.py:32
  153.1 0.1 shard_map.70
  153.3 17.1 %all_to_all.35.got_ref = f32[4,40,128]{2,1,0:T(8,128)S(1)} all-to-all(f32[4,40,128]{2,1,0:T(8,128)S(1)} %shard_map.70), channel_id=1, replica_groups=mesh['sect'=4,'tok'=4,'vocab'=32] {'sect'}, dimensions={0} | all-to-all | bytes 163840 | tf_op jit(solution)/shard_map/all_to_all | solution.py:32
  170.4 0.8 shard_map.71
Async XLA Ops:
  0.6 0.8 copy-start.1
  29.3 17.3 %copy-start = (bf16[1024,2048]{1,0:T(8,128)(2,1)S(1)}, bf16[1024,2048]{1,0:T(8,128)(2,1)}, u32[]{:S(2)}) copy-start(bf16[1024,2048]{1,0:T(8,128)(2,1)} %w_ref.5) | copy-start | bytes 12582916
  44.6 3.8 %collective-permute-start = (bf16[16,32,512]{2,1,0:T(8,128)(2,1)S(1)}, bf16[16,32,512]{2,1,0:T(8,128)(2,1)S(1)}, u32[]{:S(2)}, u32[]{:S(2)}) collective-permute-start(bf16[16,32,512]{2,1,0:T(8,128)(2,1)S(1)} %all_to_all.31.mine_ref.x_ref), channel_id=1, source_target_pairs={{0,1},{1,0},{2,3},{3,2},{4,5},{5,4},{6,7},{7,6},{8,9},{9,8},{10,11... | collective-permute-start | bytes 1572872 | tf_op jit(solution)/shard_map/ppermute | solution.py:431
  49.2 15.9 %collective-permute-start.1 = (f32[64,2048]{1,0:T(8,128)S(1)}, f32[64,2048]{1,0:T(8,128)S(1)}, u32[]{:S(2)}, u32[]{:S(2)}) collective-permute-start(f32[64,2048]{1,0:T(8,128)S(1)} %get-tuple-element.28), channel_id=1, source_target_pairs={{0,480},{1,33},{2,482},{3,35},{4,484},{5,37},{6,486},{7,39},{8,488... | collective-permute-start | bytes 1572872 | tf_op jit(solution)/shard_map/ppermute | solution.py:22
  51.1 20.0 %copy-start.3 = (bf16[4,65536]{1,0:T(4,128)(2,1)S(1)}, bf16[4,65536]{1,0:T(4,128)(2,1)}, u32[]{:S(2)}) copy-start(bf16[4,65536]{1,0:T(4,128)(2,1)} %param.6) | copy-start | bytes 1572868
  51.1 37.3 %copy-start.2 = (s32[4,4]{1,0:T(4,128)S(1)}, s32[4,4]{1,0:T(4,128)}, u32[]{:S(2)}) copy-start(s32[4,4]{1,0:T(4,128)} %pairing_ref.1) | copy-start | bytes 196
  51.1 16.0 %collective-permute-start.5 = (f32[64,2048]{1,0:T(8,128)S(1)}, f32[64,2048]{1,0:T(8,128)S(1)}, u32[]{:S(2)}, u32[]{:S(2)}) collective-permute-start(f32[64,2048]{1,0:T(8,128)S(1)} %get-tuple-element.32), channel_id=1, source_target_pairs={{0,32},{1,481},{2,34},{3,483},{4,36},{5,485},{6,38},{7,487},{8,40}... | collective-permute-start | bytes 1572872 | tf_op jit(solution)/shard_map/ppermute | solution.py:22
  58.0 28.5 %collective-permute-start.3 = (f32[64,2048]{1,0:T(8,128)S(1)}, f32[64,2048]{1,0:T(8,128)S(1)}, u32[]{:S(2)}, u32[]{:S(2)}) collective-permute-start(f32[64,2048]{1,0:T(8,128)S(1)} %get-tuple-element.29), channel_id=1, source_target_pairs={{0,32},{1,481},{2,34},{3,483},{4,36},{5,485},{6,38},{7,487},{8,40}... | collective-permute-start | bytes 1572872 | tf_op jit(solution)/shard_map/ppermute | solution.py:22
  60.9 25.7 %collective-permute-start.4 = (f32[64,2048]{1,0:T(8,128)S(1)}, f32[64,2048]{1,0:T(8,128)S(1)}, u32[]{:S(2)}, u32[]{:S(2)}) collective-permute-start(f32[64,2048]{1,0:T(8,128)S(1)} %get-tuple-element.30), channel_id=1, source_target_pairs={{0,480},{1,33},{2,482},{3,35},{4,484},{5,37},{6,486},{7,39},{8,488... | collective-permute-start | bytes 1572872 | tf_op jit(solution)/shard_map/ppermute | solution.py:22
  65.2 23.1 %collective-permute-start.2 = (f32[64,2048]{1,0:T(8,128)S(1)}, f32[64,2048]{1,0:T(8,128)S(1)}, u32[]{:S(2)}, u32[]{:S(2)}) collective-permute-start(f32[64,2048]{1,0:T(8,128)S(1)} %shard_map.64), channel_id=1, source_target_pairs={{0,480},{1,33},{2,482},{3,35},{4,484},{5,37},{6,486},{7,39},{8,488... | collective-permute-start | bytes 1572872 | tf_op jit(solution)/shard_map/ppermute | solution.py:22
  67.2 21.2 %collective-permute-start.6 = (f32[64,2048]{1,0:T(8,128)S(1)}, f32[64,2048]{1,0:T(8,128)S(1)}, u32[]{:S(2)}, u32[]{:S(2)}) collective-permute-start(f32[64,2048]{1,0:T(8,128)S(1)} %shard_map.65), channel_id=1, source_target_pairs={{0,32},{1,481},{2,34},{3,483},{4,36},{5,485},{6,38},{7,487},{8,40}... | collective-permute-start | bytes 1572872 | tf_op jit(solution)/shard_map/ppermute | solution.py:22
  101.9 12.9 %collective-permute-start.7 = (bf16[64,2048]{1,0:T(8,128)(2,1)S(1)}, bf16[64,2048]{1,0:T(8,128)(2,1)S(1)}, u32[]{:S(2)}, u32[]{:S(2)}) collective-permute-start(bf16[64,2048]{1,0:T(8,128)(2,1)S(1)} %get-tuple-element.37.refs_4_), channel_id=1, source_target_pairs={{0,32},{1,481},{2,34},{3,483},{4,36},{5,485},{6,38},{7,487},{8,40}... | collective-permute-start | bytes 786440 | tf_op jit(solution)/shard_map/ppermute | solution.py:22
  104.6 12.2 %collective-permute-start.9 = (bf16[64,2048]{1,0:T(8,128)(2,1)S(1)}, bf16[64,2048]{1,0:T(8,128)(2,1)S(1)}, u32[]{:S(2)}, u32[]{:S(2)}) collective-permute-start(bf16[64,2048]{1,0:T(8,128)(2,1)S(1)} %get-tuple-element.38.refs_5_), channel_id=1, source_target_pairs={{0,480},{1,33},{2,482},{3,35},{4,484},{5,37},{6,486},{7,39},{8,488... | collective-permute-start | bytes 786440 | tf_op jit(solution)/shard_map/ppermute | solution.py:22
  109.0 13.0 %collective-permute-start.12 = (bf16[64,2048]{1,0:T(8,128)(2,1)S(1)}, bf16[64,2048]{1,0:T(8,128)(2,1)S(1)}, u32[]{:S(2)}, u32[]{:S(2)}) collective-permute-start(bf16[64,2048]{1,0:T(8,128)(2,1)S(1)} %get-tuple-element.37.refs_4_), channel_id=1, source_target_pairs={{0,480},{1,33},{2,482},{3,35},{4,484},{5,37},{6,486},{7,39},{8,488... | collective-permute-start | bytes 786440 | tf_op jit(solution)/shard_map/ppermute | solution.py:22
  110.9 11.0 %collective-permute-start.11 = (bf16[64,2048]{1,0:T(8,128)(2,1)S(1)}, bf16[64,2048]{1,0:T(8,128)(2,1)S(1)}, u32[]{:S(2)}, u32[]{:S(2)}) collective-permute-start(bf16[64,2048]{1,0:T(8,128)(2,1)S(1)} %get-tuple-element.38.refs_5_), channel_id=1, source_target_pairs={{0,32},{1,481},{2,34},{3,483},{4,36},{5,485},{6,38},{7,487},{8,40}... | collective-permute-start | bytes 786440 | tf_op jit(solution)/shard_map/ppermute | solution.py:22
  114.9 11.5 %collective-permute-start.8 = (bf16[64,2048]{1,0:T(8,128)(2,1)S(1)}, bf16[64,2048]{1,0:T(8,128)(2,1)S(1)}, u32[]{:S(2)}, u32[]{:S(2)}) collective-permute-start(bf16[64,2048]{1,0:T(8,128)(2,1)S(1)} %collective-permute-done.7.refs_2_), channel_id=1, source_target_pairs={{0,32},{1,481},{2,34},{3,483},{4,36},{5,485},{6,38},{7,487},{8,40}... | collective-permute-start | bytes 786440 | tf_op jit(solution)/shard_map/ppermute | solution.py:22
  116.8 9.6 %collective-permute-start.10 = (bf16[64,2048]{1,0:T(8,128)(2,1)S(1)}, bf16[64,2048]{1,0:T(8,128)(2,1)S(1)}, u32[]{:S(2)}, u32[]{:S(2)}) collective-permute-start(bf16[64,2048]{1,0:T(8,128)(2,1)S(1)} %collective-permute-done.9.refs_3_), channel_id=1, source_target_pairs={{0,480},{1,33},{2,482},{3,35},{4,484},{5,37},{6,486},{7,39},{8,488... | collective-permute-start | bytes 786440 | tf_op jit(solution)/shard_map/ppermute | solution.py:22
  127.8 4.8 %collective-permute-start.13 = (f32[16,32,512]{2,1,0:T(8,128)S(1)}, f32[16,32,512]{2,1,0:T(8,128)S(1)}, u32[]{:S(2)}, u32[]{:S(2)}) collective-permute-start(f32[16,32,512]{2,1,0:T(8,128)S(1)} %get-tuple-element.42), channel_id=1, source_target_pairs={{0,1},{1,0},{2,3},{3,2},{4,5},{5,4},{6,7},{7,6},{8,9},{9,8},{10,11... | collective-permute-start | bytes 3145736 | tf_op jit(solution)/shard_map/ppermute | solution.py:494

commit v11 on v10

--- a/solution.py
+++ b/solution.py
@@ -180,7 +180,7 @@
     flipped[low] = turned[:half]
     flipped[high] = turned[half:]
     chosen = remainder(core + swapped, 2)
-    tile = 1024
+    tile = 2048
 
     @pl.loop(0, width // tile)
     def _(step):

time: 173 us -> 173 us (level)
  no operation moved by 1% of the time
where the time goes in v11:
time: 173 us; the launch traced here: 171 us
  blocking collectives  107 us (62%)
  starting transfers between devices  43.2 us (25%)
  Pallas kernels  11 us (6%)
  waiting for transfers between devices  7.41 us (4%)
    all_to_all x6, blocking collectives, exchange(): lax.all_to_all(value, axis, split_axis=0, concat_axis=0, tiled=True, **gr...  107 us
    ppermute x12, starting transfers between devices, along_z(): return lax.ppermute(value, ('sect', 'tok', 'vocab'), pairs)  38.8 us
    pallas_call x2, Pallas kernels, hidden_grads(): pl.pallas_call(functools.partial(hidden_kernel, len(earlier)), grid=(step...  3.91 us
    ppermute x12, waiting for transfers between devices, along_z(): return lax.ppermute(value, ('sect', 'tok', 'vocab'), pairs)  3.77 us
  transfers between devices with their start and end apart: 14, of which 5 were waited for; matrix products, arithmetic and copies ran while one was open for 0% of the time, Pallas kernels for 4%

profile of v11, /device:TPU:6, one launch (start us, length us, event | category | flops | bytes accessed | tf_op | source)
XLA Modules:
  0.0 170.9 jit_solution(16446469929847106976)
XLA Ops:
  0.6 0.0 copy-start.1
  0.6 0.7 copy-done.1
  1.4 0.2 shard_map.59
  1.6 27.6 %all_to_all.30.got_ref = bf16[4,32,128]{2,1,0:T(8,128)(2,1)S(1)} all-to-all(bf16[4,32,128]{2,1,0:T(8,128)(2,1)S(1)} %shard_map.59), channel_id=1, replica_groups=mesh['sect'=4,'tok'=4,'vocab'=32] {'sect'}, dimensions={0} | all-to-all | bytes 65536 | tf_op jit(solution)/shard_map/all_to_all | solution.py:32
  29.3 0.0 copy-start
  29.3 0.2 shard_map.60
  29.5 15.1 %all_to_all.31.mine_ref.x_ref = bf16[16,32,512]{2,1,0:T(8,128)(2,1)S(1)} all-to-all(bf16[16,32,512]{2,1,0:T(8,128)(2,1)S(1)} %shard_map.60), channel_id=1, replica_groups={{0,2,4,6,8,10,12,14,16,18,20,22,24,26,28,30},{1,3,5,7,9,11,13,15,17,19,..., dimensions={0} | all-to-all | bytes 1048576 | tf_op jit(solution)/shard_map/all_to_all | solution.py:32
  44.6 1.9 %collective-permute-start = (bf16[16,32,512]{2,1,0:T(8,128)(2,1)S(1)}, bf16[16,32,512]{2,1,0:T(8,128)(2,1)S(1)}, u32[]{:S(2)}, u32[]{:S(2)}) collective-permute-start(bf16[16,32,512]{2,1,0:T(8,128)(2,1)S(1)} %all_to_all.31.mine_ref.x_ref), channel_id=1, source_target_pairs={{0,1},{1,0},{2,3},{3,2},{4,5},{5,4},{6,7},{7,6},{8,9},{9,8},{10,11... | collective-permute-start | bytes 1572872 | tf_op jit(solution)/shard_map/ppermute | solution.py:431
  46.6 0.0 copy-done
  46.6 0.5 shard_map.62
  47.1 1.4 collective-permute-done.other_ref.x_ref
  48.4 0.5 shard_map.63
  48.9 1.9 %collective-permute-start.1 = (f32[64,2048]{1,0:T(8,128)S(1)}, f32[64,2048]{1,0:T(8,128)S(1)}, u32[]{:S(2)}, u32[]{:S(2)}) collective-permute-start(f32[64,2048]{1,0:T(8,128)S(1)} %get-tuple-element.28), channel_id=1, source_target_pairs={{0,480},{1,33},{2,482},{3,35},{4,484},{5,37},{6,486},{7,39},{8,488... | collective-permute-start | bytes 1572872 | tf_op jit(solution)/shard_map/ppermute | solution.py:22
  50.9 0.0 copy-start.3
  50.9 0.0 copy-start.2
  50.9 4.1 %collective-permute-start.5 = (f32[64,2048]{1,0:T(8,128)S(1)}, f32[64,2048]{1,0:T(8,128)S(1)}, u32[]{:S(2)}, u32[]{:S(2)}) collective-permute-start(f32[64,2048]{1,0:T(8,128)S(1)} %get-tuple-element.32), channel_id=1, source_target_pairs={{0,32},{1,481},{2,34},{3,483},{4,36},{5,485},{6,38},{7,487},{8,40}... | collective-permute-start | bytes 1572872 | tf_op jit(solution)/shard_map/ppermute | solution.py:22
  54.9 2.8 %shard_map.61 = (f32[64,2048]{1,0:T(8,128)S(1)}, f32[64,2048]{1,0:T(8,128)S(1)}, f32[64,2048]{1,0:T(8,128)S(1)}, f32[64,2048]{1,0:T(8,128)S(1)}, f32[128,2048]{1,0:T(8,128)S(1)}) custom-call(bf16[16,32,512]{2,1,0:T(8,128)(2,1)S(1)} %all_to_all.31.mine_ref.x_ref, bf16[16,32,512]{2,1,0:T(8,128)(2,1)S(1)} %collective-permute-done.other_ref.x_ref, ...), custom_call_target="tpu_custom_call" | custom-call | flops 1610612736 | bytes 8126464 | tf_op jit(solution)/shard_map/pallas_call | solution.py:156
  57.8 2.8 %collective-permute-start.3 = (f32[64,2048]{1,0:T(8,128)S(1)}, f32[64,2048]{1,0:T(8,128)S(1)}, u32[]{:S(2)}, u32[]{:S(2)}) collective-permute-start(f32[64,2048]{1,0:T(8,128)S(1)} %get-tuple-element.29), channel_id=1, source_target_pairs={{0,32},{1,481},{2,34},{3,483},{4,36},{5,485},{6,38},{7,487},{8,40}... | collective-permute-start | bytes 1572872 | tf_op jit(solution)/shard_map/ppermute | solution.py:22
  60.7 4.2 %collective-permute-start.4 = (f32[64,2048]{1,0:T(8,128)S(1)}, f32[64,2048]{1,0:T(8,128)S(1)}, u32[]{:S(2)}, u32[]{:S(2)}) collective-permute-start(f32[64,2048]{1,0:T(8,128)S(1)} %get-tuple-element.30), channel_id=1, source_target_pairs={{0,480},{1,33},{2,482},{3,35},{4,484},{5,37},{6,486},{7,39},{8,488... | collective-permute-start | bytes 1572872 | tf_op jit(solution)/shard_map/ppermute | solution.py:22
  64.9 0.0 collective-permute-done.1.far_ref
  64.9 0.1 shard_map.64
  65.0 1.9 %collective-permute-start.2 = (f32[64,2048]{1,0:T(8,128)S(1)}, f32[64,2048]{1,0:T(8,128)S(1)}, u32[]{:S(2)}, u32[]{:S(2)}) collective-permute-start(f32[64,2048]{1,0:T(8,128)S(1)} %shard_map.64), channel_id=1, source_target_pairs={{0,480},{1,33},{2,482},{3,35},{4,484},{5,37},{6,486},{7,39},{8,488... | collective-permute-start | bytes 1572872 | tf_op jit(solution)/shard_map/ppermute | solution.py:22
  66.9 0.0 collective-permute-done.5.far_ref
  66.9 0.1 shard_map.65
  67.0 3.9 %collective-permute-start.6 = (f32[64,2048]{1,0:T(8,128)S(1)}, f32[64,2048]{1,0:T(8,128)S(1)}, u32[]{:S(2)}, u32[]{:S(2)}) collective-permute-start(f32[64,2048]{1,0:T(8,128)S(1)} %shard_map.65), channel_id=1, source_target_pairs={{0,32},{1,481},{2,34},{3,483},{4,36},{5,485},{6,38},{7,487},{8,40}... | collective-permute-start | bytes 1572872 | tf_op jit(solution)/shard_map/ppermute | solution.py:22
  70.9 0.0 copy-done.3
  70.9 15.1 %all_to_all.32 = bf16[32,4,2048]{2,1,0:T(4,128)(2,1)S(1)} all-to-all(bf16[32,4,2048]{2,1,0:T(4,128)(2,1)S(1)} %bitcast.14), channel_id=1, replica_groups=mesh['sect'=4,'tok'=4,'vocab'=32] {'vocab'}, dimensions={0} | all-to-all | bytes 1048576 | tf_op jit(solution)/shard_map/all_to_all | solution.py:32
  86.0 0.3 copy.8
  86.3 0.0 collective-permute-done.3.near_second
  86.3 0.0 collective-permute-done.4.near_first
  86.3 1.8 %collective-permute-done.2.next_first = f32[64,2048]{1,0:T(8,128)S(1)} collective-permute-done((f32[64,2048]{1,0:T(8,128)S(1)}, f32[64,2048]{1,0:T(8,128)S(1)}, u32[]{:S(2)}, u32[]{:S(2)}) %collective-permute-start.2) | collective-permute-done | bytes 524320 | tf_op jit(solution)/shard_map/ppermute | solution.py:22
  88.1 0.1 collective-permute-done.6.next_second
  88.2 0.0 copy-done.2
  88.2 1.1 shard_map.66
  89.3 11.8 %all_to_all.33.stats_ref = f32[32,8,128]{2,1,0:T(8,128)S(1)} all-to-all(f32[32,8,128]{2,1,0:T(8,128)S(1)} %get-tuple-element.36), channel_id=1, replica_groups=mesh['sect'=4,'tok'=4,'vocab'=32] {'vocab'}, dimensions={0} | all-to-all | bytes 262144 | tf_op jit(solution)/shard_map/all_to_all | solution.py:32
  101.1 0.6 shard_map.67
  101.7 2.7 %collective-permute-start.7 = (bf16[64,2048]{1,0:T(8,128)(2,1)S(1)}, bf16[64,2048]{1,0:T(8,128)(2,1)S(1)}, u32[]{:S(2)}, u32[]{:S(2)}) collective-permute-start(bf16[64,2048]{1,0:T(8,128)(2,1)S(1)} %get-tuple-element.37.refs_4_), channel_id=1, source_target_pairs={{0,32},{1,481},{2,34},{3,483},{4,36},{5,485},{6,38},{7,487},{8,40}... | collective-permute-start | bytes 786440 | tf_op jit(solution)/shard_map/ppermute | solution.py:22
  104.4 4.4 %collective-permute-start.9 = (bf16[64,2048]{1,0:T(8,128)(2,1)S(1)}, bf16[64,2048]{1,0:T(8,128)(2,1)S(1)}, u32[]{:S(2)}, u32[]{:S(2)}) collective-permute-start(bf16[64,2048]{1,0:T(8,128)(2,1)S(1)} %get-tuple-element.38.refs_5_), channel_id=1, source_target_pairs={{0,480},{1,33},{2,482},{3,35},{4,484},{5,37},{6,486},{7,39},{8,488... | collective-permute-start | bytes 786440 | tf_op jit(solution)/shard_map/ppermute | solution.py:22
  108.8 1.9 %collective-permute-start.12 = (bf16[64,2048]{1,0:T(8,128)(2,1)S(1)}, bf16[64,2048]{1,0:T(8,128)(2,1)S(1)}, u32[]{:S(2)}, u32[]{:S(2)}) collective-permute-start(bf16[64,2048]{1,0:T(8,128)(2,1)S(1)} %get-tuple-element.37.refs_4_), channel_id=1, source_target_pairs={{0,480},{1,33},{2,482},{3,35},{4,484},{5,37},{6,486},{7,39},{8,488... | collective-permute-start | bytes 786440 | tf_op jit(solution)/shard_map/ppermute | solution.py:22
  110.7 3.9 %collective-permute-start.11 = (bf16[64,2048]{1,0:T(8,128)(2,1)S(1)}, bf16[64,2048]{1,0:T(8,128)(2,1)S(1)}, u32[]{:S(2)}, u32[]{:S(2)}) collective-permute-start(bf16[64,2048]{1,0:T(8,128)(2,1)S(1)} %get-tuple-element.38.refs_5_), channel_id=1, source_target_pairs={{0,32},{1,481},{2,34},{3,483},{4,36},{5,485},{6,38},{7,487},{8,40}... | collective-permute-start | bytes 786440 | tf_op jit(solution)/shard_map/ppermute | solution.py:22
  114.7 0.0 collective-permute-done.7.refs_2_
  114.7 1.9 %collective-permute-start.8 = (bf16[64,2048]{1,0:T(8,128)(2,1)S(1)}, bf16[64,2048]{1,0:T(8,128)(2,1)S(1)}, u32[]{:S(2)}, u32[]{:S(2)}) collective-permute-start(bf16[64,2048]{1,0:T(8,128)(2,1)S(1)} %collective-permute-done.7.refs_2_), channel_id=1, source_target_pairs={{0,32},{1,481},{2,34},{3,483},{4,36},{5,485},{6,38},{7,487},{8,40}... | collective-permute-start | bytes 786440 | tf_op jit(solution)/shard_map/ppermute | solution.py:22
  116.6 0.0 collective-permute-done.9.refs_3_
  116.6 5.1 %collective-permute-start.10 = (bf16[64,2048]{1,0:T(8,128)(2,1)S(1)}, bf16[64,2048]{1,0:T(8,128)(2,1)S(1)}, u32[]{:S(2)}, u32[]{:S(2)}) collective-permute-start(bf16[64,2048]{1,0:T(8,128)(2,1)S(1)} %collective-permute-done.9.refs_3_), channel_id=1, source_target_pairs={{0,480},{1,33},{2,482},{3,35},{4,484},{5,37},{6,486},{7,39},{8,488... | collective-permute-start | bytes 786440 | tf_op jit(solution)/shard_map/ppermute | solution.py:22
  121.7 0.0 collective-permute-done.12.refs_1_
  121.8 0.0 collective-permute-done.11.refs_0_
  121.8 2.6 %shard_map.68 = (f32[16,32,512]{2,1,0:T(8,128)S(1)}, f32[16,32,512]{2,1,0:T(8,128)S(1)}) custom-call(bf16[1024,2048]{1,0:T(8,128)(2,1)S(1)} %copy-done, bf16[64,2048]{1,0:T(8,128)(2,1)S(1)} %collective-permute-done.11.refs_0_, bf16[64,2048]{1,0:T(8,128)(2,1)S(1)} %collective-permute-done.12.refs_1_, bf16[64,2048]{1,0:T(8,128)(2,1)S(1)} %collective-permute-done.7.refs_2_, ...), custom_call_target="tpu_custom_call" | custom-call | flops 1610612736 | bytes 7340032 | tf_op jit(solution)/shard_map/pallas_call | solution.py:333
  124.3 1.9 %collective-permute-done.8.refs_0_ = bf16[64,2048]{1,0:T(8,128)(2,1)S(1)} collective-permute-done((bf16[64,2048]{1,0:T(8,128)(2,1)S(1)}, bf16[64,2048]{1,0:T(8,128)(2,1)S(1)}, u32[]{:S(2)}, u32[]{:S(2)}) %collective-permute-start.8) | collective-permute-done | bytes 262176 | tf_op jit(solution)/shard_map/ppermute | solution.py:22
  126.2 0.0 collective-permute-done.10.refs_1_
  126.2 1.4 shard_map.69
  127.6 2.5 %collective-permute-start.13 = (f32[16,32,512]{2,1,0:T(8,128)S(1)}, f32[16,32,512]{2,1,0:T(8,128)S(1)}, u32[]{:S(2)}, u32[]{:S(2)}) collective-permute-start(f32[16,32,512]{2,1,0:T(8,128)S(1)} %get-tuple-element.42), channel_id=1, source_target_pairs={{0,1},{1,0},{2,3},{3,2},{4,5},{5,4},{6,7},{7,6},{8,9},{9,8},{10,11... | collective-permute-start | bytes 3145736 | tf_op jit(solution)/shard_map/ppermute | solution.py:494
  130.1 2.3 %collective-permute-done.13 = f32[16,32,512]{2,1,0:T(8,128)S(1)} collective-permute-done((f32[16,32,512]{2,1,0:T(8,128)S(1)}, f32[16,32,512]{2,1,0:T(8,128)S(1)}, u32[]{:S(2)}, u32[]{:S(2)}) %collective-permute-start.13) | collective-permute-done | bytes 1048608 | tf_op jit(solution)/shard_map/ppermute | solution.py:494
  132.3 0.2 add.3
  132.5 20.3 %all_to_all.34.parts_ref = f32[16,32,512]{2,1,0:T(8,128)S(1)} all-to-all(f32[16,32,512]{2,1,0:T(8,128)S(1)} %add.3), channel_id=1, replica_groups={{0,2,4,6,8,10,12,14,16,18,20,22,24,26,28,30},{1,3,5,7,9,11,13,15,17,19,..., dimensions={0} | all-to-all | bytes 2097152 | tf_op jit(solution)/shard_map/all_to_all | solution.py:32
  152.9 0.1 shard_map.70
  153.0 17.1 %all_to_all.35.got_ref = f32[4,40,128]{2,1,0:T(8,128)S(1)} all-to-all(f32[4,40,128]{2,1,0:T(8,128)S(1)} %shard_map.70), channel_id=1, replica_groups=mesh['sect'=4,'tok'=4,'vocab'=32] {'sect'}, dimensions={0} | all-to-all | bytes 163840 | tf_op jit(solution)/shard_map/all_to_all | solution.py:32
  170.2 0.8 shard_map.71
Async XLA Ops:
  0.6 0.8 copy-start.1
  29.3 17.3 %copy-start = (bf16[1024,2048]{1,0:T(8,128)(2,1)S(1)}, bf16[1024,2048]{1,0:T(8,128)(2,1)}, u32[]{:S(2)}) copy-start(bf16[1024,2048]{1,0:T(8,128)(2,1)} %w_ref.5) | copy-start | bytes 12582916
  44.6 3.8 %collective-permute-start = (bf16[16,32,512]{2,1,0:T(8,128)(2,1)S(1)}, bf16[16,32,512]{2,1,0:T(8,128)(2,1)S(1)}, u32[]{:S(2)}, u32[]{:S(2)}) collective-permute-start(bf16[16,32,512]{2,1,0:T(8,128)(2,1)S(1)} %all_to_all.31.mine_ref.x_ref), channel_id=1, source_target_pairs={{0,1},{1,0},{2,3},{3,2},{4,5},{5,4},{6,7},{7,6},{8,9},{9,8},{10,11... | collective-permute-start | bytes 1572872 | tf_op jit(solution)/shard_map/ppermute | solution.py:431
  48.9 15.9 %collective-permute-start.1 = (f32[64,2048]{1,0:T(8,128)S(1)}, f32[64,2048]{1,0:T(8,128)S(1)}, u32[]{:S(2)}, u32[]{:S(2)}) collective-permute-start(f32[64,2048]{1,0:T(8,128)S(1)} %get-tuple-element.28), channel_id=1, source_target_pairs={{0,480},{1,33},{2,482},{3,35},{4,484},{5,37},{6,486},{7,39},{8,488... | collective-permute-start | bytes 1572872 | tf_op jit(solution)/shard_map/ppermute | solution.py:22
  50.9 20.0 %copy-start.3 = (bf16[4,65536]{1,0:T(4,128)(2,1)S(1)}, bf16[4,65536]{1,0:T(4,128)(2,1)}, u32[]{:S(2)}) copy-start(bf16[4,65536]{1,0:T(4,128)(2,1)} %param.6) | copy-start | bytes 1572868
  50.9 37.3 %copy-start.2 = (s32[4,4]{1,0:T(4,128)S(1)}, s32[4,4]{1,0:T(4,128)}, u32[]{:S(2)}) copy-start(s32[4,4]{1,0:T(4,128)} %pairing_ref.1) | copy-start | bytes 196
  50.9 16.0 %collective-permute-start.5 = (f32[64,2048]{1,0:T(8,128)S(1)}, f32[64,2048]{1,0:T(8,128)S(1)}, u32[]{:S(2)}, u32[]{:S(2)}) collective-permute-start(f32[64,2048]{1,0:T(8,128)S(1)} %get-tuple-element.32), channel_id=1, source_target_pairs={{0,32},{1,481},{2,34},{3,483},{4,36},{5,485},{6,38},{7,487},{8,40}... | collective-permute-start | bytes 1572872 | tf_op jit(solution)/shard_map/ppermute | solution.py:22
  57.8 28.5 %collective-permute-start.3 = (f32[64,2048]{1,0:T(8,128)S(1)}, f32[64,2048]{1,0:T(8,128)S(1)}, u32[]{:S(2)}, u32[]{:S(2)}) collective-permute-start(f32[64,2048]{1,0:T(8,128)S(1)} %get-tuple-element.29), channel_id=1, source_target_pairs={{0,32},{1,481},{2,34},{3,483},{4,36},{5,485},{6,38},{7,487},{8,40}... | collective-permute-start | bytes 1572872 | tf_op jit(solution)/shard_map/ppermute | solution.py:22
  60.7 25.6 %collective-permute-start.4 = (f32[64,2048]{1,0:T(8,128)S(1)}, f32[64,2048]{1,0:T(8,128)S(1)}, u32[]{:S(2)}, u32[]{:S(2)}) collective-permute-start(f32[64,2048]{1,0:T(8,128)S(1)} %get-tuple-element.30), channel_id=1, source_target_pairs={{0,480},{1,33},{2,482},{3,35},{4,484},{5,37},{6,486},{7,39},{8,488... | collective-permute-start | bytes 1572872 | tf_op jit(solution)/shard_map/ppermute | solution.py:22
  65.0 23.1 %collective-permute-start.2 = (f32[64,2048]{1,0:T(8,128)S(1)}, f32[64,2048]{1,0:T(8,128)S(1)}, u32[]{:S(2)}, u32[]{:S(2)}) collective-permute-start(f32[64,2048]{1,0:T(8,128)S(1)} %shard_map.64), channel_id=1, source_target_pairs={{0,480},{1,33},{2,482},{3,35},{4,484},{5,37},{6,486},{7,39},{8,488... | collective-permute-start | bytes 1572872 | tf_op jit(solution)/shard_map/ppermute | solution.py:22
  67.0 21.2 %collective-permute-start.6 = (f32[64,2048]{1,0:T(8,128)S(1)}, f32[64,2048]{1,0:T(8,128)S(1)}, u32[]{:S(2)}, u32[]{:S(2)}) collective-permute-start(f32[64,2048]{1,0:T(8,128)S(1)} %shard_map.65), channel_id=1, source_target_pairs={{0,32},{1,481},{2,34},{3,483},{4,36},{5,485},{6,38},{7,487},{8,40}... | collective-permute-start | bytes 1572872 | tf_op jit(solution)/shard_map/ppermute | solution.py:22
  101.7 12.9 %collective-permute-start.7 = (bf16[64,2048]{1,0:T(8,128)(2,1)S(1)}, bf16[64,2048]{1,0:T(8,128)(2,1)S(1)}, u32[]{:S(2)}, u32[]{:S(2)}) collective-permute-start(bf16[64,2048]{1,0:T(8,128)(2,1)S(1)} %get-tuple-element.37.refs_4_), channel_id=1, source_target_pairs={{0,32},{1,481},{2,34},{3,483},{4,36},{5,485},{6,38},{7,487},{8,40}... | collective-permute-start | bytes 786440 | tf_op jit(solution)/shard_map/ppermute | solution.py:22
  104.4 12.2 %collective-permute-start.9 = (bf16[64,2048]{1,0:T(8,128)(2,1)S(1)}, bf16[64,2048]{1,0:T(8,128)(2,1)S(1)}, u32[]{:S(2)}, u32[]{:S(2)}) collective-permute-start(bf16[64,2048]{1,0:T(8,128)(2,1)S(1)} %get-tuple-element.38.refs_5_), channel_id=1, source_target_pairs={{0,480},{1,33},{2,482},{3,35},{4,484},{5,37},{6,486},{7,39},{8,488... | collective-permute-start | bytes 786440 | tf_op jit(solution)/shard_map/ppermute | solution.py:22
  108.8 13.0 %collective-permute-start.12 = (bf16[64,2048]{1,0:T(8,128)(2,1)S(1)}, bf16[64,2048]{1,0:T(8,128)(2,1)S(1)}, u32[]{:S(2)}, u32[]{:S(2)}) collective-permute-start(bf16[64,2048]{1,0:T(8,128)(2,1)S(1)} %get-tuple-element.37.refs_4_), channel_id=1, source_target_pairs={{0,480},{1,33},{2,482},{3,35},{4,484},{5,37},{6,486},{7,39},{8,488... | collective-permute-start | bytes 786440 | tf_op jit(solution)/shard_map/ppermute | solution.py:22
  110.7 11.0 %collective-permute-start.11 = (bf16[64,2048]{1,0:T(8,128)(2,1)S(1)}, bf16[64,2048]{1,0:T(8,128)(2,1)S(1)}, u32[]{:S(2)}, u32[]{:S(2)}) collective-permute-start(bf16[64,2048]{1,0:T(8,128)(2,1)S(1)} %get-tuple-element.38.refs_5_), channel_id=1, source_target_pairs={{0,32},{1,481},{2,34},{3,483},{4,36},{5,485},{6,38},{7,487},{8,40}... | collective-permute-start | bytes 786440 | tf_op jit(solution)/shard_map/ppermute | solution.py:22
  114.7 11.5 %collective-permute-start.8 = (bf16[64,2048]{1,0:T(8,128)(2,1)S(1)}, bf16[64,2048]{1,0:T(8,128)(2,1)S(1)}, u32[]{:S(2)}, u32[]{:S(2)}) collective-permute-start(bf16[64,2048]{1,0:T(8,128)(2,1)S(1)} %collective-permute-done.7.refs_2_), channel_id=1, source_target_pairs={{0,32},{1,481},{2,34},{3,483},{4,36},{5,485},{6,38},{7,487},{8,40}... | collective-permute-start | bytes 786440 | tf_op jit(solution)/shard_map/ppermute | solution.py:22
  116.6 9.6 %collective-permute-start.10 = (bf16[64,2048]{1,0:T(8,128)(2,1)S(1)}, bf16[64,2048]{1,0:T(8,128)(2,1)S(1)}, u32[]{:S(2)}, u32[]{:S(2)}) collective-permute-start(bf16[64,2048]{1,0:T(8,128)(2,1)S(1)} %collective-permute-done.9.refs_3_), channel_id=1, source_target_pairs={{0,480},{1,33},{2,482},{3,35},{4,484},{5,37},{6,486},{7,39},{8,488... | collective-permute-start | bytes 786440 | tf_op jit(solution)/shard_map/ppermute | solution.py:22
  127.6 4.8 %collective-permute-start.13 = (f32[16,32,512]{2,1,0:T(8,128)S(1)}, f32[16,32,512]{2,1,0:T(8,128)S(1)}, u32[]{:S(2)}, u32[]{:S(2)}) collective-permute-start(f32[16,32,512]{2,1,0:T(8,128)S(1)} %get-tuple-element.42), channel_id=1, source_target_pairs={{0,1},{1,0},{2,3},{3,2},{4,5},{5,4},{6,7},{7,6},{8,9},{9,8},{10,11... | collective-permute-start | bytes 3145736 | tf_op jit(solution)/shard_map/ppermute | solution.py:494
